TPU v7x, 32 devices: a whole 2x2x4 slice. The times are simulated.
32 devices in a mesh: mp: 4 (over x, core), fsdp: 2 (over y), dp: 4 (over z).
Axes of the slice: x: 2, y: 2, z: 4, core: 2. Of those that a mesh axis runs over, the one named last changes fastest.
Arguments:
- gen_noise: float32 [4, 512, 128], P('dp', 'fsdp'), may hold values from -6 to 6
- renoise: float32 [4, 512, 128], P('dp', 'fsdp'), may hold values from -120 to 120
- gen_step: int32 [4], P('dp'), may hold values from 250 to 999
- renoise_step: int32 [4], P('dp'), may hold values from 20 to 979
- text_pooled: bfloat16 [4, 768], P('dp'), may hold values from -6 to 6
- embed: bfloat16 [3, 64, 3072], replicated, may hold values from -0.75 to 0.75
- mod_weight: bfloat16 [3, 1024, 6144], P(None, None, 'fsdp'), may hold values from -0.1875 to 0.1875
- proj_weight: bfloat16 [3, 3072, 3072], P(None, 'fsdp', 'mp'), may hold values from -0.109375 to 0.109375
- unembed: bfloat16 [3, 64, 3072], P(None, None, 'mp'), may hold values from -0.109375 to 0.109375
Outputs:
- gen_grad: float32 [3072, 3072], P('fsdp', 'mp')
- score_gap: float32 [4, 512, 128], P('dp', 'fsdp')
All inputs are finite; a program needn't handle non-finite values. Where the computation divides by a largest or mean magnitude, that divisor is 1e-20 or more.
Results may differ from a plain program's by a relative error of at most 0.03.
Values may be sent and summed in bfloat16 or wider, within the bound.
No kernel may reach another device: no remote copies, remote signals or barrier semaphores. Data moves between devices by JAX's collectives and lax.ppermute only.
A program may use at most 128 MiB of HBM per device.

v0:
```python
import math

import jax
import jax.numpy as jnp
from jax import lax
from jax.sharding import PartitionSpec as P

D = 3072
CH = 64
TEMB = 256


GUIDANCE = 3.5
EPS_NORM = 1e-06
EPS_GAP = 1e-05


def sinusoid(timesteps):
    half_size = TEMB // 2
    frequency = jnp.exp(-math.log(10000.0) * jnp.arange(half_size, dtype=jnp.float32) / half_size)
    angles = timesteps.astype(jnp.float32)[:, None] * frequency[None, :]
    return jnp.concatenate([jnp.cos(angles), jnp.sin(angles)], axis=1)


def condition(timesteps, pooled):
    joined = jnp.concatenate([sinusoid(timesteps), pooled.astype(jnp.float32)], axis=1)
    return jax.nn.silu(joined).astype(jnp.bfloat16)


def normalize(values):
    average = jnp.mean(values, axis=1, keepdims=True)
    centred = values - average
    variance = jnp.mean(centred * centred, axis=1, keepdims=True)
    return centred * lax.rsqrt(variance + EPS_NORM)


def modulate(normed, modulation):
    return (normed * (1.0 + modulation[D:]) + modulation[:D]).astype(jnp.bfloat16)


def unembed_part(residual_sum, out_weight):
    return lax.dot_general(
        residual_sum.astype(jnp.bfloat16),
        out_weight,
        (((1,), (1,)), ((), ())),
        preferred_element_type=jnp.float32,
    )


def row_product(hidden, weight_piece):
    return jnp.dot(hidden, weight_piece, preferred_element_type=jnp.float32)


def body(
    gen_noise, renoise, gen_step, renoise_step, text_pooled, embed, mod_weight, proj_weight, unembed
):
    quarter = proj_weight.shape[2]
    col_start = lax.axis_index("mp") * quarter
    blank_text = jnp.zeros_like(text_pooled)
    noisy_vec = condition(renoise_step, text_pooled)
    local_mod = jnp.concatenate(
        [
            jnp.dot(
                condition(gen_step, text_pooled), mod_weight[0], preferred_element_type=jnp.float32
            ),
            jnp.dot(noisy_vec, mod_weight[1], preferred_element_type=jnp.float32),
            jnp.dot(
                condition(renoise_step, blank_text),
                mod_weight[1],
                preferred_element_type=jnp.float32,
            ),
            jnp.dot(noisy_vec, mod_weight[2], preferred_element_type=jnp.float32),
        ],
        axis=0,
    )
    modulation = lax.all_gather(local_mod, "fsdp", axis=1, tiled=True)
    latent = gen_noise[0].reshape(-1, CH)
    latent_bf = latent.astype(jnp.bfloat16)
    token_rows = latent.shape[0]
    embedded = jnp.dot(latent_bf, embed[0], preferred_element_type=jnp.float32)
    gen_hidden = modulate(normalize(embedded), modulation[0])
    gen_part = row_product(gen_hidden, lax.all_gather(proj_weight[0], "fsdp", axis=0, tiled=True))
    gen_cols = lax.dynamic_slice_in_dim(embedded, col_start, quarter, 1)
    clean_part = unembed_part(gen_cols + gen_part, unembed[0]).reshape(-1, 2 * CH)
    clean_lat = lax.psum(clean_part, "mp")
    noise_level = renoise_step[0].astype(jnp.float32) / 1000.0
    noisy_lat = (1.0 - noise_level) * clean_lat + noise_level * renoise[0]
    noisy_bf = noisy_lat.reshape(-1, CH).astype(jnp.bfloat16)
    teacher_in = jnp.dot(noisy_bf, embed[1], preferred_element_type=jnp.float32)
    teacher_norm = normalize(teacher_in)
    cond_hidden = modulate(teacher_norm, modulation[1])
    blank_hidden = modulate(teacher_norm, modulation[2])
    fake_in = jnp.dot(noisy_bf, embed[2], preferred_element_type=jnp.float32)
    fake_hidden = modulate(normalize(fake_in), modulation[3])
    pieces = (
        lax.all_gather(proj_weight[1], "fsdp", axis=0, tiled=True),
        lax.all_gather(proj_weight[2], "fsdp", axis=0, tiled=True),
    )
    cond_part = row_product(cond_hidden, pieces[0])
    blank_part = row_product(blank_hidden, pieces[0])
    fake_part = row_product(fake_hidden, pieces[1])
    teacher_cols = lax.dynamic_slice_in_dim(teacher_in, col_start, quarter, 1)
    fake_cols = lax.dynamic_slice_in_dim(fake_in, col_start, quarter, 1)
    cond_out, blank_out, fake_out = (
        lax.psum(
            unembed_part(teacher_cols + cond_part, unembed[1])
            .reshape(-1, 2 * CH)
            .astype(jnp.bfloat16),
            "mp",
        ).astype(jnp.float32),
        lax.psum(
            unembed_part(teacher_cols + blank_part, unembed[1])
            .reshape(-1, 2 * CH)
            .astype(jnp.bfloat16),
            "mp",
        ).astype(jnp.float32),
        lax.psum(
            unembed_part(fake_cols + fake_part, unembed[2])
            .reshape(-1, 2 * CH)
            .astype(jnp.bfloat16),
            "mp",
        ).astype(jnp.float32),
    )
    real_pred = noisy_lat - noise_level * (blank_out + GUIDANCE * (cond_out - blank_out))
    fake_pred = noisy_lat - noise_level * fake_out
    seq_len = token_rows * lax.axis_size("fsdp")
    gap_total = lax.psum(jnp.sum(jnp.abs(clean_lat - real_pred)), "fsdp")
    gap_scale = gap_total / (seq_len * CH) + EPS_GAP
    score_gap = (fake_pred - real_pred) / gap_scale
    all_tokens = seq_len * lax.axis_size("dp")
    cotangent = (score_gap / math.sqrt(all_tokens)).astype(jnp.bfloat16).reshape(-1, CH)
    upstream = jnp.dot(cotangent, unembed[0], preferred_element_type=jnp.float32).astype(
        jnp.bfloat16
    )
    row_terms = lax.psum_scatter(
        lax.dot_general(
            gen_hidden, upstream, (((0,), (0,)), ((), ())), preferred_element_type=jnp.float32
        ).astype(jnp.bfloat16),
        "fsdp",
        scatter_dimension=0,
        tiled=True,
    )
    gen_grad = lax.psum(row_terms, "dp").astype(jnp.float32)
    return (gen_grad, score_gap[None])


def solution(mesh):
    return jax.shard_map(
        body,
        mesh=mesh,
        in_specs=(
            P("dp", "fsdp", None),
            P("dp", "fsdp", None),
            P("dp"),
            P("dp"),
            P("dp", None),
            P(),
            P(None, None, "fsdp"),
            P(None, "fsdp", "mp"),
            P(None, None, "mp"),
        ),
        out_specs=(P("fsdp", "mp"), P("dp", "fsdp", None)),
        check_vma=False,
    )
```

profile of v0, /device:TPU:0, one launch (start us, length us, event | category | flops | bytes accessed | tf_op | source)
XLA Modules:
  0.0 486.2 jit_solution(13634648078258376916)
XLA Ops:
  7.2 6.3 %fusion.104 = (bf16[1,1536,768]{2,1,0:T(8,128)(2,1)}, bf16[1,1536,768]{2,1,0:T(8,128)(2,1)}, bf16[1,1536,768]{2,1,0:T(8,128)(2,1)}) fusion(bf16[3,1536,768]{2,1,0:T(8,128)(2,1)} %param.16), kind=kLoop, calls=%fused_computation.116 | loop fusion | bytes 14155776 | tf_op jit(solution)/shard_map/slice | solution.py:96
  15.2 3.7 fusion
  18.9 3.7 fusion.4
  22.6 4.7 fusion.2
  27.4 4.3 fusion.6
  31.7 6.8 %all_gather.12 = f32[4,6144]{1,0:T(4,128)S(1)} all-gather(f32[4,3072]{1,0:T(4,128)S(1)} %pad_maximum_fusion), channel_id=1, replica_groups=mesh['mp'=4,'fsdp'=2,'dp'=4] {'fsdp'}, dimensions={1}, use_global_device_ids=true | all-gather | bytes 147456 | tf_op jit(solution)/shard_map/all_gather | solution.py:76
  39.6 2.6 copy-done
  43.0 37.0 %all-gather.7.cloned.1.call-done = bf16[1,3072,768]{2,1,0:T(8,128)(2,1)} async-done(((bf16[1,1536,768]{2,1,0:T(8,128)(2,1)}), bf16[1,3072,768]{2,1,0:T(8,128)(2,1)}) %all-gather.7.cloned.1.call-update) | async-done | bytes 4718608 | tf_op jit(solution)/shard_map/all_gather | solution.py:82
  80.1 7.8 %fusion.50 = f32[512,64]{1,0:T(8,128)S(1)} fusion(f32[512,3072]{1,0:T(8,128)} %copy-done, s32[]{:T(128)S(6)} %select_n.2, bf16[1,3072,768]{2,1,0:T(8,128)(2,1)} %all-gather.7.cloned.1.call-done, bf16[3,64,768]{2,1,0:T(8,128)(2,1)S(1)} %copy-done.8, f32[3072]{0:T(1024)S(1)} %bitcast.107, f32[3072]{0:T(1024)S(1)} %bitcast.109, f32[512]{0:T(512)S(1)} %add_rsqrt_fusion.2, ...), kind=kOutput, calls=%fused_computation.48 | convolution fusion | flops 2474901504 | bytes 12840964 | tf_op jit(solution)/shard_map/dot_general | solution.py:42
  90.2 30.0 %all-reduce.5.cloned.1.call-done = f32[256,128]{1,0:T(8,128)} async-done(((f32[256,128]{1,0:T(8,128)}), f32[256,128]{1,0:T(8,128)}) %all-reduce.5.cloned.1.call-update) | async-done | bytes 131088 | tf_op jit(solution)/shard_map/psum | solution.py:85
  122.3 2.6 copy-done.2
  125.7 58.8 %all-gather.9.cloned.1.call-done = bf16[1,3072,768]{2,1,0:T(8,128)(2,1)} async-done(((bf16[1,1536,768]{2,1,0:T(8,128)(2,1)}), bf16[1,3072,768]{2,1,0:T(8,128)(2,1)}) %all-gather.9.cloned.1.call-update) | async-done | bytes 4718608 | tf_op jit(solution)/shard_map/all_gather | solution.py:97
  184.5 7.9 %fusion.58 = bf16[512,64]{0,1:T(8,128)(2,1)S(1)} fusion(f32[512,3072]{1,0:T(8,128)} %copy-done.2, s32[]{:T(128)S(6)} %select_n.2, bf16[1,3072,768]{2,1,0:T(8,128)(2,1)} %all-gather.9.cloned.1.call-done, f32[3072]{0:T(1024)S(1)} %bitcast.115, f32[3072]{0:T(1024)S(1)} %bitcast.116, f32[512]{0:T(512)S(1)} %add_rsqrt_fusion.1, ...), kind=kOutput, calls=%fused_computation.51 | convolution fusion | flops 2474934272 | bytes 12775428 | tf_op jit(solution)/shard_map/dot_general | solution.py:42
  194.4 2.8 copy-done.1
  198.0 51.3 %all-gather.11.cloned.1.call-done = bf16[1,3072,768]{2,1,0:T(8,128)(2,1)} async-done(((bf16[1,1536,768]{2,1,0:T(8,128)(2,1)}), bf16[1,3072,768]{2,1,0:T(8,128)(2,1)}) %all-gather.11.cloned.1.call-update) | async-done | bytes 4718608 | tf_op jit(solution)/shard_map/all_gather | solution.py:96
  249.2 7.9 %fusion.52 = bf16[512,64]{0,1:T(8,128)(2,1)S(1)} fusion(f32[512,3072]{1,0:T(8,128)} %copy-done.1, s32[]{:T(128)S(6)} %select_n.2, bf16[1,3072,768]{2,1,0:T(8,128)(2,1)} %all-gather.11.cloned.1.call-done, f32[3072]{0:T(1024)S(1)} %bitcast.113, f32[3072]{0:T(1024)S(1)} %bitcast.114, f32[512]{0:T(512)S(1)} %add_rsqrt_fusion, ...), kind=kOutput, calls=%fused_computation.49 | convolution fusion | flops 2474934272 | bytes 12775428 | tf_op jit(solution)/shard_map/dot_general | solution.py:42
  258.0 7.9 %fusion.55 = bf16[512,64]{0,1:T(8,128)(2,1)S(1)} fusion(f32[512,3072]{1,0:T(8,128)} %copy-done.1, s32[]{:T(128)S(6)} %select_n.2, bf16[1,3072,768]{2,1,0:T(8,128)(2,1)} %all-gather.11.cloned.1.call-done, f32[3072]{0:T(1024)S(1)} %bitcast.112, f32[3072]{0:T(1024)S(1)} %bitcast.111, f32[512]{0:T(512)S(1)} %add_rsqrt_fusion, ...), kind=kOutput, calls=%fused_computation.50 | convolution fusion | flops 2474934272 | bytes 12775428 | tf_op jit(solution)/shard_map/dot_general | solution.py:42
  266.9 32.0 %all-reduce.9.cloned.1.call-done = (bf16[256,128]{1,0:T(8,128)(2,1)}, bf16[256,128]{1,0:T(8,128)(2,1)}, bf16[256,128]{1,0:T(8,128)(2,1)}) async-done(((bf16[256,128]{1,0:T(8,128)(2,1)}, bf16[256,128]{1,0:T(8,128)(2,1)}, bf16[256,128]{1,0:T(8,128)(2,1)}), (bf16[256,128]{1,0:T(8,128)(2,1)}, bf16[256,128]{1,0:T(8,128)(2,1)}, bf16[256,128]{1,0:T(8,128)(2,1)})) %all-reduce.9.cloned.1.call-update) | async-done | bytes 196624 | tf_op jit(solution)/shard_map/psum | solution.py:117
  300.5 5.8 %psum.46 = f32[]{:T(128)} all-reduce(f32[]{:T(128)} %abs_reduce_fusion), channel_id=1, replica_groups=mesh['mp'=4,'fsdp'=2,'dp'=4] {'fsdp'}, use_global_device_ids=true, to_apply=%region_11.12 | all-reduce | flops 1 | bytes 8 | tf_op jit(solution)/shard_map/psum | solution.py:127
  306.9 1.6 multiply_convert_fusion
  308.7 8.2 %convolution_convert_fusion = bf16[3072,768]{1,0:T(8,128)(2,1)} fusion(bf16[512,64]{1,0:T(8,128)(2,1)S(1)} %reshape.201, bf16[3,64,768]{2,1,0:T(8,128)(2,1)S(1)} %copy-done.8, f32[512,3072]{1,0:T(8,128)} %copy-done, f32[3072]{0:T(1024)S(1)} %bitcast.108, f32[3072]{0:T(1024)S(1)} %bitcast.110, f32[512]{0:T(512)S(1)} %add_rsqrt_fusion.2, ...), kind=kOutput, calls=%fused_computation.19 | convolution fusion | flops 2476867584 | bytes 11268096 | tf_op jit(solution)/shard_map/dot_general | solution.py:136
  316.9 60.1 %reduce-scatter.2.cloned.1.call-done = bf16[1536,768]{1,0:T(8,128)(2,1)} async-done(((bf16[3072,768]{1,0:T(8,128)(2,1)}), bf16[1536,768]{1,0:T(8,128)(2,1)}) %reduce-scatter.2.cloned.1.call-update) | async-done | bytes 2359312 | tf_op jit(solution)/shard_map/reduce_scatter | solution.py:135
  377.0 98.1 %all-reduce.7.cloned.1.call-done = bf16[1536,768]{1,0:T(8,128)(2,1)} async-done(((bf16[1536,768]{1,0:T(8,128)(2,1)}), bf16[1536,768]{1,0:T(8,128)(2,1)}) %all-reduce.7.cloned.1.call-update) | async-done | bytes 2359312 | tf_op jit(solution)/shard_map/psum | solution.py:143
  475.2 4.2 convert_element_type.139
  (64 shorter events, 13.6 us)
Async XLA Ops:
  7.2 6.4 %copy-start.6 = (f32[1,256,128]{2,1,0:T(8,128)S(1)}, f32[1,256,128]{2,1,0:T(8,128)}, u32[]{:S(2)}) copy-start(f32[1,256,128]{2,1,0:T(8,128)} %param.9) | copy-start | bytes 393220
  7.2 7.9 %copy-start.7 = (bf16[1,768]{1,0:T(2,128)(2,1)S(1)}, bf16[1,768]{1,0:T(2,128)(2,1)}, u32[]{:S(2)}) copy-start(bf16[1,768]{1,0:T(2,128)(2,1)} %param.13) | copy-start | bytes 4612
  7.2 72.9 %all-gather.7.cloned.1.call-start = ((), (), s32[]{:S(2)}) async-start(), calls=%async_computation.4 | async-start | bytes 7077888 | tf_op jit(solution)/shard_map/all_gather | solution.py:82
  13.5 106.7 %all-reduce.5.cloned.1.call-start = ((), (), s32[]{:S(2)}) async-start(), calls=%async_computation.1 | async-start | bytes 262144 | tf_op jit(solution)/shard_map/psum | solution.py:85
  22.6 15.8 %copy-start.3 = (bf16[3,64,3072]{2,1,0:T(8,128)(2,1)S(1)}, bf16[3,64,3072]{2,1,0:T(8,128)(2,1)}, u32[]{:S(2)}) copy-start(bf16[3,64,3072]{2,1,0:T(8,128)(2,1)} %param.14) | copy-start | bytes 3538948
  38.5 41.6 %copy-start.8 = (bf16[3,64,768]{2,1,0:T(8,128)(2,1)S(1)}, bf16[3,64,768]{2,1,0:T(8,128)(2,1)}, u32[]{:S(2)}) copy-start(bf16[3,64,768]{2,1,0:T(8,128)(2,1)} %param.17) | copy-start | bytes 884740
  39.5 2.6 copy-start
  80.1 40.1 %copy-start.4 = (f32[1,256,128]{2,1,0:T(8,128)S(1)}, f32[1,256,128]{2,1,0:T(8,128)}, u32[]{:S(2)}) copy-start(f32[1,256,128]{2,1,0:T(8,128)} %param.10) | copy-start | bytes 393220
  88.7 95.8 %all-gather.9.cloned.1.call-start = ((), (), s32[]{:S(2)}) async-start(), calls=%async_computation.5 | async-start | bytes 7077888 | tf_op jit(solution)/shard_map/all_gather | solution.py:97
  89.4 159.8 %all-gather.11.cloned.1.call-start = ((), (), s32[]{:S(2)}) async-start(), calls=%async_computation.6 | async-start | bytes 7077888 | tf_op jit(solution)/shard_map/all_gather | solution.py:96
  90.0 209.0 %all-reduce.9.cloned.1.call-start = ((), (), s32[]{:S(2)}) async-start(), calls=%async_computation.7 | async-start | bytes 393216 | tf_op jit(solution)/shard_map/psum | solution.py:117
  122.3 2.7 copy-start.2
  194.3 2.8 copy-start.1
  258.0 40.9 %copy-start.5 = (f32[256,128]{1,0:T(8,128)S(1)}, f32[256,128]{1,0:T(8,128)}, u32[]{:S(2)}) copy-start(f32[256,128]{1,0:T(8,128)} %all-reduce.5.cloned.1.call-done) | copy-start | bytes 393220
  266.9 110.1 %reduce-scatter.2.cloned.1.call-start = ((), (), s32[]{:S(2)}) async-start(), calls=%async_computation.2 | async-start | bytes 7077888 | tf_op jit(solution)/shard_map/reduce_scatter | solution.py:135
  316.8 158.3 %all-reduce.7.cloned.1.call-start = ((), (), s32[]{:S(2)}) async-start(), calls=%async_computation.3 | async-start | bytes 4718592 | tf_op jit(solution)/shard_map/psum | solution.py:143
Sparse Core Ops, SparseCore 0:
  13.6 66.3 all-gather.6
  88.8 31.3 all-reduce.4
  121.8 62.6 all-gather.8
  186.6 62.6 all-gather.10
  267.0 31.9 all-reduce.8
  317.0 59.9 reduce-scatter.1
  379.5 95.6 all-reduce.6
where the time goes:
time: 487 us; the launch traced here: 486 us
  waiting for transfers between devices  369 us (76%)
  matrix products  59.2 us (12%)
  local copies, waits for them, and re-layouts  18.1 us (4%)
  between operations  16.3 us (3%)
  blocking collectives  12.6 us (3%)
  other arithmetic  10.9 us (2%)
    psum x1, waiting for transfers between devices, body(): gen_grad = lax.psum(row_terms, 'dp').astype(jnp.float32)  98.1 us
    reduce_scatter x1, waiting for transfers between devices, body(): lax.psum_scatter(lax.dot_general(gen_hidden, upstream, (((0,), (0,)), (()...  60.1 us
    all_gather x1, waiting for transfers between devices, body(): lax.all_gather(proj_weight[2], 'fsdp', axis=0, tiled=True)  58.8 us
    all_gather x1, waiting for transfers between devices, body(): lax.all_gather(proj_weight[1], 'fsdp', axis=0, tiled=True)  51.3 us
    all_gather x1, waiting for transfers between devices, body(): lax.all_gather(proj_weight[0], 'fsdp', axis=0, tiled=True)  37 us
    psum x1, waiting for transfers between devices, body(): lax.psum(unembed_part(fake_cols + fake_part, unembed[2]).reshape(-1, 2 *...  32 us
    dot_general x4, matrix products, unembed_part(): lax.dot_general(residual_sum.astype(jnp.bfloat16), out_weight, (((1,), (1...  31.5 us
    psum x1, waiting for transfers between devices, body(): clean_lat = lax.psum(clean_part, 'mp')  30 us
  transfers between devices with their start and end apart: 7, of which 7 were waited for; matrix products, arithmetic and copies ran while one was open for 7% of the time, Pallas kernels for 0%

commit v1 on v0

v1 whole, which is shorter than its diff:
```python
import math

import jax
import jax.numpy as jnp
from jax import lax
from jax.sharding import PartitionSpec as P

D = 3072
CH = 64
TEMB = 256

GUIDANCE = 3.5
EPS_NORM = 1e-06
EPS_GAP = 1e-05
HI = lax.Precision.HIGHEST


def sinusoid(timesteps):
    half_size = TEMB // 2
    frequency = jnp.exp(-math.log(10000.0) * jnp.arange(half_size, dtype=jnp.float32) / half_size)
    angles = timesteps.astype(jnp.float32)[:, None] * frequency[None, :]
    return jnp.concatenate([jnp.cos(angles), jnp.sin(angles)], axis=1)


def condition(timesteps, pooled):
    joined = jnp.concatenate([sinusoid(timesteps), pooled.astype(jnp.float32)], axis=1)
    return jax.nn.silu(joined).astype(jnp.bfloat16)


def swap(x, axes, mask):
    count = lax.axis_size(axes)
    return lax.ppermute(x, axes, [(i, i ^ mask) for i in range(count)])


def plane_sum(x):
    if lax.axis_size("mp") != 4 or lax.axis_size("fsdp") != 2:
        return lax.psum(x, ("mp", "fsdp"))
    x = x + swap(x, "mp", 1)
    plane = ("mp", "fsdp")
    parts = [swap(x, plane, mask) for mask in (4, 1, 5)]
    return (x + parts[0]) + (parts[1] + parts[2])


def gather_samples(x):
    count = lax.axis_size("dp")
    if lax.axis_size("mp") != 4 or count != 4:
        blocks = lax.all_gather(x, "dp")
        return [blocks[i] for i in range(count)]
    pairs = []
    for m in range(4):
        for s in range(4):
            pairs.append((m * 4 + s, m * 4 + (s ^ (1 if m % 2 == 0 else 2))))
    near = lax.ppermute(x, ("mp", "dp"), pairs)
    far = swap(x, "dp", 3)
    return [x, near, swap(near, "mp", 1), far]


def exchange_modulation(local_mod, rows):
    if lax.axis_size("fsdp") == 2:
        f = lax.axis_index("fsdp")
        mine = lax.dynamic_slice_in_dim(local_mod, f * rows, rows, 1)
        theirs = swap(lax.dynamic_slice_in_dim(local_mod, (1 - f) * rows, rows, 1), "fsdp", 1)
        return jnp.where(f == 0, mine, theirs), jnp.where(f == 0, theirs, mine)
    whole = lax.all_gather(local_mod, "fsdp", axis=1, tiled=True)
    start = lax.axis_index("fsdp") * rows
    return (
        lax.dynamic_slice_in_dim(whole[:, :D], start, rows, 1),
        lax.dynamic_slice_in_dim(whole[:, D:], start, rows, 1),
    )


def dot(a, b, precision=HI):
    return jnp.dot(a, b, precision=precision, preferred_element_type=jnp.float32)


def both(x):
    zero = jnp.zeros_like(x)
    return jnp.concatenate(
        [jnp.concatenate([x, zero], 1), jnp.concatenate([zero, x], 1)], 0
    )


def body(
    gen_noise, renoise, gen_step, renoise_step, text_pooled, embed, mod_weight, proj_weight, unembed
):
    rows, cols = proj_weight.shape[1], proj_weight.shape[2]
    f = lax.axis_index("fsdp")
    noise_all = lax.all_gather(gen_noise[0], "fsdp", axis=0, tiled=True)
    renoise_all = lax.all_gather(renoise[0], "fsdp", axis=0, tiled=True)

    blank_text = jnp.zeros_like(text_pooled)
    gen_vec = condition(gen_step, text_pooled)
    real_vec = jnp.concatenate(
        [condition(renoise_step, text_pooled), condition(renoise_step, blank_text)], 0
    )
    teacher_mod = jnp.dot(real_vec, mod_weight[1], preferred_element_type=jnp.float32)
    local_mod = jnp.concatenate(
        [
            jnp.dot(gen_vec, mod_weight[0], preferred_element_type=jnp.float32),
            GUIDANCE * teacher_mod[0:1] + (1.0 - GUIDANCE) * teacher_mod[1:2],
            jnp.dot(real_vec[0:1], mod_weight[2], preferred_element_type=jnp.float32),
        ],
        axis=0,
    )
    shift, scale = exchange_modulation(local_mod, rows)

    centred = embed.astype(jnp.float32)
    centred = centred - jnp.mean(centred, axis=2, keepdims=True)
    gram = [dot(centred[m], centred[m].T) / D for m in range(3)]
    centred_rows = lax.dynamic_slice_in_dim(centred, f * rows, rows, 2)
    embed_cols = lax.dynamic_slice_in_dim(embed, lax.axis_index("mp") * cols, cols, 2)

    pieces = []
    for m in range(3):
        through = lax.dot_general(
            proj_weight[m], unembed[m], (((1,), (1,)), ((), ())), preferred_element_type=jnp.float32
        )
        direct = lax.dot_general(
            embed_cols[m], unembed[m], (((1,), (1,)), ((), ())), preferred_element_type=jnp.float32
        )
        direct = jnp.where(f == 0, direct, 0.0)
        modulated = dot(centred_rows[m] * (1.0 + scale[m : m + 1]), through)
        offset = dot(shift[m : m + 1], through)
        offset = jnp.concatenate([offset, jnp.zeros((7, CH), jnp.float32)], 0)
        pieces.append(
            jnp.concatenate(
                [
                    jnp.concatenate([direct, modulated], 1),
                    jnp.concatenate([offset, jnp.zeros_like(offset)], 1),
                ],
                0,
            )
        )
    maps = plane_sum(jnp.concatenate(pieces, 0)).reshape(3, CH + 8, 2 * CH)
    direct = [both(maps[m, :CH, :CH]) for m in range(3)]
    modulated = [both(maps[m, :CH, CH:]) for m in range(3)]
    offset = [jnp.concatenate([maps[m, CH : CH + 1, :CH]] * 2, 1) for m in range(3)]

    ones = both(jnp.ones((CH, CH), jnp.float32))

    def normalized(u, m):
        spread = dot(dot(u, both(gram[m])) * u, ones)
        return u * lax.rsqrt(jnp.maximum(spread, 0.0) + EPS_NORM)

    def model(u, u_norm, m):
        return dot(u, direct[m]) + dot(u_norm, modulated[m]) + offset[m]

    noise = noise_all.astype(jnp.bfloat16).astype(jnp.float32)
    noise_norm = normalized(noise, 0)
    clean = model(noise, noise_norm, 0)
    level = renoise_step[0].astype(jnp.float32) / 1000.0
    noisy = (1.0 - level) * clean + level * renoise_all
    noisy = noisy.astype(jnp.bfloat16).astype(jnp.float32)
    real_v = model(noisy, normalized(noisy, 1), 1)
    fake_v = model(noisy, normalized(noisy, 2), 2)
    total = jnp.sum(jnp.abs(clean - renoise_all + real_v))
    gap_scale = level * total / (noise_all.shape[0] * 2 * CH) + EPS_GAP
    score = level * (real_v - fake_v) / gap_scale
    local_rows = gen_noise.shape[1]
    score_gap = lax.dynamic_slice_in_dim(score, f * local_rows, local_rows, 0)

    all_tokens = noise_all.shape[0] * 2 * lax.axis_size("dp")
    cotangent = (score / math.sqrt(all_tokens)).astype(jnp.bfloat16).astype(jnp.float32)
    pairs = dot(noise_norm.T, cotangent)
    outer = pairs[:CH, :CH] + pairs[CH:, CH:]
    sums = jnp.sum(cotangent, axis=0)
    sums = sums[:CH] + sums[CH:]
    payload = jnp.concatenate(
        [
            jnp.pad(outer, ((0, 0), (0, CH))),
            jnp.pad(sums[None], ((0, 7), (0, CH))),
            jnp.concatenate([shift[0], scale[0]]).reshape(-1, 2 * CH),
        ],
        0,
    )
    blocks = gather_samples(payload)
    grad_map = jnp.zeros((CH, rows), jnp.float32)
    for block in blocks:
        block_mod = block[CH + 8 :].reshape(2, rows)
        grad_map += dot(block[:CH, :CH].T, centred_rows[0]) * (1.0 + block_mod[1:2])
        grad_map += block[CH, :CH][:, None] * block_mod[0:1]
    gen_grad = lax.dot_general(
        grad_map.astype(jnp.bfloat16),
        unembed[0],
        (((0,), (0,)), ((), ())),
        preferred_element_type=jnp.float32,
    )
    return (gen_grad, score_gap[None])


def solution(mesh):
    return jax.shard_map(
        body,
        mesh=mesh,
        in_specs=(
            P("dp", "fsdp", None),
            P("dp", "fsdp", None),
            P("dp"),
            P("dp"),
            P("dp", None),
            P(),
            P(None, None, "fsdp"),
            P(None, "fsdp", "mp"),
            P(None, None, "mp"),
        ),
        out_specs=(P("fsdp", "mp"), P("dp", "fsdp", None)),
        check_vma=False,
    )
```

time: 487 us -> 94.5 us (0.19)
  waiting for transfers between devices: 369 us -> 6.67 us
  local copies, waits for them, and re-layouts: 18.1 us -> 2.89 us
  between operations: 16.3 us -> 3.02 us
  starting transfers between devices: 0.46 us -> 10.3 us
  matrix products: 59.2 us -> 52.4 us
    psum x3 -> x0, waiting for transfers between devices: 160 us -> none  [the longest x1 98.1 us: body(): gen_grad = lax.psum(row_terms, 'dp').astype(jnp.float32)]
    all_gather x3 -> x0, waiting for transfers between devices: 147 us -> none  [the longest x1 58.8 us: body(): lax.all_gather(proj_weight[2], 'fsdp', axis=0, tiled=True)]
    reduce_scatter x1 -> x0, waiting for transfers between devices: 60.1 us -> none  [body(): lax.psum_scatter(lax.dot_general(gen_hidden, upstream, (((0,), (0,)), (()...]
    ppermute x0 -> x8, starting transfers between devices: none -> 10.3 us  [the longest x7 10.3 us: swap(): return lax.ppermute(x, axes, [(i, i ^ mask) for i in range(count)])]
    unnamed x18 -> x28, local copies, waits for them, and re-layouts: 8.14 us -> 0.71 us
    dot_general x12 -> x36, matrix products: 59.2 us -> 52.4 us  [the longest x26 22.6 us: dot(): jnp.dot(a, b, precision=precision, preferred_element_type=jnp.float32)]
    ppermute x0 -> x8, waiting for transfers between devices: none -> 6.67 us  [the longest x7 3.75 us: swap(): return lax.ppermute(x, axes, [(i, i ^ mask) for i in range(count)])]
    psum x1 -> x0, blocking collectives: 5.77 us -> none  [body(): gap_total = lax.psum(jnp.sum(jnp.abs(clean_lat - real_pred)), 'fsdp')]
  transfers between devices with their start and end apart: 7 -> 8, of which waited for: 7 -> 4; matrix products, arithmetic and copies ran while one was open for 7% -> 28% of each run, Pallas kernels for 0% -> 0%
where the time goes in v1:
time: 94.5 us; the launch traced here: 93.5 us
  matrix products  52.4 us (55%)
  blocking collectives  11.9 us (13%)
  starting transfers between devices  10.3 us (11%)
  waiting for transfers between devices  6.67 us (7%)
  other arithmetic  6.31 us (7%)
  between operations  3.02 us (3%)
  local copies, waits for them, and re-layouts  2.89 us (3%)
    dot_general x26, matrix products, dot(): jnp.dot(a, b, precision=precision, preferred_element_type=jnp.float32)  22.6 us
    ppermute x7, starting transfers between devices, swap(): return lax.ppermute(x, axes, [(i, i ^ mask) for i in range(count)])  10.3 us
    dot_general x3, matrix products, body(): lax.dot_general(proj_weight[m], unembed[m], (((1,), (1,)), ((), ())), pre...  9.81 us
    all_gather x1, blocking collectives, body(): renoise_all = lax.all_gather(renoise[0], 'fsdp', axis=0, tiled=True)  6.95 us
    dot_general x3, matrix products, body(): lax.dot_general(embed_cols[m], unembed[m], (((1,), (1,)), ((), ())), pref...  5.01 us
    all_gather x1, blocking collectives, body(): noise_all = lax.all_gather(gen_noise[0], 'fsdp', axis=0, tiled=True)  4.93 us
    dot_general x1, matrix products, body(): lax.dot_general(grad_map.astype(jnp.bfloat16), unembed[0], (((0,), (0,)),...  3.89 us
    dot_general x1, matrix products, body(): jnp.dot(real_vec, mod_weight[1], preferred_element_type=jnp.float32)  3.76 us
  transfers between devices with their start and end apart: 8, of which 4 were waited for; matrix products, arithmetic and copies ran while one was open for 28% of the time, Pallas kernels for 0%

profile of v1, /device:TPU:0, one launch (start us, length us, event | category | flops | bytes accessed | tf_op | source)
XLA Modules:
  0.0 93.5 jit_solution(11551723909566449118)
XLA Ops:
  3.5 3.7 %fusion = f32[1,3072]{1,0:T(1,128)S(1)} fusion(bf16[1024,1]{0,1:T(2,128)(2,1)S(1)} %reshape.312, bf16[3,1024,3072]{2,1,0:T(8,128)(2,1)} %param.15), kind=kOutput, calls=%fused_computation | convolution fusion | flops 6291456 | bytes 6305792 | tf_op jit(solution)/shard_map/dot_general | solution.py:101
  7.3 3.7 %fusion.4 = f32[1,3072]{1,0:T(1,128)S(1)} fusion(bf16[1024,1]{0,1:T(2,128)(2,1)S(1)} %reshape.310, bf16[3,1024,3072]{2,1,0:T(8,128)(2,1)} %param.15), kind=kOutput, calls=%fused_computation.4 | convolution fusion | flops 6291456 | bytes 6305792 | tf_op jit(solution)/shard_map/dot_general | solution.py:99
  11.0 3.8 %fusion.2 = f32[2,3072]{1,0:T(2,128)S(1)} fusion(bf16[3,1024,3072]{2,1,0:T(8,128)(2,1)} %param.15, bf16[1,1024]{1,0:T(2,128)(2,1)S(1)} %get-tuple-element.26, bf16[1,1024]{1,0:T(2,128)(2,1)S(1)} %get-tuple-element.25), kind=kOutput, calls=%fused_computation.2 | convolution fusion | flops 12591104 | bytes 6320128 | tf_op jit(solution)/shard_map/dot_general | solution.py:96
  15.5 3.0 %collective-permute-start = (f32[3,1536]{1,0:T(4,128)}, f32[3,1536]{1,0:T(4,128)}, u32[]{:S(2)}, u32[]{:S(2)}) collective-permute-start(f32[3,1536]{1,0:T(4,128)} %constant_dynamic-slice_fusion), channel_id=1, source_target_pairs={{0,4},{4,0},{1,5},{5,1},{2,6},{6,2},{3,7},{7,3},{8,12},{12,8},{9,1... | collective-permute-start | bytes 55304 | tf_op jit(solution)/shard_map/ppermute | solution.py:32
  18.5 3.2 %fusion.13 = f32[1536,64]{0,1:T(8,128)} fusion(bf16[3,1536,768]{2,1,0:T(8,128)(2,1)} %param.16, bf16[3,64,768]{2,1,0:T(8,128)(2,1)S(1)} %copy-done.7), kind=kOutput, calls=%fused_computation.15 | convolution fusion | flops 150994944 | bytes 2850816 | tf_op jit(solution)/shard_map/dot_general | solution.py:115
  21.7 3.2 %fusion.9 = f32[1536,64]{0,1:T(8,128)} fusion(bf16[3,1536,768]{2,1,0:T(8,128)(2,1)} %param.16, bf16[3,64,768]{2,1,0:T(8,128)(2,1)S(1)} %copy-done.7), kind=kOutput, calls=%fused_computation.11 | convolution fusion | flops 150994944 | bytes 2850816 | tf_op jit(solution)/shard_map/dot_general | solution.py:115
  24.9 3.3 %fusion.11 = f32[1536,64]{0,1:T(8,128)} fusion(bf16[3,1536,768]{2,1,0:T(8,128)(2,1)} %param.16, bf16[3,64,768]{2,1,0:T(8,128)(2,1)S(1)} %copy-done.7), kind=kOutput, calls=%fused_computation.13 | convolution fusion | flops 150994944 | bytes 2850816 | tf_op jit(solution)/shard_map/dot_general | solution.py:115
  33.0 1.7 %convolution_select_fusion.2 = f32[64,64]{1,0:T(8,128)} fusion(bf16[3,64,3072]{2,1,0:T(8,128)(2,1)S(1)} %copy-done, s32[]{:T(128)S(6)} %select_n.42, bf16[3,64,768]{2,1,0:T(8,128)(2,1)} %param.17, pred[]{:T(512)S(6)} %eq.2), kind=kOutput, calls=%fused_computation.62 | convolution fusion | flops 6295552 | bytes 212997 | tf_op jit(solution)/shard_map/dot_general | solution.py:118
  34.6 1.7 %convolution_select_fusion.1 = f32[64,64]{1,0:T(8,128)} fusion(bf16[3,64,3072]{2,1,0:T(8,128)(2,1)S(1)} %copy-done, s32[]{:T(128)S(6)} %add.297, s32[]{:T(128)S(6)} %select_n.42, bf16[3,64,768]{2,1,0:T(8,128)(2,1)} %param.17, pred[]{:T(512)S(6)} %eq.2), kind=kOutput, calls=%fused_computation.61 | convolution fusion | flops 6295552 | bytes 213001 | tf_op jit(solution)/shard_map/dot_general | solution.py:118
  37.2 4.9 %all-gather = bf16[1,512,128]{2,1,0:T(8,128)(2,1)S(1)} all-gather(bf16[1,256,128]{2,1,0:T(8,128)(2,1)S(1)} %convert), channel_id=2, replica_groups=mesh['mp'=4,'fsdp'=2,'dp'=4] {'fsdp'}, dimensions={1}, use_global_device_ids=true | all-gather | bytes 196608 | tf_op jit(solution)/shard_map/all_gather | solution.py:88
  42.8 1.9 %fusion.38 = f32[512,128]{1,0:T(8,128)} fusion(f32[64,64]{1,0:T(8,128)} %convolution_multiply_fusion.8, bf16[1,512,128]{2,1,0:T(8,128)(2,1)S(1)} %all-gather), kind=kOutput, calls=%fused_computation.54 | convolution fusion | flops 100876288 | bytes 409600 | tf_op jit(solution)/shard_map/dot_general | solution.py:73
  44.6 1.7 %convolution_select_fusion = f32[64,64]{1,0:T(8,128)} fusion(bf16[3,64,3072]{2,1,0:T(8,128)(2,1)S(1)} %copy-done, s32[]{:T(128)S(6)} %add.299, s32[]{:T(128)S(6)} %select_n.42, bf16[3,64,768]{2,1,0:T(8,128)(2,1)} %param.17, pred[]{:T(512)S(6)} %eq.2), kind=kOutput, calls=%fused_computation.60 | convolution fusion | flops 6295552 | bytes 213001 | tf_op jit(solution)/shard_map/dot_general | solution.py:118
  48.7 1.4 %fusion.132 = f32[1,64]{1,0:T(1,128)S(1)} fusion(f32[1536,64]{0,1:T(8,128)} %fusion.9, f32[3,1536]{1,0:T(4,128)S(1)} %get-tuple-element.15), kind=kOutput, calls=%fused_computation.207 | convolution fusion | flops 1179648 | bytes 399616 | tf_op jit(solution)/shard_map/dot_general | solution.py:73
  50.1 1.4 %fusion.134 = f32[1,64]{1,0:T(1,128)S(1)} fusion(f32[1536,64]{0,1:T(8,128)} %fusion.11, f32[3,1536]{1,0:T(4,128)S(1)} %get-tuple-element.15), kind=kOutput, calls=%fused_computation.211 | convolution fusion | flops 1179648 | bytes 399616 | tf_op jit(solution)/shard_map/dot_general | solution.py:73
  51.5 1.5 %fusion.45 = f32[64,64]{1,0:T(8,128)S(1)} fusion(f32[1536,64]{0,1:T(8,128)} %fusion.11, f32[3,64,3072]{2,1,0:T(8,128)S(1)} %convert_subtract_fusion, s32[]{:T(128)S(6)} %add.297, s32[]{:T(128)S(6)} %select_n.44, f32[1536]{0:T(1024)S(1)} %get-tuple-element.4), kind=kOutput, calls=%fused_computation.71 | convolution fusion | flops 75595776 | bytes 811016 | tf_op jit(solution)/shard_map/dot_general | solution.py:73
  57.2 6.9 %all-gather.1 = f32[1,512,128]{2,1,0:T(8,128)S(1)} all-gather(f32[1,256,128]{2,1,0:T(8,128)} %param.10), channel_id=3, replica_groups=mesh['mp'=4,'fsdp'=2,'dp'=4] {'fsdp'}, dimensions={1}, use_global_device_ids=true | all-gather | bytes 393216 | tf_op jit(solution)/shard_map/all_gather | solution.py:89
  64.2 1.5 %collective-permute-start.4 = (f32[216,128]{1,0:T(8,128)S(1)}, f32[216,128]{1,0:T(8,128)S(1)}, u32[]{:S(2)}, u32[]{:S(2)}) collective-permute-start(f32[216,128]{1,0:T(8,128)S(1)} %add.253), channel_id=1, source_target_pairs={{0,20},{4,16},{8,28},{12,24},{16,4},{20,0},{24,12},{28,8},{1,21},{... | collective-permute-start | bytes 331784 | tf_op jit(solution)/shard_map/ppermute | solution.py:32
  65.7 1.5 %collective-permute-start.3 = (f32[216,128]{1,0:T(8,128)S(1)}, f32[216,128]{1,0:T(8,128)S(1)}, u32[]{:S(2)}, u32[]{:S(2)}) collective-permute-start(f32[216,128]{1,0:T(8,128)S(1)} %add.253), channel_id=1, source_target_pairs={{0,4},{4,0},{8,12},{12,8},{16,20},{20,16},{24,28},{28,24},{1,5},{5... | collective-permute-start | bytes 331784 | tf_op jit(solution)/shard_map/ppermute | solution.py:32
  68.5 2.4 %collective-permute-done.4 = f32[216,128]{1,0:T(8,128)S(1)} collective-permute-done((f32[216,128]{1,0:T(8,128)S(1)}, f32[216,128]{1,0:T(8,128)S(1)}, u32[]{:S(2)}, u32[]{:S(2)}) %collective-permute-start.4) | collective-permute-done | bytes 110624 | tf_op jit(solution)/shard_map/ppermute | solution.py:32
  75.4 1.8 %fusion.53 = (f32[]{:T(128)}, f32[512,128]{1,0:T(8,128)}) fusion(f32[512,128]{1,0:T(8,128)S(1)} %get-tuple-element.28, f32[1,512,128]{2,1,0:T(8,128)S(1)} %all-gather.1, f32[128]{0:T(128)S(1)} %maximum_bitcast_fusion.1, f32[512,128]{1,0:T(8,128)S(1)} %fusion.90, f32[512,128]{1,0:T(8,128)S(1)} %fusion.33, f32[64,64]{1,0:T(8,128)S(1)} %get-tuple-element.8), kind=kOutput, calls=%fused_computation.81 | convolution fusion | flops 101138432 | bytes 1327620 | tf_op jit(solution)/shard_map/dot_general | solution.py:73
  77.9 1.4 %convert_reduce_fusion.1 = (f32[128]{0:T(128)S(1)}, f32[512,128]{1,0:T(8,128)S(1)}) fusion(f32[]{:T(128)S(6)} %add.273, f32[512,128]{1,0:T(8,128)} %get-tuple-element.30, f32[128]{0:T(128)S(1)} %maximum_bitcast_fusion.2, f32[512,128]{1,0:T(8,128)S(1)} %fusion.80, f32[512,128]{1,0:T(8,128)S(1)} %fusion.29, f32[64,64]{1,0:T(8,128)S(1)} %get-tuple-element.6, ...), kind=kOutput, calls=%fused_computation.82 | convolution fusion | flops 101334912 | bytes 1065992 | tf_op jit(solution)/shard_map/dot_general | solution.py:73
  79.9 3.7 %collective-permute-start.7 = (f32[96,128]{1,0:T(8,128)S(1)}, f32[96,128]{1,0:T(8,128)S(1)}, u32[]{:S(2)}, u32[]{:S(2)}) collective-permute-start(f32[96,128]{1,0:T(8,128)S(1)} %fusion.105), channel_id=1, source_target_pairs={{0,3},{1,2},{2,1},{3,0},{4,7},{5,6},{6,5},{7,4},{8,11},{9,10},{10,... | collective-permute-start | bytes 147464 | tf_op jit(solution)/shard_map/ppermute | solution.py:32
  84.8 2.9 %collective-permute-done.5 = f32[96,128]{1,0:T(8,128)S(1)} collective-permute-done((f32[96,128]{1,0:T(8,128)S(1)}, f32[96,128]{1,0:T(8,128)S(1)}, u32[]{:S(2)}, u32[]{:S(2)}) %collective-permute-start.5) | collective-permute-done | bytes 49184 | tf_op jit(solution)/shard_map/ppermute | solution.py:53
  89.6 3.9 %fusion.63 = f32[1536,768]{1,0:T(8,128)} fusion(bf16[64,1536]{1,0:T(8,128)(2,1)S(1)} %fusion.24, bf16[3,64,768]{2,1,0:T(8,128)(2,1)} %param.17), kind=kOutput, calls=%fused_computation.98 | convolution fusion | flops 150994944 | bytes 5013504 | tf_op jit(solution)/shard_map/dot_general | solution.py:182
  (101 shorter events, 24.3 us)
Async XLA Ops:
  11.0 7.4 %copy-start.7 = (bf16[3,64,768]{2,1,0:T(8,128)(2,1)S(1)}, bf16[3,64,768]{2,1,0:T(8,128)(2,1)}, u32[]{:S(2)}) copy-start(bf16[3,64,768]{2,1,0:T(8,128)(2,1)} %param.17) | copy-start | bytes 884740
  14.9 10.1 %copy-start.9 = (f32[3,3072]{1,0:T(4,128)}, f32[3,3072]{1,0:T(4,128)S(1)}, u32[]{:S(2)}) copy-start(f32[3,3072]{1,0:T(4,128)S(1)} %pad_maximum_fusion) | copy-start | bytes 110596
  15.5 30.9 %collective-permute-start = (f32[3,1536]{1,0:T(4,128)}, f32[3,1536]{1,0:T(4,128)}, u32[]{:S(2)}, u32[]{:S(2)}) collective-permute-start(f32[3,1536]{1,0:T(4,128)} %constant_dynamic-slice_fusion), channel_id=1, source_target_pairs={{0,4},{4,0},{1,5},{5,1},{2,6},{6,2},{3,7},{7,3},{8,12},{12,8},{9,1... | collective-permute-start | bytes 55304 | tf_op jit(solution)/shard_map/ppermute | solution.py:32
  24.9 3.3 %copy-start = (bf16[3,64,3072]{2,1,0:T(8,128)(2,1)S(1)}, bf16[3,64,3072]{2,1,0:T(8,128)(2,1)}, u32[]{:S(2)}) copy-start(bf16[3,64,3072]{2,1,0:T(8,128)(2,1)} %param.14) | copy-start | bytes 3538948
  42.1 0.7 copy-start.1
  46.3 6.7 %copy-start.4 = (f32[1536,64]{0,1:T(8,128)S(1)}, f32[1536,64]{0,1:T(8,128)}, u32[]{:S(2)}) copy-start(f32[1536,64]{0,1:T(8,128)} %fusion.9) | copy-start | bytes 1179652
  46.3 7.2 %copy-start.3 = (f32[1536,64]{0,1:T(8,128)S(1)}, f32[1536,64]{0,1:T(8,128)}, u32[]{:S(2)}) copy-start(f32[1536,64]{0,1:T(8,128)} %fusion.13) | copy-start | bytes 1179652
  46.3 9.4 %copy-start.10 = (f32[64,64]{1,0:T(8,128)S(1)}, f32[64,64]{1,0:T(8,128)}, u32[]{:S(2)}) copy-start(f32[64,64]{1,0:T(8,128)} %convolution_select_fusion) | copy-start | bytes 49156
  46.3 9.6 %copy-start.2 = (bf16[1,512,128]{2,1,0:T(8,128)(2,1)S(1)}, bf16[1,512,128]{2,1,0:T(8,128)(2,1)}, u32[]{:S(2)}) copy-start(bf16[1,512,128]{2,1,0:T(8,128)(2,1)} %copy-done.1) | copy-start | bytes 393220
  46.3 9.6 %copy-start.5 = (f32[512,128]{1,0:T(8,128)S(1)}, f32[512,128]{1,0:T(8,128)}, u32[]{:S(2)}) copy-start(f32[512,128]{1,0:T(8,128)} %fusion.38) | copy-start | bytes 786436
  47.2 2.9 %copy-start.8 = (f32[3,1536]{1,0:T(4,128)}, f32[3,1536]{1,0:T(4,128)S(1)}, u32[]{:S(2)}) copy-start(f32[3,1536]{1,0:T(4,128)S(1)} %get-tuple-element.15) | copy-start | bytes 55300
  54.0 19.3 %copy-start.12 = (f32[64,64]{1,0:T(8,128)S(1)}, f32[64,64]{1,0:T(8,128)}, u32[]{:S(2)}) copy-start(f32[64,64]{1,0:T(8,128)} %convolution_multiply_fusion.6) | copy-start | bytes 49156
  54.9 18.8 %copy-start.6 = (f32[128,128]{1,0:T(8,128)S(1)}, f32[128,128]{1,0:T(8,128)}, u32[]{:S(2)}) copy-start(f32[128,128]{1,0:T(8,128)} %constant.62.clone.1) | copy-start | bytes 196612
  55.9 8.3 %collective-permute-start.1 = (f32[216,128]{1,0:T(8,128)S(1)}, f32[216,128]{1,0:T(8,128)S(1)}, u32[]{:S(2)}, u32[]{:S(2)}) collective-permute-start(f32[216,128]{1,0:T(8,128)S(1)} %constant_dynamic-update-slice_fusion), channel_id=1, source_target_pairs={{0,8},{8,0},{16,24},{24,16},{1,9},{9,1},{17,25},{25,17},{2,10},{10... | collective-permute-start | bytes 331784 | tf_op jit(solution)/shard_map/ppermute | solution.py:32
  64.1 10.2 %copy-start.11 = (f32[64,64]{1,0:T(8,128)S(1)}, f32[64,64]{1,0:T(8,128)}, u32[]{:S(2)}) copy-start(f32[64,64]{1,0:T(8,128)} %convolution_multiply_fusion.7) | copy-start | bytes 49156
  64.2 6.7 %collective-permute-start.4 = (f32[216,128]{1,0:T(8,128)S(1)}, f32[216,128]{1,0:T(8,128)S(1)}, u32[]{:S(2)}, u32[]{:S(2)}) collective-permute-start(f32[216,128]{1,0:T(8,128)S(1)} %add.253), channel_id=1, source_target_pairs={{0,20},{4,16},{8,28},{12,24},{16,4},{20,0},{24,12},{28,8},{1,21},{... | collective-permute-start | bytes 331784 | tf_op jit(solution)/shard_map/ppermute | solution.py:32
  65.7 6.5 %collective-permute-start.3 = (f32[216,128]{1,0:T(8,128)S(1)}, f32[216,128]{1,0:T(8,128)S(1)}, u32[]{:S(2)}, u32[]{:S(2)}) collective-permute-start(f32[216,128]{1,0:T(8,128)S(1)} %add.253), channel_id=1, source_target_pairs={{0,4},{4,0},{8,12},{12,8},{16,20},{20,16},{24,28},{28,24},{1,5},{5... | collective-permute-start | bytes 331784 | tf_op jit(solution)/shard_map/ppermute | solution.py:32
  67.2 5.0 %collective-permute-start.2 = (f32[216,128]{1,0:T(8,128)S(1)}, f32[216,128]{1,0:T(8,128)S(1)}, u32[]{:S(2)}, u32[]{:S(2)}) collective-permute-start(f32[216,128]{1,0:T(8,128)S(1)} %add.253), channel_id=1, source_target_pairs={{0,16},{4,20},{8,24},{12,28},{16,0},{20,4},{24,8},{28,12},{1,17},{... | collective-permute-start | bytes 331784 | tf_op jit(solution)/shard_map/ppermute | solution.py:32
  79.9 7.8 %collective-permute-start.7 = (f32[96,128]{1,0:T(8,128)S(1)}, f32[96,128]{1,0:T(8,128)S(1)}, u32[]{:S(2)}, u32[]{:S(2)}) collective-permute-start(f32[96,128]{1,0:T(8,128)S(1)} %fusion.105), channel_id=1, source_target_pairs={{0,3},{1,2},{2,1},{3,0},{4,7},{5,6},{6,5},{7,4},{8,11},{9,10},{10,... | collective-permute-start | bytes 147464 | tf_op jit(solution)/shard_map/ppermute | solution.py:32
  83.6 4.1 %collective-permute-start.5 = (f32[96,128]{1,0:T(8,128)S(1)}, f32[96,128]{1,0:T(8,128)S(1)}, u32[]{:S(2)}, u32[]{:S(2)}) collective-permute-start(f32[96,128]{1,0:T(8,128)S(1)} %fusion.105), channel_id=1, source_target_pairs={{0,1},{1,0},{2,3},{3,2},{8,10},{9,11},{10,8},{11,9},{16,17},{17,16... | collective-permute-start | bytes 147464 | tf_op jit(solution)/shard_map/ppermute | solution.py:53
  87.7 1.2 %collective-permute-start.6 = (f32[96,128]{1,0:T(8,128)S(1)}, f32[96,128]{1,0:T(8,128)S(1)}, u32[]{:S(2)}, u32[]{:S(2)}) collective-permute-start(f32[96,128]{1,0:T(8,128)S(1)} %collective-permute-done.5), channel_id=1, source_target_pairs={{0,8},{8,0},{16,24},{24,16},{1,9},{9,1},{17,25},{25,17},{2,10},{10... | collective-permute-start | bytes 147464 | tf_op jit(solution)/shard_map/ppermute | solution.py:32

commit v2 on v1

--- a/solution.py
+++ b/solution.py
@@ -3,6 +3,8 @@
 import jax
 import jax.numpy as jnp
 from jax import lax
+from jax.experimental import pallas as pl
+from jax.experimental.pallas import tpu as pltpu
 from jax.sharding import PartitionSpec as P
 
 D = 3072
@@ -80,7 +82,7 @@
     )
 
 
-def body(
+def plain_body(
     gen_noise, renoise, gen_step, renoise_step, text_pooled, embed, mod_weight, proj_weight, unembed
 ):
     rows, cols = proj_weight.shape[1], proj_weight.shape[2]
@@ -188,9 +190,395 @@
     return (gen_grad, score_gap[None])
 
 
+def vmem_params():
+    return pltpu.CompilerParams(vmem_limit_bytes=48 * 1024 * 1024)
+
+
+def whole_specs(count):
+    return [pl.BlockSpec(memory_space=pltpu.VMEM)] * count
+
+
+def split_two(x):
+    high = x.astype(jnp.bfloat16)
+    return high, (x - high.astype(jnp.float32)).astype(jnp.bfloat16)
+
+
+def split_three(x):
+    high = x.astype(jnp.bfloat16)
+    rest = x - high.astype(jnp.float32)
+    middle = rest.astype(jnp.bfloat16)
+    return high, middle, (rest - middle.astype(jnp.float32)).astype(jnp.bfloat16)
+
+
+def lane_index(shape):
+    return lax.broadcasted_iota(jnp.int32, shape, len(shape) - 1)
+
+
+def block_diagonal(left_copy, right_copy):
+    lanes = lane_index(left_copy.shape)
+    top = jnp.where(lanes < CH, left_copy, 0.0)
+    bottom = jnp.where(lanes >= CH, right_copy, 0.0)
+    return jnp.concatenate([top, bottom], 0)
+
+
+MOD_PIECES = 4
+
+
+def mod_kernel(vec_ref, weight_ref, out_ref, buffer, sems):
+    width = buffer.shape[2]
+    depth = buffer.shape[1] // MOD_PIECES
+    start = pl.multiple_of((lax.axis_index("mp") % 2) * width, 128)
+
+    def piece(m, k):
+        part = pl.ds(k * depth, depth)
+        return pltpu.make_async_copy(
+            weight_ref.at[m, part, pl.ds(start, width)], buffer.at[m, part], sems.at[m, k]
+        )
+
+    for m in range(3):
+        for k in range(MOD_PIECES):
+            piece(m, k).start()
+    rows = []
+    for m in range(3):
+        total = jnp.zeros((8, width), jnp.float32)
+        for k in range(MOD_PIECES):
+            piece(m, k).wait()
+            part = slice(k * depth, (k + 1) * depth)
+            total += jnp.dot(
+                vec_ref[:, part], buffer[m, part], preferred_element_type=jnp.float32
+            )
+        rows.append(total)
+    out_ref[...] = jnp.zeros_like(out_ref)
+    out_ref[0:1] = rows[0][0:1]
+    out_ref[1:2] = GUIDANCE * rows[1][1:2] + (1.0 - GUIDANCE) * rows[1][2:3]
+    out_ref[2:3] = rows[2][1:2]
+
+
+def local_modulation(vectors, mod_weight, width):
+    depth = mod_weight.shape[1]
+    return pl.pallas_call(
+        mod_kernel,
+        out_shape=jax.ShapeDtypeStruct((8, width), jnp.float32),
+        in_specs=[pl.BlockSpec(memory_space=pltpu.VMEM), pl.BlockSpec(memory_space=pl.ANY)],
+        out_specs=pl.BlockSpec(memory_space=pltpu.VMEM),
+        scratch_shapes=[
+            pltpu.VMEM((3, depth, width), jnp.bfloat16),
+            pltpu.SemaphoreType.DMA((3, MOD_PIECES)),
+        ],
+        compiler_params=vmem_params(),
+        cost_estimate=pl.CostEstimate(
+            flops=48 * depth * width, bytes_accessed=6 * depth * width, transcendentals=0
+        ),
+        name="modulation",
+    )(vectors, mod_weight)
+
+
+PROJ_PIECES = 2
+
+
+def weights_kernel(
+    embed_ref, unembed_ref, proj_ref, through_ref, direct_ref, gram_ref, rows_ref, buffer, sems
+):
+    rows, cols = buffer.shape[1:]
+    depth = rows // PROJ_PIECES
+
+    def piece(m, k):
+        part = pl.ds(k * depth, depth)
+        return pltpu.make_async_copy(proj_ref.at[m, part], buffer.at[m, part], sems.at[m, k])
+
+    for m in range(3):
+        for k in range(PROJ_PIECES):
+            piece(m, k).start()
+    f = lax.axis_index("fsdp")
+    row_start = pl.multiple_of(f * rows, 128)
+    col_start = pl.multiple_of(lax.axis_index("mp") * cols, 128)
+    contract = (((1,), (1,)), ((), ()))
+    for m in range(3):
+        whole = embed_ref[m].astype(jnp.float32)
+        average = jnp.sum(whole, axis=1, keepdims=True) * (1.0 / D)
+        centred = whole - average
+        high, low = split_two(centred)
+        high_high = lax.dot_general(high, high, contract, preferred_element_type=jnp.float32)
+        high_low = lax.dot_general(high, low, contract, preferred_element_type=jnp.float32)
+        low_low = lax.dot_general(low, low, contract, preferred_element_type=jnp.float32)
+        gram = (high_high + (high_low + high_low.T) + low_low) * (1.0 / D)
+        gram = jnp.concatenate([gram, gram], 1)
+        gram_ref[m] = jnp.concatenate(split_three(block_diagonal(gram, gram)), 1)
+        rows_ref[m] = embed_ref[m, :, pl.ds(row_start, rows)].astype(jnp.float32) - average
+        nothing = jnp.zeros((CH, cols), jnp.bfloat16)
+        left = jnp.concatenate([unembed_ref[m], nothing], 0)
+        direct = lax.dot_general(
+            embed_ref[m, :, pl.ds(col_start, cols)],
+            left,
+            contract,
+            preferred_element_type=jnp.float32,
+        )
+        direct_ref[m] = jnp.where(f == 0, direct, 0.0)
+    for m in range(3):
+        right = jnp.concatenate([jnp.zeros((CH, cols), jnp.bfloat16), unembed_ref[m]], 0)
+        for k in range(PROJ_PIECES):
+            piece(m, k).wait()
+            part = slice(k * depth, (k + 1) * depth)
+            through_ref[m, part] = lax.dot_general(
+                buffer[m, part], right, contract, preferred_element_type=jnp.float32
+            ).astype(jnp.bfloat16)
+
+
+def weight_products(embed, unembed, proj_weight):
+    rows, cols = proj_weight.shape[1:]
+    return pl.pallas_call(
+        weights_kernel,
+        out_shape=[
+            jax.ShapeDtypeStruct((3, rows, 2 * CH), jnp.bfloat16),
+            jax.ShapeDtypeStruct((3, CH, 2 * CH), jnp.float32),
+            jax.ShapeDtypeStruct((3, 2 * CH, 6 * CH), jnp.bfloat16),
+            jax.ShapeDtypeStruct((3, CH, rows), jnp.float32),
+        ],
+        in_specs=whole_specs(2) + [pl.BlockSpec(memory_space=pl.ANY)],
+        out_specs=whole_specs(4),
+        scratch_shapes=[
+            pltpu.VMEM((3, rows, cols), jnp.bfloat16),
+            pltpu.SemaphoreType.DMA((3, PROJ_PIECES)),
+        ],
+        compiler_params=vmem_params(),
+        cost_estimate=pl.CostEstimate(
+            flops=12 * CH * rows * cols, bytes_accessed=6 * rows * cols, transcendentals=0
+        ),
+        name="weight_products",
+    )(embed, unembed, proj_weight)
+
+
+def maps_kernel(mine_ref, first_ref, second_ref, rows_ref, through_ref, direct_ref, maps_ref, mod_ref):
+    rows = rows_ref.shape[2]
+    f = lax.axis_index("fsdp")
+    core = lax.axis_index("mp") % 2
+    mine, first, second = mine_ref[...], first_ref[...], second_ref[...]
+    shift = jnp.where(f == 0, jnp.where(core == 0, mine, first), jnp.where(core == 0, second, first))
+    scale = jnp.where(f == 0, jnp.where(core == 0, first, second), jnp.where(core == 0, first, mine))
+    for m in range(3):
+        left = jnp.concatenate(
+            [
+                rows_ref[m] * (1.0 + scale[m : m + 1]),
+                shift[m : m + 1],
+                jnp.zeros((7, rows), jnp.float32),
+            ],
+            0,
+        )
+        product = jnp.dot(
+            left.astype(jnp.bfloat16), through_ref[m], preferred_element_type=jnp.float32
+        )
+        base = m * (CH + 8)
+        maps_ref[base : base + CH] = product[:CH] + direct_ref[m]
+        maps_ref[base + CH : base + CH + 8] = product[CH:]
+    for j in range(rows // 128):
+        part = slice(j * 128, (j + 1) * 128)
+        mod_ref[j : j + 1] = shift[0:1, part]
+        mod_ref[rows // 128 + j : rows // 128 + j + 1] = scale[0:1, part]
+
+
+def modulated_maps(mine, first, second, rows_part, through, direct):
+    rows = rows_part.shape[2]
+    return pl.pallas_call(
+        maps_kernel,
+        out_shape=[
+            jax.ShapeDtypeStruct((3 * (CH + 8), 2 * CH), jnp.float32),
+            jax.ShapeDtypeStruct((2 * rows // 128, 128), jnp.float32),
+        ],
+        in_specs=whole_specs(6),
+        out_specs=whole_specs(2),
+        compiler_params=vmem_params(),
+        name="modulated_maps",
+    )(mine, first, second, rows_part, through, direct)
+
+
+def token_kernel(
+    level_ref,
+    noise_ref,
+    noise_other_ref,
+    renoise_ref,
+    renoise_other_ref,
+    gram_ref,
+    maps_a,
+    maps_b,
+    maps_c,
+    maps_d,
+    mod_ref,
+    score_ref,
+    payload_ref,
+):
+    half = noise_ref.shape[0]
+    level = level_ref[0]
+    maps = (maps_a[...] + maps_b[...]) + (maps_c[...] + maps_d[...])
+    width = 2 * CH
+    lanes = lane_index((width, width))
+    subs = lax.broadcasted_iota(jnp.int32, (width, width), 0)
+    ones = jnp.where((lanes < CH) == (subs < CH), 1.0, 0.0).astype(jnp.bfloat16)
+    ones = jnp.concatenate([ones, ones], 0)
+
+    def model_matrix(m):
+        base = m * (CH + 8)
+        pair = maps[base : base + CH]
+        turned = pltpu.roll(pair, CH, 1)
+        direct = split_two(block_diagonal(pair, turned))
+        modulated = split_two(block_diagonal(turned, pair))
+        offset = maps[base + CH : base + CH + 1]
+        offset = offset + pltpu.roll(offset, CH, 1)
+        return jnp.concatenate(direct + modulated + (gram_ref[m],), 1), offset
+
+    def inverse_deviation(u, by_gram):
+        squares = jnp.concatenate(split_two(by_gram * u), 1)
+        spread = jnp.dot(squares, ones, preferred_element_type=jnp.float32)
+        return lax.rsqrt(jnp.maximum(spread, 0.0) + EPS_NORM)
+
+    def model(u, product, offset):
+        part = [product[:, i * width : (i + 1) * width] for i in range(7)]
+        inverse = inverse_deviation(u.astype(jnp.float32), part[4] + part[5] + part[6])
+        return (part[0] + part[1]) + inverse * (part[2] + part[3]) + offset, inverse
+
+    matrices = [model_matrix(m) for m in range(3)]
+    noise = jnp.concatenate([noise_ref[...], noise_other_ref[...]], 0).astype(jnp.bfloat16)
+    renoise = jnp.concatenate([renoise_ref[...], renoise_other_ref[...]], 0)
+    product = jnp.dot(noise, matrices[0][0], preferred_element_type=jnp.float32)
+    clean, inverse = model(noise, product, matrices[0][1])
+    noise_norm = noise.astype(jnp.float32) * inverse
+    noisy = ((1.0 - level) * clean + level * renoise).astype(jnp.bfloat16)
+    product = jnp.dot(noisy, matrices[1][0], preferred_element_type=jnp.float32)
+    real_v, _ = model(noisy, product, matrices[1][1])
+    product = jnp.dot(noisy, matrices[2][0], preferred_element_type=jnp.float32)
+    fake_v, _ = model(noisy, product, matrices[2][1])
+    total = jnp.sum(jnp.abs(clean - renoise + real_v))
+    gap_scale = level * total * (1.0 / (2 * half * width)) + EPS_GAP
+    score = level * (real_v - fake_v) / gap_scale
+    score_ref[...] = score[:half]
+    tokens = 4 * half * lax.axis_size("dp")
+    cotangent = (score * (1.0 / math.sqrt(tokens))).astype(jnp.bfloat16)
+    pairs = lax.dot_general(
+        noise_norm.astype(jnp.bfloat16),
+        cotangent,
+        (((0,), (0,)), ((), ())),
+        preferred_element_type=jnp.float32,
+    )
+    payload_ref[:CH] = pairs[:CH] + pltpu.roll(pairs[CH:], CH, 1)
+    sums = jnp.sum(cotangent.astype(jnp.float32), axis=0, keepdims=True)
+    payload_ref[CH : CH + 8] = jnp.concatenate(
+        [sums + pltpu.roll(sums, CH, 1), jnp.zeros((7, width), jnp.float32)], 0
+    )
+    payload_ref[CH + 8 :] = mod_ref[...]
+
+
+def token_phase(level, noise, noise_other, renoise, renoise_other, gram, maps, mod):
+    half = noise.shape[0]
+    return pl.pallas_call(
+        token_kernel,
+        out_shape=[
+            jax.ShapeDtypeStruct((half, 2 * CH), jnp.float32),
+            jax.ShapeDtypeStruct((CH + 8 + mod.shape[0], 2 * CH), jnp.float32),
+        ],
+        in_specs=[pl.BlockSpec(memory_space=pltpu.SMEM)] + whole_specs(10),
+        out_specs=whole_specs(2),
+        compiler_params=vmem_params(),
+        name="tokens",
+    )(level, noise, noise_other, renoise, renoise_other, gram, *maps, mod)
+
+
+GRAD_TILE = 256
+
+
+def grad_kernel(block_a, block_b, block_c, block_d, rows_ref, unembed_ref, grad_ref):
+    tile = grad_ref.shape[0]
+    step = pl.program_id(0)
+    count = (block_a.shape[0] - CH - 8) // 2
+    per_tile = tile // 128
+    lefts, rights = [], []
+    embed_rows = rows_ref[0]
+    for block in (block_a, block_b, block_c, block_d):
+        lefts.append(block[: CH + 8])
+        shift, scale = [], []
+        for j in range(per_tile):
+            shift.append(block[pl.ds(CH + 8 + step * per_tile + j, 1)])
+            scale.append(block[pl.ds(CH + 8 + count + step * per_tile + j, 1)])
+        rights += [
+            embed_rows * (1.0 + jnp.concatenate(scale, 1)),
+            jnp.concatenate(shift, 1),
+            jnp.zeros((7, tile), jnp.float32),
+        ]
+    left = jnp.concatenate(lefts, 0)[:, :CH].astype(jnp.bfloat16)
+    right = jnp.concatenate(rights, 0).astype(jnp.bfloat16)
+    grad_map = lax.dot_general(
+        right, left, (((0,), (0,)), ((), ())), preferred_element_type=jnp.float32
+    )
+    grad_ref[...] = jnp.dot(
+        grad_map.astype(jnp.bfloat16), unembed_ref[0], preferred_element_type=jnp.float32
+    )
+
+
+def gradient(blocks, rows_part, unembed):
+    rows = rows_part.shape[2]
+    cols = unembed.shape[2]
+    block_spec = pl.BlockSpec(blocks[0].shape, lambda i: (0, 0))
+    return pl.pallas_call(
+        grad_kernel,
+        grid=(rows // GRAD_TILE,),
+        out_shape=jax.ShapeDtypeStruct((rows, cols), jnp.float32),
+        in_specs=[block_spec] * 4
+        + [
+            pl.BlockSpec((1, CH, GRAD_TILE), lambda i: (0, 0, i)),
+            pl.BlockSpec((1, CH, cols), lambda i: (0, 0, 0)),
+        ],
+        out_specs=pl.BlockSpec((GRAD_TILE, cols), lambda i: (i, 0)),
+        compiler_params=vmem_params(),
+        name="gradient",
+    )(*blocks, rows_part, unembed)
+
+
+def exchange_halves(x):
+    pairs_first, pairs_second = [], []
+    for chip in range(2):
+        for y, core, to_y, to_core in ((1, 0, 0, 0), (0, 0, 0, 1), (0, 1, 1, 1), (1, 1, 1, 0)):
+            pairs_first.append((chip * 4 + core * 2 + y, chip * 4 + to_core * 2 + to_y))
+        for y, core, to_y, to_core in ((1, 0, 0, 1), (0, 1, 1, 0)):
+            pairs_second.append((chip * 4 + core * 2 + y, chip * 4 + to_core * 2 + to_y))
+    axes = ("mp", "fsdp")
+    return lax.ppermute(x, axes, pairs_first), lax.ppermute(x, axes, pairs_second)
+
+
+def body(
+    gen_noise, renoise, gen_step, renoise_step, text_pooled, embed, mod_weight, proj_weight, unembed
+):
+    blank_text = jnp.zeros_like(text_pooled)
+    vectors = jnp.concatenate(
+        [
+            condition(gen_step, text_pooled),
+            condition(renoise_step, text_pooled),
+            condition(renoise_step, blank_text),
+            jnp.zeros((5, TEMB + text_pooled.shape[1]), jnp.bfloat16),
+        ],
+        axis=0,
+    )
+    mine = local_modulation(vectors, mod_weight, mod_weight.shape[2] // 2)
+    first, second = exchange_halves(mine)
+    noise_other = swap(gen_noise[0], "fsdp", 1)
+    renoise_other = swap(renoise[0], "fsdp", 1)
+    through, direct, gram, rows_part = weight_products(embed, unembed, proj_weight)
+    maps, mod = modulated_maps(mine, first, second, rows_part, through, direct)
+    maps = maps + swap(maps, "mp", 1)
+    plane = ("mp", "fsdp")
+    maps = [maps] + [swap(maps, plane, mask) for mask in (4, 1, 5)]
+    level = renoise_step.astype(jnp.float32) / 1000.0
+    score_gap, payload = token_phase(
+        level, gen_noise[0], noise_other, renoise[0], renoise_other, gram, maps, mod
+    )
+    blocks = gather_samples(payload)
+    return (gradient(blocks, rows_part, unembed), score_gap[None])
+
+
+def fits_kernels(mesh):
+    return mesh.shape["mp"] == 4 and mesh.shape["fsdp"] == 2 and mesh.shape["dp"] == 4
+
+
 def solution(mesh):
     return jax.shard_map(
-        body,
+        body if fits_kernels(mesh) else plain_body,
         mesh=mesh,
         in_specs=(
             P("dp", "fsdp", None),

time: 94.5 us -> 47.1 us (0.50)
  matrix products: 52.4 us -> 0 us
  Pallas kernels: 0 us -> 17.7 us
  blocking collectives: 11.9 us -> 0 us
  other arithmetic: 6.31 us -> 0.92 us
  waiting for transfers between devices: 6.67 us -> 11.3 us
  starting transfers between devices: 10.3 us -> 14.9 us
  local copies, waits for them, and re-layouts: 2.89 us -> 0.11 us
  between operations: 3.02 us -> 2.02 us
    dot_general x36 -> x0, matrix products: 52.4 us -> none  [the longest x26 22.6 us: dot(): jnp.dot(a, b, precision=precision, preferred_element_type=jnp.float32)]
    pallas_call x0 -> x5, Pallas kernels: none -> 17.7 us  [the longest x1 6.41 us: weight_products(): pl.pallas_call(weights_kernel, out_shape=[jax.ShapeDtypeStruct((3, rows,...]
    all_gather x2 -> x0, blocking collectives: 11.9 us -> none  [the longest x1 6.95 us: body(): renoise_all = lax.all_gather(renoise[0], 'fsdp', axis=0, tiled=True)]
    ppermute x7 -> x8, waiting for transfers between devices: 3.75 us -> 11.1 us  [swap(): return lax.ppermute(x, axes, [(i, i ^ mask) for i in range(count)])]
    ppermute x0 -> x2, starting transfers between devices: none -> 5.14 us  [the longest x1 4.34 us: exchange_halves(): lax.ppermute(x, axes, pairs_first)]
    ppermute x1, waiting for transfers between devices: 2.92 us -> 0.14 us  [gather_samples(): near = lax.ppermute(x, ('mp', 'dp'), pairs)]
    unnamed x4 -> x0, other arithmetic: 2.7 us -> none
    ppermute x7 -> x8, starting transfers between devices: 10.3 us -> 8.21 us  [swap(): return lax.ppermute(x, axes, [(i, i ^ mask) for i in range(count)])]
  transfers between devices with their start and end apart: 8 -> 11, of which waited for: 4 -> 5; matrix products, arithmetic and copies ran while one was open for 28% -> 0% of each run, Pallas kernels for 0% -> 14%
where the time goes in v2:
time: 47.1 us; the launch traced here: 46.9 us
  Pallas kernels  17.7 us (38%)
  starting transfers between devices  14.9 us (32%)
  waiting for transfers between devices  11.3 us (24%)
  between operations  2.02 us (4%)
  other arithmetic  0.92 us (2%)
    ppermute x8, waiting for transfers between devices, swap(): return lax.ppermute(x, axes, [(i, i ^ mask) for i in range(count)])  11.1 us
    ppermute x8, starting transfers between devices, swap(): return lax.ppermute(x, axes, [(i, i ^ mask) for i in range(count)])  8.21 us
    pallas_call x1, Pallas kernels, weight_products(): pl.pallas_call(weights_kernel, out_shape=[jax.ShapeDtypeStruct((3, rows,...  6.41 us
    pallas_call x1, Pallas kernels, gradient(): pl.pallas_call(grad_kernel, grid=(rows // GRAD_TILE,), out_shape=jax.Shap...  4.74 us
    ppermute x1, starting transfers between devices, exchange_halves(): lax.ppermute(x, axes, pairs_first)  4.34 us
    pallas_call x1, Pallas kernels, local_modulation(): pl.pallas_call(mod_kernel, out_shape=jax.ShapeDtypeStruct((8, width), jnp...  4.12 us
    pallas_call x1, Pallas kernels, token_phase(): pl.pallas_call(token_kernel, out_shape=[jax.ShapeDtypeStruct((half, 2 * C...  2.03 us
    ppermute x1, starting transfers between devices, gather_samples(): near = lax.ppermute(x, ('mp', 'dp'), pairs)  1.57 us
  transfers between devices with their start and end apart: 11, of which 5 were waited for; matrix products, arithmetic and copies ran while one was open for 0% of the time, Pallas kernels for 14%

profile of v2, /device:TPU:0, one launch (start us, length us, event | category | flops | bytes accessed | tf_op | source)
XLA Modules:
  0.0 46.9 jit_solution(9790393538125305724)
XLA Ops:
  2.0 0.1 sine_bitcast_fusion
  2.0 0.7 %convert_element_type.50 = f32[1,768]{1,0:T(1,128)S(1)} convert(bf16[1,768]{1,0:T(2,128)(2,1)} %param.13) | non-fusion elementwise | flops 768 | bytes 4608 | tf_op jit(solution)/shard_map/convert_element_type | solution.py:28
  2.7 0.1 pad.3.clone
  2.9 0.1 maximum_maximum_fusion.vec_ref
  2.9 4.1 %modulation.1.mine_ref = f32[8,1536]{1,0:T(8,128)S(1)} custom-call(bf16[8,1024]{1,0:T(8,128)(2,1)S(1)} %maximum_maximum_fusion.vec_ref, bf16[3,1024,3072]{2,1,0:T(8,128)(2,1)} %weight_ref.1), custom_call_target="tpu_custom_call" | custom-call | flops 75497472 | bytes 9437184 | tf_op jit(solution)/shard_map/modulation/pallas_call | solution.py:259
  7.1 0.8 %collective-permute-start.3 = (f32[8,1536]{1,0:T(8,128)S(1)}, f32[8,1536]{1,0:T(8,128)S(1)}, u32[]{:S(2)}, u32[]{:S(2)}) collective-permute-start(f32[8,1536]{1,0:T(8,128)S(1)} %modulation.1.mine_ref), channel_id=1, source_target_pairs={{4,8},{8,4},{20,24},{24,20},{5,9},{9,5},{21,25},{25,21},{6,10},{10... | collective-permute-start | bytes 147464 | tf_op jit(solution)/shard_map/ppermute | solution.py:542
  7.9 4.3 %collective-permute-start.2 = (f32[8,1536]{1,0:T(8,128)S(1)}, f32[8,1536]{1,0:T(8,128)S(1)}, u32[]{:S(2)}, u32[]{:S(2)}) collective-permute-start(f32[8,1536]{1,0:T(8,128)S(1)} %modulation.1.mine_ref), channel_id=1, source_target_pairs={{4,0},{0,8},{8,12},{12,4},{20,16},{16,24},{24,28},{28,20},{5,1},{1... | collective-permute-start | bytes 147464 | tf_op jit(solution)/shard_map/ppermute | solution.py:542
  12.2 6.4 %weight_products.1 = (bf16[3,1536,128]{2,1,0:T(8,128)(2,1)S(1)}, f32[3,64,128]{2,1,0:T(8,128)S(1)}, bf16[3,128,384]{2,1,0:T(8,128)(2,1)S(1)}, f32[3,64,1536]{2,1,0:T(8,128)S(1)}) custom-call(bf16[3,64,3072]{2,1,0:T(8,128)(2,1)S(1)} %copy-done.1, bf16[3,64,768]{2,1,0:T(8,128)(2,1)S(1)} %copy-done, bf16[3,1536,768]{2,1,0:T(8,128)(2,1)} %proj_ref.1), custom_call_target="tpu_custom_call" | custom-call | flops 905969664 | bytes 7077888 | tf_op jit(solution)/shard_map/weight_products/pallas_call | solution.py:329
  18.7 0.4 modulated_maps.1
  19.0 0.1 collective-permute-start.4
  19.1 0.4 collective-permute-start
  19.5 1.7 %collective-permute-start.1 = (f32[256,128]{1,0:T(8,128)S(1)}, f32[256,128]{1,0:T(8,128)S(1)}, u32[]{:S(2)}, u32[]{:S(2)}) collective-permute-start(f32[256,128]{1,0:T(8,128)S(1)} %bitcast.16), channel_id=1, source_target_pairs={{0,4},{4,0},{1,5},{5,1},{2,6},{6,2},{3,7},{7,3},{8,12},{12,8},{9,1... | collective-permute-start | bytes 393224 | tf_op jit(solution)/shard_map/ppermute | solution.py:34
  21.2 1.3 %collective-permute-start.7 = (f32[216,128]{1,0:T(8,128)S(1)}, f32[216,128]{1,0:T(8,128)S(1)}, u32[]{:S(2)}, u32[]{:S(2)}) collective-permute-start(f32[216,128]{1,0:T(8,128)S(1)} %add.40.maps_a), channel_id=1, source_target_pairs={{0,20},{4,16},{8,28},{12,24},{16,4},{20,0},{24,12},{28,8},{1,21},{... | collective-permute-start | bytes 331784 | tf_op jit(solution)/shard_map/ppermute | solution.py:34
  22.6 1.7 %collective-permute-start.6 = (f32[216,128]{1,0:T(8,128)S(1)}, f32[216,128]{1,0:T(8,128)S(1)}, u32[]{:S(2)}, u32[]{:S(2)}) collective-permute-start(f32[216,128]{1,0:T(8,128)S(1)} %add.40.maps_a), channel_id=1, source_target_pairs={{0,4},{4,0},{8,12},{12,8},{16,20},{20,16},{24,28},{28,24},{1,5},{5... | collective-permute-start | bytes 331784 | tf_op jit(solution)/shard_map/ppermute | solution.py:34
  24.3 0.5 %collective-permute-start.5 = (f32[216,128]{1,0:T(8,128)S(1)}, f32[216,128]{1,0:T(8,128)S(1)}, u32[]{:S(2)}, u32[]{:S(2)}) collective-permute-start(f32[216,128]{1,0:T(8,128)S(1)} %add.40.maps_a), channel_id=1, source_target_pairs={{0,16},{4,20},{8,24},{12,28},{16,0},{20,4},{24,8},{28,12},{1,17},{... | collective-permute-start | bytes 331784 | tf_op jit(solution)/shard_map/ppermute | solution.py:34
  24.8 2.8 %collective-permute-done.noise_other_ref = f32[256,128]{1,0:T(8,128)S(1)} collective-permute-done((f32[256,128]{1,0:T(8,128)S(1)}, f32[256,128]{1,0:T(8,128)S(1)}, u32[]{:S(2)}, u32[]{:S(2)}) %collective-permute-start) | collective-permute-done | bytes 131104 | tf_op jit(solution)/shard_map/ppermute | solution.py:34
  27.6 3.1 %collective-permute-done.1.renoise_other_ref = f32[256,128]{1,0:T(8,128)S(1)} collective-permute-done((f32[256,128]{1,0:T(8,128)S(1)}, f32[256,128]{1,0:T(8,128)S(1)}, u32[]{:S(2)}, u32[]{:S(2)}) %collective-permute-start.1) | collective-permute-done | bytes 131104 | tf_op jit(solution)/shard_map/ppermute | solution.py:34
  30.7 1.9 %collective-permute-done.6.maps_c = f32[216,128]{1,0:T(8,128)S(1)} collective-permute-done((f32[216,128]{1,0:T(8,128)S(1)}, f32[216,128]{1,0:T(8,128)S(1)}, u32[]{:S(2)}, u32[]{:S(2)}) %collective-permute-start.6) | collective-permute-done | bytes 110624 | tf_op jit(solution)/shard_map/ppermute | solution.py:34
  32.6 2.0 %tokens.1 = (f32[256,128]{1,0:T(8,128)}, f32[96,128]{1,0:T(8,128)S(1)}) custom-call(f32[1]{0:T(128)S(6)} %div.46.level_ref, f32[256,128]{1,0:T(8,128)S(1)} %bitcast.15, f32[256,128]{1,0:T(8,128)S(1)} %collective-permute-done.noise_other_ref, f32[256,128]{1,0:T(8,128)S(1)} %bitcast.17, f32[256,128]{1,0:T(8,128)S(1)} %collective-permute-done.1.renoise_other_ref, ...), custom_call_target="tpu_custom_call" | custom-call | tf_op jit(solution)/shard_map/tokens/pallas_call | solution.py:471
  34.6 1.6 %collective-permute-start.8 = (f32[96,128]{1,0:T(8,128)S(1)}, f32[96,128]{1,0:T(8,128)S(1)}, u32[]{:S(2)}, u32[]{:S(2)}) collective-permute-start(f32[96,128]{1,0:T(8,128)S(1)} %get-tuple-element.16.block_a), channel_id=1, source_target_pairs={{0,1},{1,0},{2,3},{3,2},{8,10},{9,11},{10,8},{11,9},{16,17},{17,16... | collective-permute-start | bytes 147464 | tf_op jit(solution)/shard_map/ppermute | solution.py:55
  36.2 2.5 %collective-permute-start.10 = (f32[96,128]{1,0:T(8,128)S(1)}, f32[96,128]{1,0:T(8,128)S(1)}, u32[]{:S(2)}, u32[]{:S(2)}) collective-permute-start(f32[96,128]{1,0:T(8,128)S(1)} %get-tuple-element.16.block_a), channel_id=1, source_target_pairs={{0,3},{1,2},{2,1},{3,0},{4,7},{5,6},{6,5},{7,4},{8,11},{9,10},{10,... | collective-permute-start | bytes 147464 | tf_op jit(solution)/shard_map/ppermute | solution.py:34
  38.7 0.1 collective-permute-done.8.block_b
  38.8 3.3 %collective-permute-done.10.block_d = f32[96,128]{1,0:T(8,128)S(1)} collective-permute-done((f32[96,128]{1,0:T(8,128)S(1)}, f32[96,128]{1,0:T(8,128)S(1)}, u32[]{:S(2)}, u32[]{:S(2)}) %collective-permute-start.10) | collective-permute-done | bytes 49184 | tf_op jit(solution)/shard_map/ppermute | solution.py:34
  42.2 4.7 %gradient.1 = f32[1536,768]{1,0:T(8,128)} custom-call(f32[96,128]{1,0:T(8,128)S(1)} %get-tuple-element.16.block_a, f32[96,128]{1,0:T(8,128)S(1)} %collective-permute-done.8.block_b, f32[96,128]{1,0:T(8,128)S(1)} %collective-permute-done.9.block_c, f32[96,128]{1,0:T(8,128)S(1)} %collective-permute-done.10.block_d, ...), custom_call_target="tpu_custom_call" | custom-call | tf_op jit(solution)/shard_map/gradient/pallas_call | solution.py:519
  (21 shorter events, 0.2 us)
Async XLA Ops:
  2.9 9.3 %copy-start = (bf16[3,64,768]{2,1,0:T(8,128)(2,1)S(1)}, bf16[3,64,768]{2,1,0:T(8,128)(2,1)}, u32[]{:S(2)}) copy-start(bf16[3,64,768]{2,1,0:T(8,128)(2,1)} %unembed_ref.3) | copy-start | bytes 884740
  2.9 9.3 %copy-start.1 = (bf16[3,64,3072]{2,1,0:T(8,128)(2,1)S(1)}, bf16[3,64,3072]{2,1,0:T(8,128)(2,1)}, u32[]{:S(2)}) copy-start(bf16[3,64,3072]{2,1,0:T(8,128)(2,1)} %embed_ref.1) | copy-start | bytes 3538948
  7.1 12.1 %copy-start.2 = (f32[1,256,128]{2,1,0:T(8,128)S(1)}, f32[1,256,128]{2,1,0:T(8,128)}, u32[]{:S(2)}) copy-start(f32[1,256,128]{2,1,0:T(8,128)} %param.9) | copy-start | bytes 393220
  7.1 12.4 %copy-start.3 = (f32[1,256,128]{2,1,0:T(8,128)S(1)}, f32[1,256,128]{2,1,0:T(8,128)}, u32[]{:S(2)}) copy-start(f32[1,256,128]{2,1,0:T(8,128)} %param.10) | copy-start | bytes 393220
  7.1 11.6 %collective-permute-start.3 = (f32[8,1536]{1,0:T(8,128)S(1)}, f32[8,1536]{1,0:T(8,128)S(1)}, u32[]{:S(2)}, u32[]{:S(2)}) collective-permute-start(f32[8,1536]{1,0:T(8,128)S(1)} %modulation.1.mine_ref), channel_id=1, source_target_pairs={{4,8},{8,4},{20,24},{24,20},{5,9},{9,5},{21,25},{25,21},{6,10},{10... | collective-permute-start | bytes 147464 | tf_op jit(solution)/shard_map/ppermute | solution.py:542
  7.9 10.8 %collective-permute-start.2 = (f32[8,1536]{1,0:T(8,128)S(1)}, f32[8,1536]{1,0:T(8,128)S(1)}, u32[]{:S(2)}, u32[]{:S(2)}) collective-permute-start(f32[8,1536]{1,0:T(8,128)S(1)} %modulation.1.mine_ref), channel_id=1, source_target_pairs={{4,0},{0,8},{8,12},{12,4},{20,16},{16,24},{24,28},{28,20},{5,1},{1... | collective-permute-start | bytes 147464 | tf_op jit(solution)/shard_map/ppermute | solution.py:542
  19.0 2.2 %collective-permute-start.4 = (f32[216,128]{1,0:T(8,128)S(1)}, f32[216,128]{1,0:T(8,128)S(1)}, u32[]{:S(2)}, u32[]{:S(2)}) collective-permute-start(f32[216,128]{1,0:T(8,128)S(1)} %get-tuple-element.14), channel_id=1, source_target_pairs={{0,8},{8,0},{16,24},{24,16},{1,9},{9,1},{17,25},{25,17},{2,10},{10... | collective-permute-start | bytes 331784 | tf_op jit(solution)/shard_map/ppermute | solution.py:34
  19.1 8.4 %collective-permute-start = (f32[256,128]{1,0:T(8,128)S(1)}, f32[256,128]{1,0:T(8,128)S(1)}, u32[]{:S(2)}, u32[]{:S(2)}) collective-permute-start(f32[256,128]{1,0:T(8,128)S(1)} %bitcast.14), channel_id=1, source_target_pairs={{0,4},{4,0},{1,5},{5,1},{2,6},{6,2},{3,7},{7,3},{8,12},{12,8},{9,1... | collective-permute-start | bytes 393224 | tf_op jit(solution)/shard_map/ppermute | solution.py:34
  19.5 11.2 %collective-permute-start.1 = (f32[256,128]{1,0:T(8,128)S(1)}, f32[256,128]{1,0:T(8,128)S(1)}, u32[]{:S(2)}, u32[]{:S(2)}) collective-permute-start(f32[256,128]{1,0:T(8,128)S(1)} %bitcast.16), channel_id=1, source_target_pairs={{0,4},{4,0},{1,5},{5,1},{2,6},{6,2},{3,7},{7,3},{8,12},{12,8},{9,1... | collective-permute-start | bytes 393224 | tf_op jit(solution)/shard_map/ppermute | solution.py:34
  21.2 9.4 %collective-permute-start.7 = (f32[216,128]{1,0:T(8,128)S(1)}, f32[216,128]{1,0:T(8,128)S(1)}, u32[]{:S(2)}, u32[]{:S(2)}) collective-permute-start(f32[216,128]{1,0:T(8,128)S(1)} %add.40.maps_a), channel_id=1, source_target_pairs={{0,20},{4,16},{8,28},{12,24},{16,4},{20,0},{24,12},{28,8},{1,21},{... | collective-permute-start | bytes 331784 | tf_op jit(solution)/shard_map/ppermute | solution.py:34
  22.6 10.0 %collective-permute-start.6 = (f32[216,128]{1,0:T(8,128)S(1)}, f32[216,128]{1,0:T(8,128)S(1)}, u32[]{:S(2)}, u32[]{:S(2)}) collective-permute-start(f32[216,128]{1,0:T(8,128)S(1)} %add.40.maps_a), channel_id=1, source_target_pairs={{0,4},{4,0},{8,12},{12,8},{16,20},{20,16},{24,28},{28,24},{1,5},{5... | collective-permute-start | bytes 331784 | tf_op jit(solution)/shard_map/ppermute | solution.py:34
  24.3 8.3 %collective-permute-start.5 = (f32[216,128]{1,0:T(8,128)S(1)}, f32[216,128]{1,0:T(8,128)S(1)}, u32[]{:S(2)}, u32[]{:S(2)}) collective-permute-start(f32[216,128]{1,0:T(8,128)S(1)} %add.40.maps_a), channel_id=1, source_target_pairs={{0,16},{4,20},{8,24},{12,28},{16,0},{20,4},{24,8},{28,12},{1,17},{... | collective-permute-start | bytes 331784 | tf_op jit(solution)/shard_map/ppermute | solution.py:34
  34.6 4.2 %collective-permute-start.8 = (f32[96,128]{1,0:T(8,128)S(1)}, f32[96,128]{1,0:T(8,128)S(1)}, u32[]{:S(2)}, u32[]{:S(2)}) collective-permute-start(f32[96,128]{1,0:T(8,128)S(1)} %get-tuple-element.16.block_a), channel_id=1, source_target_pairs={{0,1},{1,0},{2,3},{3,2},{8,10},{9,11},{10,8},{11,9},{16,17},{17,16... | collective-permute-start | bytes 147464 | tf_op jit(solution)/shard_map/ppermute | solution.py:55
  36.2 6.0 %collective-permute-start.10 = (f32[96,128]{1,0:T(8,128)S(1)}, f32[96,128]{1,0:T(8,128)S(1)}, u32[]{:S(2)}, u32[]{:S(2)}) collective-permute-start(f32[96,128]{1,0:T(8,128)S(1)} %get-tuple-element.16.block_a), channel_id=1, source_target_pairs={{0,3},{1,2},{2,1},{3,0},{4,7},{5,6},{6,5},{7,4},{8,11},{9,10},{10,... | collective-permute-start | bytes 147464 | tf_op jit(solution)/shard_map/ppermute | solution.py:34
  38.8 3.3 %collective-permute-start.9 = (f32[96,128]{1,0:T(8,128)S(1)}, f32[96,128]{1,0:T(8,128)S(1)}, u32[]{:S(2)}, u32[]{:S(2)}) collective-permute-start(f32[96,128]{1,0:T(8,128)S(1)} %collective-permute-done.8.block_b), channel_id=1, source_target_pairs={{0,8},{8,0},{16,24},{24,16},{1,9},{9,1},{17,25},{25,17},{2,10},{10... | collective-permute-start | bytes 147464 | tf_op jit(solution)/shard_map/ppermute | solution.py:34

commit v3 on v1

--- a/solution.py
+++ b/solution.py
@@ -3,6 +3,8 @@
 import jax
 import jax.numpy as jnp
 from jax import lax
+from jax.experimental import pallas as pl
+from jax.experimental.pallas import tpu as pltpu
 from jax.sharding import PartitionSpec as P
 
 D = 3072
@@ -80,7 +82,7 @@
     )
 
 
-def body(
+def plain_body(
     gen_noise, renoise, gen_step, renoise_step, text_pooled, embed, mod_weight, proj_weight, unembed
 ):
     rows, cols = proj_weight.shape[1], proj_weight.shape[2]
@@ -188,9 +190,526 @@
     return (gen_grad, score_gap[None])
 
 
+def vmem_params():
+    return pltpu.CompilerParams(vmem_limit_bytes=48 * 1024 * 1024)
+
+
+def whole_specs(count):
+    return [pl.BlockSpec(memory_space=pltpu.VMEM)] * count
+
+
+def split_two(x):
+    high = x.astype(jnp.bfloat16)
+    return high, (x - high.astype(jnp.float32)).astype(jnp.bfloat16)
+
+
+def split_three(x):
+    high = x.astype(jnp.bfloat16)
+    rest = x - high.astype(jnp.float32)
+    middle = rest.astype(jnp.bfloat16)
+    return high, middle, (rest - middle.astype(jnp.float32)).astype(jnp.bfloat16)
+
+
+def lane_index(shape):
+    return lax.broadcasted_iota(jnp.int32, shape, len(shape) - 1)
+
+
+def block_diagonal(left_copy, right_copy):
+    lanes = lane_index(left_copy.shape)
+    top = jnp.where(lanes < CH, left_copy, 0.0)
+    bottom = jnp.where(lanes >= CH, right_copy, 0.0)
+    return jnp.concatenate([top, bottom], 0)
+
+
+MOD_PIECES = 4
+PROJ_PIECES = 2
+IN_FLIGHT = 6
+PACK = 128
+CONTRACT_LAST = (((1,), (1,)), ((), ()))
+CONTRACT_FIRST = (((0,), (0,)), ((), ()))
+
+
+def stream_kernel(
+    gen_step_ref,
+    renoise_step_ref,
+    text_hbm,
+    noise_hbm,
+    renoise_hbm,
+    mod_hbm,
+    proj_hbm,
+    unembed_hbm,
+    mod_ref,
+    latents_ref,
+    through_ref,
+    text_ref,
+    noise_ref,
+    renoise_ref,
+    unembed_ref,
+    mod_buffer,
+    proj_buffer,
+    mod_sems,
+    proj_sems,
+    small_sems,
+):
+    width = mod_buffer.shape[2]
+    rows, cols = proj_buffer.shape[1:]
+    mod_depth = mod_buffer.shape[1] // MOD_PIECES
+    proj_depth = rows // PROJ_PIECES
+    mod_start = pl.multiple_of((lax.axis_index("mp") % 2) * width, 128)
+
+    def mod_piece(m, k):
+        part = pl.ds(k * mod_depth, mod_depth)
+        return pltpu.make_async_copy(
+            mod_hbm.at[m, part, pl.ds(mod_start, width)], mod_buffer.at[m, part], mod_sems.at[m, k]
+        )
+
+    def proj_piece(m, k):
+        part = pl.ds(k * proj_depth, proj_depth)
+        return pltpu.make_async_copy(
+            proj_hbm.at[m, part], proj_buffer.at[m, part], proj_sems.at[m, k]
+        )
+
+    small = [
+        pltpu.make_async_copy(source, target, small_sems.at[k])
+        for k, (source, target) in enumerate(
+            (
+                (text_hbm, text_ref),
+                (unembed_hbm, unembed_ref),
+                (noise_hbm, noise_ref),
+                (renoise_hbm, renoise_ref),
+            )
+        )
+    ]
+    order = []
+    for m in range(3):
+        order += [proj_piece(m, k) for k in range(PROJ_PIECES)]
+        order += [mod_piece(m, k) for k in range(MOD_PIECES)]
+    order = small[:2] + order[:IN_FLIGHT] + small[2:] + order[IN_FLIGHT:]
+    ahead = IN_FLIGHT + 4
+    for copy in order[:ahead]:
+        copy.start()
+
+    def take(position):
+        order[position].wait()
+        if position + ahead < len(order):
+            order[position + ahead].start()
+
+    take(0)
+    half_size = TEMB // 2
+    place = lane_index((8, half_size)).astype(jnp.float32)
+    frequency = jnp.exp(place * (-math.log(10000.0) / half_size))
+    level = lax.broadcasted_iota(jnp.int32, (8, half_size), 0)
+    steps = jnp.where(level == 0, gen_step_ref[0], renoise_step_ref[0]).astype(jnp.float32)
+    angles = steps * frequency
+    text = jnp.broadcast_to(text_ref[...].astype(jnp.float32), (8, text_ref.shape[1]))
+    text = jnp.where(lax.broadcasted_iota(jnp.int32, text.shape, 0) < 2, text, 0.0)
+    joined = jnp.concatenate([jnp.cos(angles), jnp.sin(angles), text], 1)
+    vectors = (joined / (1.0 + jnp.exp(-joined))).astype(jnp.bfloat16)
+    packs = width // PACK
+    mod_ref[...] = jnp.zeros_like(mod_ref)
+    take(1)
+    place = 2
+    for m in range(3):
+        total = jnp.zeros((8, width), jnp.float32)
+        for k in range(PROJ_PIECES + MOD_PIECES):
+            if place == IN_FLIGHT + 2:
+                take(place)
+                take(place + 1)
+                latents = jnp.where(lax.axis_index("mp") % 2 == 0, noise_ref[...], renoise_ref[...])
+                latents_ref[...] = latents.astype(jnp.bfloat16)
+                place += 2
+            take(place)
+            place += 1
+            if k < PROJ_PIECES:
+                part = slice(k * proj_depth, (k + 1) * proj_depth)
+                through_ref[m, :, part] = lax.dot_general(
+                    unembed_ref[m],
+                    proj_buffer[m, part],
+                    CONTRACT_LAST,
+                    preferred_element_type=jnp.float32,
+                ).astype(jnp.bfloat16)
+            else:
+                part = slice((k - PROJ_PIECES) * mod_depth, (k - PROJ_PIECES + 1) * mod_depth)
+                total += jnp.dot(
+                    vectors[:, part], mod_buffer[m, part], preferred_element_type=jnp.float32
+                )
+        if m == 0:
+            line = total[0:1]
+        elif m == 1:
+            line = GUIDANCE * total[1:2] + (1.0 - GUIDANCE) * total[2:3]
+        else:
+            line = total[1:2]
+        for j in range(packs):
+            mod_ref[m * packs + j : m * packs + j + 1] = line[:, j * PACK : (j + 1) * PACK]
+
+
+def streamed_weights(
+    gen_step, renoise_step, text, noise, renoise, mod_weight, proj_weight, unembed
+):
+    depth, width = mod_weight.shape[1], mod_weight.shape[2] // 2
+    rows, cols = proj_weight.shape[1:]
+    pack_rows = -(-3 * width // PACK // 8) * 8
+    return pl.pallas_call(
+        stream_kernel,
+        out_shape=[
+            jax.ShapeDtypeStruct((pack_rows, PACK), jnp.float32),
+            jax.ShapeDtypeStruct(noise.shape, jnp.bfloat16),
+            jax.ShapeDtypeStruct((3, CH, rows), jnp.bfloat16),
+        ],
+        in_specs=[pl.BlockSpec(memory_space=pltpu.SMEM)] * 2
+        + [pl.BlockSpec(memory_space=pltpu.HBM)] * 6,
+        out_specs=whole_specs(3),
+        scratch_shapes=[
+            pltpu.VMEM(text.shape, text.dtype),
+            pltpu.VMEM(noise.shape, noise.dtype),
+            pltpu.VMEM(renoise.shape, renoise.dtype),
+            pltpu.VMEM(unembed.shape, unembed.dtype),
+            pltpu.VMEM((3, depth, width), jnp.bfloat16),
+            pltpu.VMEM((3, rows, cols), jnp.bfloat16),
+            pltpu.SemaphoreType.DMA((3, MOD_PIECES)),
+            pltpu.SemaphoreType.DMA((3, PROJ_PIECES)),
+            pltpu.SemaphoreType.DMA((4,)),
+        ],
+        compiler_params=vmem_params(),
+        name="stream_weights",
+    )(
+        gen_step,
+        renoise_step,
+        *(
+            pltpu.with_memory_space_constraint(x, pltpu.HBM)
+            for x in (text, noise, renoise, mod_weight, proj_weight, unembed)
+        ),
+    )
+
+
+def embed_kernel(embed_ref, unembed_ref, gram_ref, rows_ref, direct_ref):
+    rows, cols = rows_ref.shape[2], unembed_ref.shape[2]
+    f = lax.axis_index("fsdp")
+    row_start = pl.multiple_of(f * rows, 128)
+    col_start = pl.multiple_of(lax.axis_index("mp") * cols, 128)
+    nothing = jnp.zeros((CH, cols), jnp.bfloat16)
+    for m in range(3):
+        whole = embed_ref[m].astype(jnp.float32)
+        average = jnp.sum(whole, axis=1, keepdims=True) * (1.0 / D)
+        rows_ref[m] = embed_ref[m, :, pl.ds(row_start, rows)].astype(jnp.float32) - average
+        direct = lax.dot_general(
+            embed_ref[m, :, pl.ds(col_start, cols)],
+            jnp.concatenate([unembed_ref[m], nothing], 0),
+            CONTRACT_LAST,
+            preferred_element_type=jnp.float32,
+        )
+        direct_ref[m] = jnp.where(f == 0, direct, 0.0)
+        pair = jnp.concatenate(split_two(whole - average), 0)
+        product = lax.dot_general(pair, pair, CONTRACT_LAST, preferred_element_type=jnp.float32)
+        product = product[:CH] + product[CH:]
+        gram = (product + pltpu.roll(product, CH, 1)) * (1.0 / D)
+        gram_ref[m] = jnp.concatenate(split_three(block_diagonal(gram, gram)), 1)
+
+
+def embed_products(embed, unembed, rows):
+    return pl.pallas_call(
+        embed_kernel,
+        out_shape=[
+            jax.ShapeDtypeStruct((3, 2 * CH, 6 * CH), jnp.bfloat16),
+            jax.ShapeDtypeStruct((3, CH, rows), jnp.float32),
+            jax.ShapeDtypeStruct((3, CH, 2 * CH), jnp.float32),
+        ],
+        in_specs=whole_specs(2),
+        out_specs=whole_specs(3),
+        compiler_params=vmem_params(),
+        cost_estimate=pl.CostEstimate(
+            flops=6 * 128 * 128 * D, bytes_accessed=6 * CH * D, transcendentals=0
+        ),
+        name="embed_products",
+    )(embed, unembed)
+
+
+def pair_ones():
+    shape = (2 * CH, 2 * CH)
+    lanes = lane_index(shape)
+    subs = lax.broadcasted_iota(jnp.int32, shape, 0)
+    ones = jnp.where((lanes < CH) == (subs < CH), 1.0, 0.0).astype(jnp.bfloat16)
+    return jnp.concatenate([ones, ones], 0)
+
+
+def inverse_deviation(u, by_gram, ones):
+    squares = jnp.concatenate(split_two(by_gram * u), 1)
+    spread = jnp.dot(squares, ones, preferred_element_type=jnp.float32)
+    return lax.rsqrt(jnp.maximum(spread, 0.0) + EPS_NORM)
+
+
+def columns(product, i):
+    return product[:, i * 2 * CH : (i + 1) * 2 * CH]
+
+
+def sample_latents(noise_ref, first_ref, second_ref):
+    first, second = first_ref[...], second_ref[...]
+    core = lax.axis_index("mp") % 2
+    other = jnp.where(core == 0, first, second)
+    other_renoise = jnp.where(core == 0, second, first)
+    return jnp.concatenate([noise_ref[...].astype(jnp.bfloat16), other], 0), other_renoise
+
+
+def noise_kernel(noise_ref, first_ref, second_ref, gram_ref, inverse_ref, normal_ref):
+    noise, _ = sample_latents(noise_ref, first_ref, second_ref)
+    product = jnp.dot(noise, gram_ref[0], preferred_element_type=jnp.float32)
+    noise = noise.astype(jnp.float32)
+    by_gram = columns(product, 0) + columns(product, 1) + columns(product, 2)
+    inverse = inverse_deviation(noise, by_gram, pair_ones())
+    inverse_ref[...] = inverse
+    normal_ref[...] = (noise * inverse).astype(jnp.bfloat16)
+
+
+def noise_statistics(noise, first, second, gram):
+    shape = (2 * noise.shape[0], noise.shape[1])
+    return pl.pallas_call(
+        noise_kernel,
+        out_shape=[
+            jax.ShapeDtypeStruct(shape, jnp.float32),
+            jax.ShapeDtypeStruct(shape, jnp.bfloat16),
+        ],
+        in_specs=whole_specs(4),
+        out_specs=whole_specs(2),
+        compiler_params=vmem_params(),
+        name="noise_statistics",
+    )(noise, first, second, gram)
+
+
+def maps_kernel(kept_ref, got_ref, rows_ref, through_ref, direct_ref, maps_ref, mod_ref):
+    rows = rows_ref.shape[2]
+    packs = rows // PACK
+    f = lax.axis_index("fsdp")
+    kept, got = kept_ref[...], got_ref[...]
+    shift = jnp.where(f == 0, kept, got)
+    scale = jnp.where(f == 0, got, kept)
+    for m in range(3):
+        pieces = []
+        for j in range(packs):
+            line = slice(m * packs + j, m * packs + j + 1)
+            pieces.append(
+                jnp.concatenate(
+                    [
+                        rows_ref[m, :, j * PACK : (j + 1) * PACK] * (1.0 + scale[line]),
+                        shift[line],
+                        jnp.zeros((7, PACK), jnp.float32),
+                    ],
+                    0,
+                )
+            )
+        left = jnp.concatenate(pieces, 1).astype(jnp.bfloat16)
+        through = jnp.concatenate([jnp.zeros((CH, rows), jnp.bfloat16), through_ref[m]], 0)
+        product = lax.dot_general(
+            left, through, CONTRACT_LAST, preferred_element_type=jnp.float32
+        )
+        base = m * (CH + 8)
+        maps_ref[base : base + CH] = product[:CH] + direct_ref[m]
+        maps_ref[base + CH : base + CH + 8] = product[CH:]
+    rest = jnp.zeros((mod_ref.shape[0] - 2 * packs, PACK), jnp.float32)
+    mod_ref[...] = jnp.concatenate([shift[:packs], scale[:packs], rest], 0).astype(jnp.bfloat16)
+
+
+def modulated_maps(kept, got, rows_part, through, direct):
+    packs = rows_part.shape[2] // PACK
+    return pl.pallas_call(
+        maps_kernel,
+        out_shape=[
+            jax.ShapeDtypeStruct((3 * (CH + 8), 2 * CH), jnp.float32),
+            jax.ShapeDtypeStruct((-(-2 * packs // 16) * 16, PACK), jnp.bfloat16),
+        ],
+        in_specs=whole_specs(5),
+        out_specs=whole_specs(2),
+        compiler_params=vmem_params(),
+        name="modulated_maps",
+    )(kept, got, rows_part, through, direct)
+
+
+MAP_ROWS = CH + 16
+
+
+def token_kernel(
+    level_ref,
+    noise_ref,
+    first_ref,
+    second_ref,
+    renoise_ref,
+    inverse_ref,
+    normal_ref,
+    gram_ref,
+    maps_a,
+    maps_b,
+    maps_c,
+    maps_d,
+    mod_ref,
+    score_ref,
+    payload_ref,
+):
+    half = renoise_ref.shape[0]
+    level = level_ref[0]
+    maps = [part[...].astype(jnp.float32) for part in (maps_a, maps_b, maps_c, maps_d)]
+    maps = (maps[0] + maps[1]) + (maps[2] + maps[3])
+    width = 2 * CH
+    ones = pair_ones()
+
+    def model_matrix(m):
+        base = m * (CH + 8)
+        pair = maps[base : base + CH]
+        turned = pltpu.roll(pair, CH, 1)
+        direct = split_two(block_diagonal(pair, turned))
+        modulated = split_two(block_diagonal(turned, pair))
+        offset = maps[base + CH : base + CH + 1]
+        return jnp.concatenate(direct + modulated, 1), offset + pltpu.roll(offset, CH, 1)
+
+    def combine(product, inverse, offset):
+        direct = columns(product, 0) + columns(product, 1)
+        return direct + inverse * (columns(product, 2) + columns(product, 3)) + offset
+
+    noise, other_renoise = sample_latents(noise_ref, first_ref, second_ref)
+    renoise = jnp.concatenate([renoise_ref[...], other_renoise.astype(jnp.float32)], 0)
+    matrix, offset = model_matrix(0)
+    product = jnp.dot(noise, matrix, preferred_element_type=jnp.float32)
+    clean = combine(product, inverse_ref[...], offset)
+    noisy = ((1.0 - level) * clean + level * renoise).astype(jnp.bfloat16)
+    noisy_wide = noisy.astype(jnp.float32)
+
+    def velocity(m):
+        matrix, offset = model_matrix(m)
+        matrix = jnp.concatenate([matrix, gram_ref[m]], 1)
+        product = jnp.dot(noisy, matrix, preferred_element_type=jnp.float32)
+        by_gram = columns(product, 4) + columns(product, 5) + columns(product, 6)
+        return combine(product, inverse_deviation(noisy_wide, by_gram, ones), offset)
+
+    real_v = velocity(1)
+    fake_v = velocity(2)
+    total = jnp.sum(jnp.abs(clean - renoise + real_v))
+    gap_scale = level * total * (1.0 / (2 * half * width)) + EPS_GAP
+    score = level * (real_v - fake_v) / gap_scale
+    score_ref[...] = score[:half]
+    tokens = 4 * half * lax.axis_size("dp")
+    cotangent = (score * (1.0 / math.sqrt(tokens))).astype(jnp.bfloat16)
+    pairs = lax.dot_general(
+        normal_ref[...], cotangent, CONTRACT_FIRST, preferred_element_type=jnp.float32
+    )
+    outer = pairs[:CH] + pltpu.roll(pairs[CH:], CH, 1)
+    sums = jnp.sum(cotangent.astype(jnp.float32), axis=0, keepdims=True)
+    sums = sums + pltpu.roll(sums, CH, 1)
+    rest = jnp.zeros((MAP_ROWS - CH - 1, width), jnp.float32)
+    payload_ref[:MAP_ROWS] = jnp.concatenate([outer, sums, rest], 0).astype(jnp.bfloat16)
+    payload_ref[MAP_ROWS:] = mod_ref[...]
+
+
+def token_phase(level, noise, first, second, renoise, inverse, normal, gram, maps, mod):
+    return pl.pallas_call(
+        token_kernel,
+        out_shape=[
+            jax.ShapeDtypeStruct(renoise.shape, jnp.float32),
+            jax.ShapeDtypeStruct((MAP_ROWS + mod.shape[0], 2 * CH), jnp.bfloat16),
+        ],
+        in_specs=[pl.BlockSpec(memory_space=pltpu.SMEM)] + whole_specs(12),
+        out_specs=whole_specs(2),
+        compiler_params=vmem_params(),
+        name="tokens",
+    )(level, noise, first, second, renoise, inverse, normal, gram, *maps, mod)
+
+
+GRAD_PIECES = 6
+
+
+def grad_kernel(block_a, block_b, block_c, block_d, rows_ref, unembed_ref, grad_hbm, buffer, sems):
+    rows = rows_ref.shape[2]
+    packs = rows // PACK
+    depth = rows // GRAD_PIECES
+    blocks = [block[...] for block in (block_a, block_b, block_c, block_d)]
+    left = jnp.concatenate([block[:MAP_ROWS, :CH] for block in blocks], 0)
+    mods = [block[MAP_ROWS:].astype(jnp.float32) for block in blocks]
+    unembed = unembed_ref[0]
+
+    def piece(k):
+        part = pl.ds(k * depth, depth)
+        return pltpu.make_async_copy(buffer.at[part], grad_hbm.at[part], sems.at[k])
+
+    for k in range(GRAD_PIECES):
+        tiles = []
+        for j in range(k * depth // PACK, (k + 1) * depth // PACK):
+            embed_tile = rows_ref[0, :, j * PACK : (j + 1) * PACK]
+            column = []
+            for mod in mods:
+                column += [
+                    embed_tile * (1.0 + mod[packs + j : packs + j + 1]),
+                    mod[j : j + 1],
+                    jnp.zeros((MAP_ROWS - CH - 1, PACK), jnp.float32),
+                ]
+            tiles.append(jnp.concatenate(column, 0).astype(jnp.bfloat16))
+        right = jnp.concatenate(tiles, 1)
+        grad_map = lax.dot_general(
+            left, right, CONTRACT_FIRST, preferred_element_type=jnp.float32
+        ).astype(jnp.bfloat16)
+        buffer[k * depth : (k + 1) * depth] = lax.dot_general(
+            grad_map, unembed, CONTRACT_FIRST, preferred_element_type=jnp.float32
+        )
+        piece(k).start()
+    for k in range(GRAD_PIECES):
+        piece(k).wait()
+
+
+def gradient(blocks, rows_part, unembed):
+    rows = rows_part.shape[2]
+    cols = unembed.shape[2]
+    return pl.pallas_call(
+        grad_kernel,
+        out_shape=jax.ShapeDtypeStruct((rows, cols), jnp.float32),
+        in_specs=whole_specs(6),
+        out_specs=pl.BlockSpec(memory_space=pl.ANY),
+        scratch_shapes=[
+            pltpu.VMEM((rows, cols), jnp.float32),
+            pltpu.SemaphoreType.DMA((GRAD_PIECES,)),
+        ],
+        compiler_params=vmem_params(),
+        name="gradient",
+    )(*blocks, rows_part, unembed)
+
+
+def body(
+    gen_noise, renoise, gen_step, renoise_step, text_pooled, embed, mod_weight, proj_weight, unembed
+):
+    mine, latents, through = streamed_weights(
+        gen_step,
+        renoise_step,
+        text_pooled,
+        gen_noise[0],
+        renoise[0],
+        mod_weight,
+        proj_weight,
+        unembed,
+    )
+    f = lax.axis_index("fsdp")
+    theirs = swap(mine, "mp", 1)
+    own_half = lax.axis_index("mp") % 2 == f
+    kept = jnp.where(own_half, mine, theirs)
+    got = swap(jnp.where(own_half, theirs, mine), "fsdp", 1)
+    first = swap(latents, "fsdp", 1)
+    got, first = lax.optimization_barrier((got, first))
+    second = swap(first, "mp", 1)
+    gram, rows_part, direct = embed_products(embed, unembed, proj_weight.shape[1])
+    maps, mod = modulated_maps(kept, got, rows_part, through, direct)
+    maps = (maps + swap(maps, "mp", 1)).astype(jnp.bfloat16)
+    inverse, normal = noise_statistics(gen_noise[0], first, second, gram)
+    plane = ("mp", "fsdp")
+    maps = [maps] + [swap(maps, plane, mask) for mask in (4, 1, 5)]
+    level = renoise_step.astype(jnp.float32) / 1000.0
+    score_gap, payload = token_phase(
+        level, gen_noise[0], first, second, renoise[0], inverse, normal, gram, maps, mod
+    )
+    blocks = gather_samples(payload)
+    return (gradient(blocks, rows_part, unembed), score_gap[None])
+
+
+def fits_kernels(mesh):
+    return mesh.shape["mp"] == 4 and mesh.shape["fsdp"] == 2 and mesh.shape["dp"] == 4
+
+
 def solution(mesh):
     return jax.shard_map(
-        body,
+        body if fits_kernels(mesh) else plain_body,
         mesh=mesh,
         in_specs=(
             P("dp", "fsdp", None),

time: 94.5 us -> 37.6 us (0.40)
  matrix products: 52.4 us -> 0 us
  Pallas kernels: 0 us -> 14.4 us
  blocking collectives: 11.9 us -> 0 us
  other arithmetic: 6.31 us -> 0.02 us
  local copies, waits for them, and re-layouts: 2.89 us -> 0.02 us
  starting transfers between devices: 10.3 us -> 12.4 us
  waiting for transfers between devices: 6.67 us -> 8.58 us
  between operations: 3.02 us -> 2 us
    dot_general x36 -> x0, matrix products: 52.4 us -> none  [the longest x26 22.6 us: dot(): jnp.dot(a, b, precision=precision, preferred_element_type=jnp.float32)]
    pallas_call x0 -> x6, Pallas kernels: none -> 14.4 us  [the longest x1 7.25 us: streamed_weights(): pl.pallas_call(stream_kernel, out_shape=[jax.ShapeDtypeStruct((pack_rows,...]
    all_gather x2 -> x0, blocking collectives: 11.9 us -> none  [the longest x1 6.95 us: body(): renoise_all = lax.all_gather(renoise[0], 'fsdp', axis=0, tiled=True)]
    ppermute x7 -> x10, waiting for transfers between devices: 3.75 us -> 8.58 us  [swap(): return lax.ppermute(x, axes, [(i, i ^ mask) for i in range(count)])]
    ppermute x1, waiting for transfers between devices: 2.92 us -> 0.01 us  [gather_samples(): near = lax.ppermute(x, ('mp', 'dp'), pairs)]
    unnamed x4 -> x0, other arithmetic: 2.7 us -> none
    ppermute x1, starting transfers between devices: 0.01 us -> 1.58 us  [gather_samples(): near = lax.ppermute(x, ('mp', 'dp'), pairs)]
    convert_element_type x4 -> x1, other arithmetic: 1.44 us -> 0.02 us  [body(): maps = (maps + swap(maps, 'mp', 1)).astype(jnp.bfloat16)]
  transfers between devices with their start and end apart: 8 -> 11, of which waited for: 4 -> 6; matrix products, arithmetic and copies ran while one was open for 28% -> 0% of each run, Pallas kernels for 0% -> 5%
where the time goes in v3:
time: 37.6 us; the launch traced here: 37.5 us
  Pallas kernels  14.4 us (38%)
  starting transfers between devices  12.4 us (33%)
  waiting for transfers between devices  8.58 us (23%)
  between operations  2 us (5%)
    ppermute x10, starting transfers between devices, swap(): return lax.ppermute(x, axes, [(i, i ^ mask) for i in range(count)])  10.8 us
    ppermute x10, waiting for transfers between devices, swap(): return lax.ppermute(x, axes, [(i, i ^ mask) for i in range(count)])  8.58 us
    pallas_call x1, Pallas kernels, streamed_weights(): pl.pallas_call(stream_kernel, out_shape=[jax.ShapeDtypeStruct((pack_rows,...  7.25 us
    pallas_call x1, Pallas kernels, gradient(): pl.pallas_call(grad_kernel, out_shape=jax.ShapeDtypeStruct((rows, cols),...  2.88 us
    pallas_call x1, Pallas kernels, token_phase(): pl.pallas_call(token_kernel, out_shape=[jax.ShapeDtypeStruct(renoise.shap...  2.02 us
    ppermute x1, starting transfers between devices, gather_samples(): near = lax.ppermute(x, ('mp', 'dp'), pairs)  1.58 us
    pallas_call x1, Pallas kernels, embed_products(): pl.pallas_call(embed_kernel, out_shape=[jax.ShapeDtypeStruct((3, 2 * CH,...  1.21 us
  transfers between devices with their start and end apart: 11, of which 6 were waited for; matrix products, arithmetic and copies ran while one was open for 0% of the time, Pallas kernels for 5%

profile of v3, /device:TPU:0, one launch (start us, length us, event | category | flops | bytes accessed | tf_op | source)
XLA Modules:
  0.0 37.5 jit_solution(11438472074399378703)
XLA Ops:
  2.0 7.3 %stream_weights.1 = (f32[40,128]{1,0:T(8,128)S(1)}, bf16[256,128]{1,0:T(8,128)(2,1)S(1)}, bf16[3,64,1536]{2,1,0:T(8,128)(2,1)S(1)}) custom-call(s32[1]{0:T(128)S(6)} %copy.11.gen_step_ref, s32[1]{0:T(128)S(6)} %copy.12.renoise_step_ref, bf16[1,768]{1,0:T(2,128)(2,1)} %text_hbm.1, f32[256,128]{1,0:T(8,128)} %bitcast.3, f32[256,128]{1,0:T(8,128)} %bitcast.6, ...), custom_call_target="tpu_custom_call" | custom-call | tf_op jit(solution)/shard_map/stream_weights/pallas_call | solution.py:352
  9.2 0.5 %collective-permute-start = (f32[40,128]{1,0:T(8,128)S(1)}, f32[40,128]{1,0:T(8,128)S(1)}, u32[]{:S(2)}, u32[]{:S(2)}) collective-permute-start(f32[40,128]{1,0:T(8,128)S(1)} %get-tuple-element.16), channel_id=1, source_target_pairs={{0,8},{8,0},{16,24},{24,16},{1,9},{9,1},{17,25},{25,17},{2,10},{10... | collective-permute-start | bytes 61448 | tf_op jit(solution)/shard_map/ppermute | solution.py:34
  9.7 2.6 %collective-permute-start.2 = (bf16[256,128]{1,0:T(8,128)(2,1)S(1)}, bf16[256,128]{1,0:T(8,128)(2,1)S(1)}, u32[]{:S(2)}, u32[]{:S(2)}) collective-permute-start(bf16[256,128]{1,0:T(8,128)(2,1)S(1)} %get-tuple-element.17), channel_id=1, source_target_pairs={{0,4},{4,0},{1,5},{5,1},{2,6},{6,2},{3,7},{7,3},{8,12},{12,8},{9,1... | collective-permute-start | bytes 196616 | tf_op jit(solution)/shard_map/ppermute | solution.py:34
  12.3 0.0 collective-permute-done
  12.3 1.1 %collective-permute-start.1 = (f32[40,128]{1,0:T(8,128)S(1)}, f32[40,128]{1,0:T(8,128)S(1)}, u32[]{:S(2)}, u32[]{:S(2)}) collective-permute-start(f32[40,128]{1,0:T(8,128)S(1)} %get-tuple-element.31), channel_id=1, source_target_pairs={{0,4},{4,0},{1,5},{5,1},{2,6},{6,2},{3,7},{7,3},{8,12},{12,8},{9,1... | collective-permute-start | bytes 61448 | tf_op jit(solution)/shard_map/ppermute | solution.py:34
  13.5 1.2 %embed_products.1 = (bf16[3,128,384]{2,1,0:T(8,128)(2,1)S(1)}, f32[3,64,1536]{2,1,0:T(8,128)S(1)}, f32[3,64,128]{2,1,0:T(8,128)S(1)}) custom-call(bf16[3,64,3072]{2,1,0:T(8,128)(2,1)S(1)} %copy-done.2, bf16[3,64,768]{2,1,0:T(8,128)(2,1)S(1)} %copy-done), custom_call_target="tpu_custom_call" | custom-call | flops 301989888 | bytes 1179648 | tf_op jit(solution)/shard_map/embed_products/pallas_call | solution.py:410
  14.7 1.5 %collective-permute-done.1.got_ref = f32[40,128]{1,0:T(8,128)S(1)} collective-permute-done((f32[40,128]{1,0:T(8,128)S(1)}, f32[40,128]{1,0:T(8,128)S(1)}, u32[]{:S(2)}, u32[]{:S(2)}) %collective-permute-start.1) | collective-permute-done | bytes 20512 | tf_op jit(solution)/shard_map/ppermute | solution.py:34
  16.2 0.0 collective-permute-done.2.first_ref
  16.2 0.5 %modulated_maps.1 = (f32[216,128]{1,0:T(8,128)S(1)}, bf16[32,128]{1,0:T(8,128)(2,1)S(1)}) custom-call(f32[40,128]{1,0:T(8,128)S(1)} %get-tuple-element.30.kept_ref, f32[40,128]{1,0:T(8,128)S(1)} %collective-permute-done.1.got_ref, f32[3,64,1536]{2,1,0:T(8,128)S(1)} %get-tuple-element.23.rows_ref, bf16[3,64,1536]{2,1,0:T(8,128)(2,1)S(1)} %get-tuple-element.24.through_ref, ...), custom_call_target="tpu_custom_call" | custom-call | tf_op jit(solution)/shard_map/modulated_maps/pallas_call | solution.py:513
  16.7 0.1 collective-permute-start.4
  16.8 0.5 %collective-permute-start.3 = (bf16[256,128]{1,0:T(8,128)(2,1)S(1)}, bf16[256,128]{1,0:T(8,128)(2,1)S(1)}, u32[]{:S(2)}, u32[]{:S(2)}) collective-permute-start(bf16[256,128]{1,0:T(8,128)(2,1)S(1)} %collective-permute-done.2.first_ref), channel_id=1, source_target_pairs={{0,8},{8,0},{16,24},{24,16},{1,9},{9,1},{17,25},{25,17},{2,10},{10... | collective-permute-start | bytes 196616 | tf_op jit(solution)/shard_map/ppermute | solution.py:34
  17.3 0.8 %collective-permute-done.4 = f32[216,128]{1,0:T(8,128)S(1)} collective-permute-done((f32[216,128]{1,0:T(8,128)S(1)}, f32[216,128]{1,0:T(8,128)S(1)}, u32[]{:S(2)}, u32[]{:S(2)}) %collective-permute-start.4) | collective-permute-done | bytes 110624 | tf_op jit(solution)/shard_map/ppermute | solution.py:34
  18.1 2.0 %collective-permute-start.7 = (bf16[216,128]{1,0:T(8,128)(2,1)S(1)}, bf16[216,128]{1,0:T(8,128)(2,1)S(1)}, u32[]{:S(2)}, u32[]{:S(2)}) collective-permute-start(bf16[216,128]{1,0:T(8,128)(2,1)S(1)} %add_convert_fusion.maps_a), channel_id=1, source_target_pairs={{0,20},{4,16},{8,28},{12,24},{16,4},{20,0},{24,12},{28,8},{1,21},{... | collective-permute-start | bytes 165896 | tf_op jit(solution)/shard_map/ppermute | solution.py:34
  20.2 1.0 %collective-permute-start.6 = (bf16[216,128]{1,0:T(8,128)(2,1)S(1)}, bf16[216,128]{1,0:T(8,128)(2,1)S(1)}, u32[]{:S(2)}, u32[]{:S(2)}) collective-permute-start(bf16[216,128]{1,0:T(8,128)(2,1)S(1)} %add_convert_fusion.maps_a), channel_id=1, source_target_pairs={{0,4},{4,0},{8,12},{12,8},{16,20},{20,16},{24,28},{28,24},{1,5},{5... | collective-permute-start | bytes 165896 | tf_op jit(solution)/shard_map/ppermute | solution.py:34
  21.1 0.5 %collective-permute-start.5 = (bf16[216,128]{1,0:T(8,128)(2,1)S(1)}, bf16[216,128]{1,0:T(8,128)(2,1)S(1)}, u32[]{:S(2)}, u32[]{:S(2)}) collective-permute-start(bf16[216,128]{1,0:T(8,128)(2,1)S(1)} %add_convert_fusion.maps_a), channel_id=1, source_target_pairs={{0,16},{4,20},{8,24},{12,28},{16,0},{20,4},{24,8},{28,12},{1,17},{... | collective-permute-start | bytes 165896 | tf_op jit(solution)/shard_map/ppermute | solution.py:34
  21.7 0.5 %noise_statistics.1 = (f32[512,128]{1,0:T(8,128)S(1)}, bf16[512,128]{1,0:T(8,128)(2,1)S(1)}) custom-call(f32[256,128]{1,0:T(8,128)S(1)} %bitcast.4, bf16[256,128]{1,0:T(8,128)(2,1)S(1)} %collective-permute-done.2.first_ref, bf16[256,128]{1,0:T(8,128)(2,1)S(1)} %collective-permute-done.3.second_ref, bf16[3,128,384]{2,1,0:T(8,128)(2,1)S(1)} %get-tuple-element.19.gram_ref), custom_call_target="tpu_custom_call" | custom-call | tf_op jit(solution)/shard_map/noise_statistics/pallas_call | solution.py:465
  22.2 1.1 %collective-permute-done.7.maps_d = bf16[216,128]{1,0:T(8,128)(2,1)S(1)} collective-permute-done((bf16[216,128]{1,0:T(8,128)(2,1)S(1)}, bf16[216,128]{1,0:T(8,128)(2,1)S(1)}, u32[]{:S(2)}, u32[]{:S(2)}) %collective-permute-start.7) | collective-permute-done | bytes 55328 | tf_op jit(solution)/shard_map/ppermute | solution.py:34
  23.4 1.0 %collective-permute-done.6.maps_c = bf16[216,128]{1,0:T(8,128)(2,1)S(1)} collective-permute-done((bf16[216,128]{1,0:T(8,128)(2,1)S(1)}, bf16[216,128]{1,0:T(8,128)(2,1)S(1)}, u32[]{:S(2)}, u32[]{:S(2)}) %collective-permute-start.6) | collective-permute-done | bytes 55328 | tf_op jit(solution)/shard_map/ppermute | solution.py:34
  24.4 0.9 %collective-permute-done.5.maps_b = bf16[216,128]{1,0:T(8,128)(2,1)S(1)} collective-permute-done((bf16[216,128]{1,0:T(8,128)(2,1)S(1)}, bf16[216,128]{1,0:T(8,128)(2,1)S(1)}, u32[]{:S(2)}, u32[]{:S(2)}) %collective-permute-start.5) | collective-permute-done | bytes 55328 | tf_op jit(solution)/shard_map/ppermute | solution.py:34
  25.3 2.0 %tokens.1 = (f32[256,128]{1,0:T(8,128)}, bf16[112,128]{1,0:T(8,128)(2,1)S(1)}) custom-call(f32[1]{0:T(128)S(6)} %div.3.level_ref, f32[256,128]{1,0:T(8,128)S(1)} %bitcast.5, bf16[256,128]{1,0:T(8,128)(2,1)S(1)} %collective-permute-done.2.first_ref, bf16[256,128]{1,0:T(8,128)(2,1)S(1)} %collective-permute-done.3.second_ref, f32[256,128]{1,0:T(8,128)S(1)} %bitcast.7, ...), custom_call_target="tpu_custom_call" | custom-call | tf_op jit(solution)/shard_map/tokens/pallas_call | solution.py:601
  27.3 1.6 %collective-permute-start.8 = (bf16[112,128]{1,0:T(8,128)(2,1)S(1)}, bf16[112,128]{1,0:T(8,128)(2,1)S(1)}, u32[]{:S(2)}, u32[]{:S(2)}) collective-permute-start(bf16[112,128]{1,0:T(8,128)(2,1)S(1)} %get-tuple-element.28.block_a), channel_id=1, source_target_pairs={{0,1},{1,0},{2,3},{3,2},{8,10},{9,11},{10,8},{11,9},{16,17},{17,16... | collective-permute-start | bytes 86024 | tf_op jit(solution)/shard_map/ppermute | solution.py:55
  28.9 2.5 %collective-permute-start.10 = (bf16[112,128]{1,0:T(8,128)(2,1)S(1)}, bf16[112,128]{1,0:T(8,128)(2,1)S(1)}, u32[]{:S(2)}, u32[]{:S(2)}) collective-permute-start(bf16[112,128]{1,0:T(8,128)(2,1)S(1)} %get-tuple-element.28.block_a), channel_id=1, source_target_pairs={{0,3},{1,2},{2,1},{3,0},{4,7},{5,6},{6,5},{7,4},{8,11},{9,10},{10,... | collective-permute-start | bytes 86024 | tf_op jit(solution)/shard_map/ppermute | solution.py:34
  31.4 3.2 %collective-permute-done.10.block_d = bf16[112,128]{1,0:T(8,128)(2,1)S(1)} collective-permute-done((bf16[112,128]{1,0:T(8,128)(2,1)S(1)}, bf16[112,128]{1,0:T(8,128)(2,1)S(1)}, u32[]{:S(2)}, u32[]{:S(2)}) %collective-permute-start.10) | collective-permute-done | bytes 28704 | tf_op jit(solution)/shard_map/ppermute | solution.py:34
  34.6 2.9 %gradient.1 = f32[1536,768]{1,0:T(8,128)} custom-call(bf16[112,128]{1,0:T(8,128)(2,1)S(1)} %get-tuple-element.28.block_a, bf16[112,128]{1,0:T(8,128)(2,1)S(1)} %collective-permute-done.8.block_b, bf16[112,128]{1,0:T(8,128)(2,1)S(1)} %collective-permute-done.9.block_c, bf16[112,128]{1,0:T(8,128)(2,1)S(1)} %collective-permute-done.10.block_d, ...), custom_call_target="tpu_custom_call" | custom-call | tf_op jit(solution)/shard_map/gradient/pallas_call | solution.py:657
  (14 shorter events, 0.1 us)
Async XLA Ops:
  1.9 11.5 %copy-start = (bf16[3,64,768]{2,1,0:T(8,128)(2,1)S(1)}, bf16[3,64,768]{2,1,0:T(8,128)(2,1)}, u32[]{:S(2)}) copy-start(bf16[3,64,768]{2,1,0:T(8,128)(2,1)} %unembed_ref.3) | copy-start | bytes 884740
  1.9 11.5 %copy-start.2 = (bf16[3,64,3072]{2,1,0:T(8,128)(2,1)S(1)}, bf16[3,64,3072]{2,1,0:T(8,128)(2,1)}, u32[]{:S(2)}) copy-start(bf16[3,64,3072]{2,1,0:T(8,128)(2,1)} %embed_ref.1) | copy-start | bytes 3538948
  1.9 19.7 %copy-start.1 = (f32[1,256,128]{2,1,0:T(8,128)S(1)}, f32[1,256,128]{2,1,0:T(8,128)}, u32[]{:S(2)}) copy-start(f32[1,256,128]{2,1,0:T(8,128)} %param.9) | copy-start | bytes 393220
  2.0 23.4 %copy-start.3 = (f32[1,256,128]{2,1,0:T(8,128)S(1)}, f32[1,256,128]{2,1,0:T(8,128)}, u32[]{:S(2)}) copy-start(f32[1,256,128]{2,1,0:T(8,128)} %param.10) | copy-start | bytes 393220
  9.2 3.1 %collective-permute-start = (f32[40,128]{1,0:T(8,128)S(1)}, f32[40,128]{1,0:T(8,128)S(1)}, u32[]{:S(2)}, u32[]{:S(2)}) collective-permute-start(f32[40,128]{1,0:T(8,128)S(1)} %get-tuple-element.16), channel_id=1, source_target_pairs={{0,8},{8,0},{16,24},{24,16},{1,9},{9,1},{17,25},{25,17},{2,10},{10... | collective-permute-start | bytes 61448 | tf_op jit(solution)/shard_map/ppermute | solution.py:34
  9.7 6.5 %collective-permute-start.2 = (bf16[256,128]{1,0:T(8,128)(2,1)S(1)}, bf16[256,128]{1,0:T(8,128)(2,1)S(1)}, u32[]{:S(2)}, u32[]{:S(2)}) collective-permute-start(bf16[256,128]{1,0:T(8,128)(2,1)S(1)} %get-tuple-element.17), channel_id=1, source_target_pairs={{0,4},{4,0},{1,5},{5,1},{2,6},{6,2},{3,7},{7,3},{8,12},{12,8},{9,1... | collective-permute-start | bytes 196616 | tf_op jit(solution)/shard_map/ppermute | solution.py:34
  12.3 3.8 %collective-permute-start.1 = (f32[40,128]{1,0:T(8,128)S(1)}, f32[40,128]{1,0:T(8,128)S(1)}, u32[]{:S(2)}, u32[]{:S(2)}) collective-permute-start(f32[40,128]{1,0:T(8,128)S(1)} %get-tuple-element.31), channel_id=1, source_target_pairs={{0,4},{4,0},{1,5},{5,1},{2,6},{6,2},{3,7},{7,3},{8,12},{12,8},{9,1... | collective-permute-start | bytes 61448 | tf_op jit(solution)/shard_map/ppermute | solution.py:34
  16.7 1.4 %collective-permute-start.4 = (f32[216,128]{1,0:T(8,128)S(1)}, f32[216,128]{1,0:T(8,128)S(1)}, u32[]{:S(2)}, u32[]{:S(2)}) collective-permute-start(f32[216,128]{1,0:T(8,128)S(1)} %get-tuple-element.26), channel_id=1, source_target_pairs={{0,8},{8,0},{16,24},{24,16},{1,9},{9,1},{17,25},{25,17},{2,10},{10... | collective-permute-start | bytes 331784 | tf_op jit(solution)/shard_map/ppermute | solution.py:34
  16.8 4.9 %collective-permute-start.3 = (bf16[256,128]{1,0:T(8,128)(2,1)S(1)}, bf16[256,128]{1,0:T(8,128)(2,1)S(1)}, u32[]{:S(2)}, u32[]{:S(2)}) collective-permute-start(bf16[256,128]{1,0:T(8,128)(2,1)S(1)} %collective-permute-done.2.first_ref), channel_id=1, source_target_pairs={{0,8},{8,0},{16,24},{24,16},{1,9},{9,1},{17,25},{25,17},{2,10},{10... | collective-permute-start | bytes 196616 | tf_op jit(solution)/shard_map/ppermute | solution.py:34
  18.1 5.2 %collective-permute-start.7 = (bf16[216,128]{1,0:T(8,128)(2,1)S(1)}, bf16[216,128]{1,0:T(8,128)(2,1)S(1)}, u32[]{:S(2)}, u32[]{:S(2)}) collective-permute-start(bf16[216,128]{1,0:T(8,128)(2,1)S(1)} %add_convert_fusion.maps_a), channel_id=1, source_target_pairs={{0,20},{4,16},{8,28},{12,24},{16,4},{20,0},{24,12},{28,8},{1,21},{... | collective-permute-start | bytes 165896 | tf_op jit(solution)/shard_map/ppermute | solution.py:34
  20.2 4.2 %collective-permute-start.6 = (bf16[216,128]{1,0:T(8,128)(2,1)S(1)}, bf16[216,128]{1,0:T(8,128)(2,1)S(1)}, u32[]{:S(2)}, u32[]{:S(2)}) collective-permute-start(bf16[216,128]{1,0:T(8,128)(2,1)S(1)} %add_convert_fusion.maps_a), channel_id=1, source_target_pairs={{0,4},{4,0},{8,12},{12,8},{16,20},{20,16},{24,28},{28,24},{1,5},{5... | collective-permute-start | bytes 165896 | tf_op jit(solution)/shard_map/ppermute | solution.py:34
  21.1 4.2 %collective-permute-start.5 = (bf16[216,128]{1,0:T(8,128)(2,1)S(1)}, bf16[216,128]{1,0:T(8,128)(2,1)S(1)}, u32[]{:S(2)}, u32[]{:S(2)}) collective-permute-start(bf16[216,128]{1,0:T(8,128)(2,1)S(1)} %add_convert_fusion.maps_a), channel_id=1, source_target_pairs={{0,16},{4,20},{8,24},{12,28},{16,0},{20,4},{24,8},{28,12},{1,17},{... | collective-permute-start | bytes 165896 | tf_op jit(solution)/shard_map/ppermute | solution.py:34
  27.3 4.1 %collective-permute-start.8 = (bf16[112,128]{1,0:T(8,128)(2,1)S(1)}, bf16[112,128]{1,0:T(8,128)(2,1)S(1)}, u32[]{:S(2)}, u32[]{:S(2)}) collective-permute-start(bf16[112,128]{1,0:T(8,128)(2,1)S(1)} %get-tuple-element.28.block_a), channel_id=1, source_target_pairs={{0,1},{1,0},{2,3},{3,2},{8,10},{9,11},{10,8},{11,9},{16,17},{17,16... | collective-permute-start | bytes 86024 | tf_op jit(solution)/shard_map/ppermute | solution.py:55
  28.9 5.7 %collective-permute-start.10 = (bf16[112,128]{1,0:T(8,128)(2,1)S(1)}, bf16[112,128]{1,0:T(8,128)(2,1)S(1)}, u32[]{:S(2)}, u32[]{:S(2)}) collective-permute-start(bf16[112,128]{1,0:T(8,128)(2,1)S(1)} %get-tuple-element.28.block_a), channel_id=1, source_target_pairs={{0,3},{1,2},{2,1},{3,0},{4,7},{5,6},{6,5},{7,4},{8,11},{9,10},{10,... | collective-permute-start | bytes 86024 | tf_op jit(solution)/shard_map/ppermute | solution.py:34
  31.4 3.2 %collective-permute-start.9 = (bf16[112,128]{1,0:T(8,128)(2,1)S(1)}, bf16[112,128]{1,0:T(8,128)(2,1)S(1)}, u32[]{:S(2)}, u32[]{:S(2)}) collective-permute-start(bf16[112,128]{1,0:T(8,128)(2,1)S(1)} %collective-permute-done.8.block_b), channel_id=1, source_target_pairs={{0,8},{8,0},{16,24},{24,16},{1,9},{9,1},{17,25},{25,17},{2,10},{10... | collective-permute-start | bytes 86024 | tf_op jit(solution)/shard_map/ppermute | solution.py:34

commit v4 on v3

--- a/solution.py
+++ b/solution.py
@@ -41,6 +41,16 @@
     plane = ("mp", "fsdp")
     parts = [swap(x, plane, mask) for mask in (4, 1, 5)]
     return (x + parts[0]) + (parts[1] + parts[2])
+
+
+def chip_blocks(x):
+    pairs = []
+    for m in range(4):
+        for f in range(2):
+            pairs.append((m * 2 + f, (m * 2 + f) ^ (4 if m % 2 == 0 else 1)))
+    side = lax.ppermute(x, ("mp", "fsdp"), pairs)
+    across = swap(x, ("mp", "fsdp"), 5)
+    return [x, side, swap(side, "mp", 1), across]
 
 
 def gather_samples(x):
@@ -614,7 +624,21 @@
 GRAD_PIECES = 6
 
 
-def grad_kernel(block_a, block_b, block_c, block_d, rows_ref, unembed_ref, grad_hbm, buffer, sems):
+def grad_kernel(
+    block_a,
+    block_b,
+    block_c,
+    block_d,
+    rows_ref,
+    unembed_ref,
+    score_ref,
+    grad_hbm,
+    score_hbm,
+    buffer,
+    sems,
+):
+    score_copy = pltpu.make_async_copy(score_ref, score_hbm, sems.at[GRAD_PIECES])
+    score_copy.start()
     rows = rows_ref.shape[2]
     packs = rows // PACK
     depth = rows // GRAD_PIECES
@@ -627,45 +651,49 @@
         part = pl.ds(k * depth, depth)
         return pltpu.make_async_copy(buffer.at[part], grad_hbm.at[part], sems.at[k])
 
+    tiles = []
+    for j in range(packs):
+        embed_tile = rows_ref[0, :, j * PACK : (j + 1) * PACK]
+        column = []
+        for mod in mods:
+            column += [
+                embed_tile * (1.0 + mod[packs + j : packs + j + 1]),
+                mod[j : j + 1],
+                jnp.zeros((MAP_ROWS - CH - 1, PACK), jnp.float32),
+            ]
+        tiles.append(jnp.concatenate(column, 0).astype(jnp.bfloat16))
+    grad_map = lax.dot_general(
+        left, jnp.concatenate(tiles, 1), CONTRACT_FIRST, preferred_element_type=jnp.float32
+    ).astype(jnp.bfloat16)
     for k in range(GRAD_PIECES):
-        tiles = []
-        for j in range(k * depth // PACK, (k + 1) * depth // PACK):
-            embed_tile = rows_ref[0, :, j * PACK : (j + 1) * PACK]
-            column = []
-            for mod in mods:
-                column += [
-                    embed_tile * (1.0 + mod[packs + j : packs + j + 1]),
-                    mod[j : j + 1],
-                    jnp.zeros((MAP_ROWS - CH - 1, PACK), jnp.float32),
-                ]
-            tiles.append(jnp.concatenate(column, 0).astype(jnp.bfloat16))
-        right = jnp.concatenate(tiles, 1)
-        grad_map = lax.dot_general(
-            left, right, CONTRACT_FIRST, preferred_element_type=jnp.float32
-        ).astype(jnp.bfloat16)
-        buffer[k * depth : (k + 1) * depth] = lax.dot_general(
-            grad_map, unembed, CONTRACT_FIRST, preferred_element_type=jnp.float32
+        part = slice(k * depth, (k + 1) * depth)
+        buffer[part] = lax.dot_general(
+            grad_map[:, part], unembed, CONTRACT_FIRST, preferred_element_type=jnp.float32
         )
         piece(k).start()
     for k in range(GRAD_PIECES):
         piece(k).wait()
-
-
-def gradient(blocks, rows_part, unembed):
+    score_copy.wait()
+
+
+def gradient(blocks, rows_part, unembed, score):
     rows = rows_part.shape[2]
     cols = unembed.shape[2]
     return pl.pallas_call(
         grad_kernel,
-        out_shape=jax.ShapeDtypeStruct((rows, cols), jnp.float32),
-        in_specs=whole_specs(6),
-        out_specs=pl.BlockSpec(memory_space=pl.ANY),
+        out_shape=[
+            jax.ShapeDtypeStruct((rows, cols), jnp.float32),
+            jax.ShapeDtypeStruct(score.shape, jnp.float32),
+        ],
+        in_specs=whole_specs(7),
+        out_specs=[pl.BlockSpec(memory_space=pl.ANY)] * 2,
         scratch_shapes=[
             pltpu.VMEM((rows, cols), jnp.float32),
-            pltpu.SemaphoreType.DMA((GRAD_PIECES,)),
+            pltpu.SemaphoreType.DMA((GRAD_PIECES + 1,)),
         ],
         compiler_params=vmem_params(),
         name="gradient",
-    )(*blocks, rows_part, unembed)
+    )(*blocks, rows_part, unembed, score)
 
 
 def body(
@@ -693,14 +721,14 @@
     maps, mod = modulated_maps(kept, got, rows_part, through, direct)
     maps = (maps + swap(maps, "mp", 1)).astype(jnp.bfloat16)
     inverse, normal = noise_statistics(gen_noise[0], first, second, gram)
-    plane = ("mp", "fsdp")
-    maps = [maps] + [swap(maps, plane, mask) for mask in (4, 1, 5)]
+    maps = chip_blocks(maps)
     level = renoise_step.astype(jnp.float32) / 1000.0
-    score_gap, payload = token_phase(
+    score, payload = token_phase(
         level, gen_noise[0], first, second, renoise[0], inverse, normal, gram, maps, mod
     )
     blocks = gather_samples(payload)
-    return (gradient(blocks, rows_part, unembed), score_gap[None])
+    gen_grad, score_gap = gradient(blocks, rows_part, unembed, score)
+    return (gen_grad, score_gap[None])
 
 
 def fits_kernels(mesh):

time: 37.6 us -> 36.6 us (0.973)
  starting transfers between devices: 12.4 us -> 11.3 us
  waiting for transfers between devices: 8.58 us -> 9.31 us
  Pallas kernels: 14.4 us -> 13.8 us
    ppermute x10 -> x9, starting transfers between devices: 10.8 us -> 8.1 us  [swap(): return lax.ppermute(x, axes, [(i, i ^ mask) for i in range(count)])]
    ppermute x0 -> x1, starting transfers between devices: none -> 1.55 us  [chip_blocks(): side = lax.ppermute(x, ('mp', 'fsdp'), pairs)]
    ppermute x0 -> x1, waiting for transfers between devices: none -> 1.33 us  [chip_blocks(): side = lax.ppermute(x, ('mp', 'fsdp'), pairs)]
    ppermute x10 -> x9, waiting for transfers between devices: 8.58 us -> 7.97 us  [swap(): return lax.ppermute(x, axes, [(i, i ^ mask) for i in range(count)])]
    pallas_call x1, Pallas kernels: 2.02 us -> 1.42 us  [token_phase(): pl.pallas_call(token_kernel, out_shape=[jax.ShapeDtypeStruct(renoise.shap...]
  transfers between devices with their start and end apart: 11 -> 11, of which waited for: 6 -> 5; matrix products, arithmetic and copies ran while one was open for 0% -> 0% of each run, Pallas kernels for 5% -> 5%
where the time goes in v4:
time: 36.6 us; the launch traced here: 36.4 us
  Pallas kernels  13.8 us (38%)
  starting transfers between devices  11.3 us (31%)
  waiting for transfers between devices  9.31 us (25%)
  between operations  2.01 us (5%)
    ppermute x9, starting transfers between devices, swap(): return lax.ppermute(x, axes, [(i, i ^ mask) for i in range(count)])  8.1 us
    ppermute x9, waiting for transfers between devices, swap(): return lax.ppermute(x, axes, [(i, i ^ mask) for i in range(count)])  7.97 us
    pallas_call x1, Pallas kernels, streamed_weights(): pl.pallas_call(stream_kernel, out_shape=[jax.ShapeDtypeStruct((pack_rows,...  7.25 us
    pallas_call x1, Pallas kernels, gradient(): pl.pallas_call(grad_kernel, out_shape=[jax.ShapeDtypeStruct((rows, cols),...  2.79 us
    ppermute x1, starting transfers between devices, gather_samples(): near = lax.ppermute(x, ('mp', 'dp'), pairs)  1.65 us
    ppermute x1, starting transfers between devices, chip_blocks(): side = lax.ppermute(x, ('mp', 'fsdp'), pairs)  1.55 us
    pallas_call x1, Pallas kernels, token_phase(): pl.pallas_call(token_kernel, out_shape=[jax.ShapeDtypeStruct(renoise.shap...  1.42 us
    ppermute x1, waiting for transfers between devices, chip_blocks(): side = lax.ppermute(x, ('mp', 'fsdp'), pairs)  1.33 us
  transfers between devices with their start and end apart: 11, of which 5 were waited for; matrix products, arithmetic and copies ran while one was open for 0% of the time, Pallas kernels for 5%

profile of v4, /device:TPU:0, one launch (start us, length us, event | category | flops | bytes accessed | tf_op | source)
XLA Modules:
  0.0 36.4 jit_solution(8655950734034635222)
XLA Ops:
  2.0 7.3 %stream_weights.1 = (f32[40,128]{1,0:T(8,128)S(1)}, bf16[256,128]{1,0:T(8,128)(2,1)S(1)}, bf16[3,64,1536]{2,1,0:T(8,128)(2,1)S(1)}) custom-call(s32[1]{0:T(128)S(6)} %copy.11.gen_step_ref, s32[1]{0:T(128)S(6)} %copy.12.renoise_step_ref, bf16[1,768]{1,0:T(2,128)(2,1)} %text_hbm.1, f32[256,128]{1,0:T(8,128)} %bitcast.3, f32[256,128]{1,0:T(8,128)} %bitcast.6, ...), custom_call_target="tpu_custom_call" | custom-call | tf_op jit(solution)/shard_map/stream_weights/pallas_call | solution.py:362
  9.2 0.5 %collective-permute-start = (f32[40,128]{1,0:T(8,128)S(1)}, f32[40,128]{1,0:T(8,128)S(1)}, u32[]{:S(2)}, u32[]{:S(2)}) collective-permute-start(f32[40,128]{1,0:T(8,128)S(1)} %get-tuple-element.18), channel_id=1, source_target_pairs={{0,8},{8,0},{16,24},{24,16},{1,9},{9,1},{17,25},{25,17},{2,10},{10... | collective-permute-start | bytes 61448 | tf_op jit(solution)/shard_map/ppermute | solution.py:34
  9.7 2.6 %collective-permute-start.2 = (bf16[256,128]{1,0:T(8,128)(2,1)S(1)}, bf16[256,128]{1,0:T(8,128)(2,1)S(1)}, u32[]{:S(2)}, u32[]{:S(2)}) collective-permute-start(bf16[256,128]{1,0:T(8,128)(2,1)S(1)} %get-tuple-element.19), channel_id=1, source_target_pairs={{0,4},{4,0},{1,5},{5,1},{2,6},{6,2},{3,7},{7,3},{8,12},{12,8},{9,1... | collective-permute-start | bytes 196616 | tf_op jit(solution)/shard_map/ppermute | solution.py:34
  12.3 0.0 collective-permute-done
  12.3 1.1 %collective-permute-start.1 = (f32[40,128]{1,0:T(8,128)S(1)}, f32[40,128]{1,0:T(8,128)S(1)}, u32[]{:S(2)}, u32[]{:S(2)}) collective-permute-start(f32[40,128]{1,0:T(8,128)S(1)} %get-tuple-element.35), channel_id=1, source_target_pairs={{0,4},{4,0},{1,5},{5,1},{2,6},{6,2},{3,7},{7,3},{8,12},{12,8},{9,1... | collective-permute-start | bytes 61448 | tf_op jit(solution)/shard_map/ppermute | solution.py:34
  13.5 1.2 %embed_products.1 = (bf16[3,128,384]{2,1,0:T(8,128)(2,1)S(1)}, f32[3,64,1536]{2,1,0:T(8,128)S(1)}, f32[3,64,128]{2,1,0:T(8,128)S(1)}) custom-call(bf16[3,64,3072]{2,1,0:T(8,128)(2,1)S(1)} %copy-done.2, bf16[3,64,768]{2,1,0:T(8,128)(2,1)S(1)} %copy-done), custom_call_target="tpu_custom_call" | custom-call | flops 301989888 | bytes 1179648 | tf_op jit(solution)/shard_map/embed_products/pallas_call | solution.py:420
  14.7 1.5 %collective-permute-done.1.got_ref = f32[40,128]{1,0:T(8,128)S(1)} collective-permute-done((f32[40,128]{1,0:T(8,128)S(1)}, f32[40,128]{1,0:T(8,128)S(1)}, u32[]{:S(2)}, u32[]{:S(2)}) %collective-permute-start.1) | collective-permute-done | bytes 20512 | tf_op jit(solution)/shard_map/ppermute | solution.py:34
  16.2 0.0 collective-permute-done.2.first_ref
  16.2 0.5 %modulated_maps.1 = (f32[216,128]{1,0:T(8,128)S(1)}, bf16[32,128]{1,0:T(8,128)(2,1)S(1)}) custom-call(f32[40,128]{1,0:T(8,128)S(1)} %get-tuple-element.34.kept_ref, f32[40,128]{1,0:T(8,128)S(1)} %collective-permute-done.1.got_ref, f32[3,64,1536]{2,1,0:T(8,128)S(1)} %get-tuple-element.25.rows_ref, bf16[3,64,1536]{2,1,0:T(8,128)(2,1)S(1)} %get-tuple-element.26.through_ref, ...), custom_call_target="tpu_custom_call" | custom-call | tf_op jit(solution)/shard_map/modulated_maps/pallas_call | solution.py:523
  16.7 0.1 collective-permute-start.4
  16.8 1.3 %collective-permute-done.4 = f32[216,128]{1,0:T(8,128)S(1)} collective-permute-done((f32[216,128]{1,0:T(8,128)S(1)}, f32[216,128]{1,0:T(8,128)S(1)}, u32[]{:S(2)}, u32[]{:S(2)}) %collective-permute-start.4) | collective-permute-done | bytes 110624 | tf_op jit(solution)/shard_map/ppermute | solution.py:34
  18.1 1.6 %collective-permute-start.5 = (bf16[216,128]{1,0:T(8,128)(2,1)S(1)}, bf16[216,128]{1,0:T(8,128)(2,1)S(1)}, u32[]{:S(2)}, u32[]{:S(2)}) collective-permute-start(bf16[216,128]{1,0:T(8,128)(2,1)S(1)} %add_convert_fusion.maps_a), channel_id=1, source_target_pairs={{0,16},{4,20},{8,12},{12,8},{16,0},{20,4},{24,28},{28,24},{1,17},{... | collective-permute-start | bytes 165896 | tf_op jit(solution)/shard_map/ppermute | solution.py:51
  19.7 0.0 collective-permute-start.3
  19.7 1.3 %collective-permute-start.7 = (bf16[216,128]{1,0:T(8,128)(2,1)S(1)}, bf16[216,128]{1,0:T(8,128)(2,1)S(1)}, u32[]{:S(2)}, u32[]{:S(2)}) collective-permute-start(bf16[216,128]{1,0:T(8,128)(2,1)S(1)} %add_convert_fusion.maps_a), channel_id=1, source_target_pairs={{0,20},{4,16},{8,28},{12,24},{16,4},{20,0},{24,12},{28,8},{1,21},{... | collective-permute-start | bytes 165896 | tf_op jit(solution)/shard_map/ppermute | solution.py:34
  21.0 1.3 %collective-permute-done.5.maps_b = bf16[216,128]{1,0:T(8,128)(2,1)S(1)} collective-permute-done((bf16[216,128]{1,0:T(8,128)(2,1)S(1)}, bf16[216,128]{1,0:T(8,128)(2,1)S(1)}, u32[]{:S(2)}, u32[]{:S(2)}) %collective-permute-start.5) | collective-permute-done | bytes 55328 | tf_op jit(solution)/shard_map/ppermute | solution.py:51
  22.4 0.6 %noise_statistics.1 = (f32[512,128]{1,0:T(8,128)S(1)}, bf16[512,128]{1,0:T(8,128)(2,1)S(1)}) custom-call(f32[256,128]{1,0:T(8,128)S(1)} %bitcast.4, bf16[256,128]{1,0:T(8,128)(2,1)S(1)} %collective-permute-done.2.first_ref, bf16[256,128]{1,0:T(8,128)(2,1)S(1)} %collective-permute-done.3.second_ref, bf16[3,128,384]{2,1,0:T(8,128)(2,1)S(1)} %get-tuple-element.21.gram_ref), custom_call_target="tpu_custom_call" | custom-call | tf_op jit(solution)/shard_map/noise_statistics/pallas_call | solution.py:475
  22.9 1.9 %collective-permute-done.7.maps_d = bf16[216,128]{1,0:T(8,128)(2,1)S(1)} collective-permute-done((bf16[216,128]{1,0:T(8,128)(2,1)S(1)}, bf16[216,128]{1,0:T(8,128)(2,1)S(1)}, u32[]{:S(2)}, u32[]{:S(2)}) %collective-permute-start.7) | collective-permute-done | bytes 55328 | tf_op jit(solution)/shard_map/ppermute | solution.py:34
  24.9 0.0 collective-permute-done.6.maps_c
  24.9 1.4 %tokens.1 = (f32[256,128]{1,0:T(8,128)S(1)}, bf16[112,128]{1,0:T(8,128)(2,1)S(1)}) custom-call(f32[1]{0:T(128)S(6)} %div.3.level_ref, f32[256,128]{1,0:T(8,128)S(1)} %bitcast.5, bf16[256,128]{1,0:T(8,128)(2,1)S(1)} %collective-permute-done.2.first_ref, bf16[256,128]{1,0:T(8,128)(2,1)S(1)} %collective-permute-done.3.second_ref, f32[256,128]{1,0:T(8,128)S(1)} %bitcast.7, ...), custom_call_target="tpu_custom_call" | custom-call | tf_op jit(solution)/shard_map/tokens/pallas_call | solution.py:611
  26.3 1.6 %collective-permute-start.8 = (bf16[112,128]{1,0:T(8,128)(2,1)S(1)}, bf16[112,128]{1,0:T(8,128)(2,1)S(1)}, u32[]{:S(2)}, u32[]{:S(2)}) collective-permute-start(bf16[112,128]{1,0:T(8,128)(2,1)S(1)} %get-tuple-element.30.block_a), channel_id=1, source_target_pairs={{0,1},{1,0},{2,3},{3,2},{8,10},{9,11},{10,8},{11,9},{16,17},{17,16... | collective-permute-start | bytes 86024 | tf_op jit(solution)/shard_map/ppermute | solution.py:65
  28.0 2.5 %collective-permute-start.10 = (bf16[112,128]{1,0:T(8,128)(2,1)S(1)}, bf16[112,128]{1,0:T(8,128)(2,1)S(1)}, u32[]{:S(2)}, u32[]{:S(2)}) collective-permute-start(bf16[112,128]{1,0:T(8,128)(2,1)S(1)} %get-tuple-element.30.block_a), channel_id=1, source_target_pairs={{0,3},{1,2},{2,1},{3,0},{4,7},{5,6},{6,5},{7,4},{8,11},{9,10},{10,... | collective-permute-start | bytes 86024 | tf_op jit(solution)/shard_map/ppermute | solution.py:34
  30.4 3.2 %collective-permute-done.10.block_d = bf16[112,128]{1,0:T(8,128)(2,1)S(1)} collective-permute-done((bf16[112,128]{1,0:T(8,128)(2,1)S(1)}, bf16[112,128]{1,0:T(8,128)(2,1)S(1)}, u32[]{:S(2)}, u32[]{:S(2)}) %collective-permute-start.10) | collective-permute-done | bytes 28704 | tf_op jit(solution)/shard_map/ppermute | solution.py:34
  33.6 0.0 collective-permute-done.9.block_c
  33.6 2.8 %gradient.1 = (f32[1536,768]{1,0:T(8,128)}, f32[256,128]{1,0:T(8,128)}) custom-call(bf16[112,128]{1,0:T(8,128)(2,1)S(1)} %get-tuple-element.30.block_a, bf16[112,128]{1,0:T(8,128)(2,1)S(1)} %collective-permute-done.8.block_b, bf16[112,128]{1,0:T(8,128)(2,1)S(1)} %collective-permute-done.9.block_c, bf16[112,128]{1,0:T(8,128)(2,1)S(1)} %collective-permute-done.10.block_d, ...), custom_call_target="tpu_custom_call" | custom-call | tf_op jit(solution)/shard_map/gradient/pallas_call | solution.py:682
  (14 shorter events, 0.1 us)
Async XLA Ops:
  1.9 11.5 %copy-start = (bf16[3,64,768]{2,1,0:T(8,128)(2,1)S(1)}, bf16[3,64,768]{2,1,0:T(8,128)(2,1)}, u32[]{:S(2)}) copy-start(bf16[3,64,768]{2,1,0:T(8,128)(2,1)} %unembed_ref.3) | copy-start | bytes 884740
  1.9 11.5 %copy-start.2 = (bf16[3,64,3072]{2,1,0:T(8,128)(2,1)S(1)}, bf16[3,64,3072]{2,1,0:T(8,128)(2,1)}, u32[]{:S(2)}) copy-start(bf16[3,64,3072]{2,1,0:T(8,128)(2,1)} %embed_ref.1) | copy-start | bytes 3538948
  1.9 20.4 %copy-start.1 = (f32[1,256,128]{2,1,0:T(8,128)S(1)}, f32[1,256,128]{2,1,0:T(8,128)}, u32[]{:S(2)}) copy-start(f32[1,256,128]{2,1,0:T(8,128)} %param.9) | copy-start | bytes 393220
  2.0 22.9 %copy-start.3 = (f32[1,256,128]{2,1,0:T(8,128)S(1)}, f32[1,256,128]{2,1,0:T(8,128)}, u32[]{:S(2)}) copy-start(f32[1,256,128]{2,1,0:T(8,128)} %param.10) | copy-start | bytes 393220
  9.2 3.1 %collective-permute-start = (f32[40,128]{1,0:T(8,128)S(1)}, f32[40,128]{1,0:T(8,128)S(1)}, u32[]{:S(2)}, u32[]{:S(2)}) collective-permute-start(f32[40,128]{1,0:T(8,128)S(1)} %get-tuple-element.18), channel_id=1, source_target_pairs={{0,8},{8,0},{16,24},{24,16},{1,9},{9,1},{17,25},{25,17},{2,10},{10... | collective-permute-start | bytes 61448 | tf_op jit(solution)/shard_map/ppermute | solution.py:34
  9.7 6.5 %collective-permute-start.2 = (bf16[256,128]{1,0:T(8,128)(2,1)S(1)}, bf16[256,128]{1,0:T(8,128)(2,1)S(1)}, u32[]{:S(2)}, u32[]{:S(2)}) collective-permute-start(bf16[256,128]{1,0:T(8,128)(2,1)S(1)} %get-tuple-element.19), channel_id=1, source_target_pairs={{0,4},{4,0},{1,5},{5,1},{2,6},{6,2},{3,7},{7,3},{8,12},{12,8},{9,1... | collective-permute-start | bytes 196616 | tf_op jit(solution)/shard_map/ppermute | solution.py:34
  12.3 3.8 %collective-permute-start.1 = (f32[40,128]{1,0:T(8,128)S(1)}, f32[40,128]{1,0:T(8,128)S(1)}, u32[]{:S(2)}, u32[]{:S(2)}) collective-permute-start(f32[40,128]{1,0:T(8,128)S(1)} %get-tuple-element.35), channel_id=1, source_target_pairs={{0,4},{4,0},{1,5},{5,1},{2,6},{6,2},{3,7},{7,3},{8,12},{12,8},{9,1... | collective-permute-start | bytes 61448 | tf_op jit(solution)/shard_map/ppermute | solution.py:34
  16.7 1.4 %collective-permute-start.4 = (f32[216,128]{1,0:T(8,128)S(1)}, f32[216,128]{1,0:T(8,128)S(1)}, u32[]{:S(2)}, u32[]{:S(2)}) collective-permute-start(f32[216,128]{1,0:T(8,128)S(1)} %get-tuple-element.28), channel_id=1, source_target_pairs={{0,8},{8,0},{16,24},{24,16},{1,9},{9,1},{17,25},{25,17},{2,10},{10... | collective-permute-start | bytes 331784 | tf_op jit(solution)/shard_map/ppermute | solution.py:34
  18.1 4.2 %collective-permute-start.5 = (bf16[216,128]{1,0:T(8,128)(2,1)S(1)}, bf16[216,128]{1,0:T(8,128)(2,1)S(1)}, u32[]{:S(2)}, u32[]{:S(2)}) collective-permute-start(bf16[216,128]{1,0:T(8,128)(2,1)S(1)} %add_convert_fusion.maps_a), channel_id=1, source_target_pairs={{0,16},{4,20},{8,12},{12,8},{16,0},{20,4},{24,28},{28,24},{1,17},{... | collective-permute-start | bytes 165896 | tf_op jit(solution)/shard_map/ppermute | solution.py:51
  19.7 2.7 %collective-permute-start.3 = (bf16[256,128]{1,0:T(8,128)(2,1)S(1)}, bf16[256,128]{1,0:T(8,128)(2,1)S(1)}, u32[]{:S(2)}, u32[]{:S(2)}) collective-permute-start(bf16[256,128]{1,0:T(8,128)(2,1)S(1)} %collective-permute-done.2.first_ref), channel_id=1, source_target_pairs={{0,8},{8,0},{16,24},{24,16},{1,9},{9,1},{17,25},{25,17},{2,10},{10... | collective-permute-start | bytes 196616 | tf_op jit(solution)/shard_map/ppermute | solution.py:34
  19.7 5.2 %collective-permute-start.7 = (bf16[216,128]{1,0:T(8,128)(2,1)S(1)}, bf16[216,128]{1,0:T(8,128)(2,1)S(1)}, u32[]{:S(2)}, u32[]{:S(2)}) collective-permute-start(bf16[216,128]{1,0:T(8,128)(2,1)S(1)} %add_convert_fusion.maps_a), channel_id=1, source_target_pairs={{0,20},{4,16},{8,28},{12,24},{16,4},{20,0},{24,12},{28,8},{1,21},{... | collective-permute-start | bytes 165896 | tf_op jit(solution)/shard_map/ppermute | solution.py:34
  22.4 2.5 %collective-permute-start.6 = (bf16[216,128]{1,0:T(8,128)(2,1)S(1)}, bf16[216,128]{1,0:T(8,128)(2,1)S(1)}, u32[]{:S(2)}, u32[]{:S(2)}) collective-permute-start(bf16[216,128]{1,0:T(8,128)(2,1)S(1)} %collective-permute-done.5.maps_b), channel_id=1, source_target_pairs={{0,8},{8,0},{16,24},{24,16},{1,9},{9,1},{17,25},{25,17},{2,10},{10... | collective-permute-start | bytes 165896 | tf_op jit(solution)/shard_map/ppermute | solution.py:34
  26.3 4.1 %collective-permute-start.8 = (bf16[112,128]{1,0:T(8,128)(2,1)S(1)}, bf16[112,128]{1,0:T(8,128)(2,1)S(1)}, u32[]{:S(2)}, u32[]{:S(2)}) collective-permute-start(bf16[112,128]{1,0:T(8,128)(2,1)S(1)} %get-tuple-element.30.block_a), channel_id=1, source_target_pairs={{0,1},{1,0},{2,3},{3,2},{8,10},{9,11},{10,8},{11,9},{16,17},{17,16... | collective-permute-start | bytes 86024 | tf_op jit(solution)/shard_map/ppermute | solution.py:65
  28.0 5.7 %collective-permute-start.10 = (bf16[112,128]{1,0:T(8,128)(2,1)S(1)}, bf16[112,128]{1,0:T(8,128)(2,1)S(1)}, u32[]{:S(2)}, u32[]{:S(2)}) collective-permute-start(bf16[112,128]{1,0:T(8,128)(2,1)S(1)} %get-tuple-element.30.block_a), channel_id=1, source_target_pairs={{0,3},{1,2},{2,1},{3,0},{4,7},{5,6},{6,5},{7,4},{8,11},{9,10},{10,... | collective-permute-start | bytes 86024 | tf_op jit(solution)/shard_map/ppermute | solution.py:34
  30.4 3.2 %collective-permute-start.9 = (bf16[112,128]{1,0:T(8,128)(2,1)S(1)}, bf16[112,128]{1,0:T(8,128)(2,1)S(1)}, u32[]{:S(2)}, u32[]{:S(2)}) collective-permute-start(bf16[112,128]{1,0:T(8,128)(2,1)S(1)} %collective-permute-done.8.block_b), channel_id=1, source_target_pairs={{0,8},{8,0},{16,24},{24,16},{1,9},{9,1},{17,25},{25,17},{2,10},{10... | collective-permute-start | bytes 86024 | tf_op jit(solution)/shard_map/ppermute | solution.py:34

commit v5 on v4

--- a/solution.py
+++ b/solution.py
@@ -232,8 +232,9 @@
 
 
 MOD_PIECES = 4
-PROJ_PIECES = 2
-IN_FLIGHT = 6
+PROJ_PIECES = 3
+IN_FLIGHT = 12
+LATENTS_AFTER = 8
 PACK = 128
 CONTRACT_LAST = (((1,), (1,)), ((), ()))
 CONTRACT_FIRST = (((0,), (0,)), ((), ()))
@@ -294,15 +295,14 @@
     for m in range(3):
         order += [proj_piece(m, k) for k in range(PROJ_PIECES)]
         order += [mod_piece(m, k) for k in range(MOD_PIECES)]
-    order = small[:2] + order[:IN_FLIGHT] + small[2:] + order[IN_FLIGHT:]
-    ahead = IN_FLIGHT + 4
-    for copy in order[:ahead]:
+    order = small[:2] + order[:LATENTS_AFTER] + small[2:] + order[LATENTS_AFTER:]
+    for copy in order[:IN_FLIGHT]:
         copy.start()
 
     def take(position):
         order[position].wait()
-        if position + ahead < len(order):
-            order[position + ahead].start()
+        if position + IN_FLIGHT < len(order):
+            order[position + IN_FLIGHT].start()
 
     take(0)
     half_size = TEMB // 2
@@ -322,7 +322,7 @@
     for m in range(3):
         total = jnp.zeros((8, width), jnp.float32)
         for k in range(PROJ_PIECES + MOD_PIECES):
-            if place == IN_FLIGHT + 2:
+            if place == LATENTS_AFTER + 2:
                 take(place)
                 take(place + 1)
                 latents = jnp.where(lax.axis_index("mp") % 2 == 0, noise_ref[...], renoise_ref[...])

time: 36.6 us -> 36 us (0.984)
  Pallas kernels: 13.8 us -> 13.2 us
    pallas_call x1, Pallas kernels: 7.25 us -> 6.71 us  [streamed_weights(): pl.pallas_call(stream_kernel, out_shape=[jax.ShapeDtypeStruct((pack_rows,...]
where the time goes in v5:
time: 36 us; the launch traced here: 35.9 us
  Pallas kernels  13.2 us (37%)
  starting transfers between devices  11.3 us (31%)
  waiting for transfers between devices  9.31 us (26%)
  between operations  2.01 us (6%)
    ppermute x9, starting transfers between devices, swap(): return lax.ppermute(x, axes, [(i, i ^ mask) for i in range(count)])  8.1 us
    ppermute x9, waiting for transfers between devices, swap(): return lax.ppermute(x, axes, [(i, i ^ mask) for i in range(count)])  7.98 us
    pallas_call x1, Pallas kernels, streamed_weights(): pl.pallas_call(stream_kernel, out_shape=[jax.ShapeDtypeStruct((pack_rows,...  6.71 us
    pallas_call x1, Pallas kernels, gradient(): pl.pallas_call(grad_kernel, out_shape=[jax.ShapeDtypeStruct((rows, cols),...  2.79 us
    ppermute x1, starting transfers between devices, gather_samples(): near = lax.ppermute(x, ('mp', 'dp'), pairs)  1.64 us
    ppermute x1, starting transfers between devices, chip_blocks(): side = lax.ppermute(x, ('mp', 'fsdp'), pairs)  1.55 us
    pallas_call x1, Pallas kernels, token_phase(): pl.pallas_call(token_kernel, out_shape=[jax.ShapeDtypeStruct(renoise.shap...  1.43 us
    ppermute x1, waiting for transfers between devices, chip_blocks(): side = lax.ppermute(x, ('mp', 'fsdp'), pairs)  1.33 us
  transfers between devices with their start and end apart: 11, of which 5 were waited for; matrix products, arithmetic and copies ran while one was open for 0% of the time, Pallas kernels for 5%

profile of v5, /device:TPU:0, one launch (start us, length us, event | category | flops | bytes accessed | tf_op | source)
XLA Modules:
  0.0 35.9 jit_solution(708148661924571338)
XLA Ops:
  2.0 6.7 %stream_weights.1 = (f32[40,128]{1,0:T(8,128)S(1)}, bf16[256,128]{1,0:T(8,128)(2,1)S(1)}, bf16[3,64,1536]{2,1,0:T(8,128)(2,1)S(1)}) custom-call(s32[1]{0:T(128)S(6)} %copy.11.gen_step_ref, s32[1]{0:T(128)S(6)} %copy.12.renoise_step_ref, bf16[1,768]{1,0:T(2,128)(2,1)} %text_hbm.1, f32[256,128]{1,0:T(8,128)} %bitcast.3, f32[256,128]{1,0:T(8,128)} %bitcast.6, ...), custom_call_target="tpu_custom_call" | custom-call | tf_op jit(solution)/shard_map/stream_weights/pallas_call | solution.py:362
  8.7 0.5 %collective-permute-start = (f32[40,128]{1,0:T(8,128)S(1)}, f32[40,128]{1,0:T(8,128)S(1)}, u32[]{:S(2)}, u32[]{:S(2)}) collective-permute-start(f32[40,128]{1,0:T(8,128)S(1)} %get-tuple-element.18), channel_id=1, source_target_pairs={{0,8},{8,0},{16,24},{24,16},{1,9},{9,1},{17,25},{25,17},{2,10},{10... | collective-permute-start | bytes 61448 | tf_op jit(solution)/shard_map/ppermute | solution.py:34
  9.2 2.6 %collective-permute-start.2 = (bf16[256,128]{1,0:T(8,128)(2,1)S(1)}, bf16[256,128]{1,0:T(8,128)(2,1)S(1)}, u32[]{:S(2)}, u32[]{:S(2)}) collective-permute-start(bf16[256,128]{1,0:T(8,128)(2,1)S(1)} %get-tuple-element.19), channel_id=1, source_target_pairs={{0,4},{4,0},{1,5},{5,1},{2,6},{6,2},{3,7},{7,3},{8,12},{12,8},{9,1... | collective-permute-start | bytes 196616 | tf_op jit(solution)/shard_map/ppermute | solution.py:34
  11.8 0.0 collective-permute-done
  11.8 1.1 %collective-permute-start.1 = (f32[40,128]{1,0:T(8,128)S(1)}, f32[40,128]{1,0:T(8,128)S(1)}, u32[]{:S(2)}, u32[]{:S(2)}) collective-permute-start(f32[40,128]{1,0:T(8,128)S(1)} %get-tuple-element.35), channel_id=1, source_target_pairs={{0,4},{4,0},{1,5},{5,1},{2,6},{6,2},{3,7},{7,3},{8,12},{12,8},{9,1... | collective-permute-start | bytes 61448 | tf_op jit(solution)/shard_map/ppermute | solution.py:34
  12.9 1.2 %embed_products.1 = (bf16[3,128,384]{2,1,0:T(8,128)(2,1)S(1)}, f32[3,64,1536]{2,1,0:T(8,128)S(1)}, f32[3,64,128]{2,1,0:T(8,128)S(1)}) custom-call(bf16[3,64,3072]{2,1,0:T(8,128)(2,1)S(1)} %copy-done.2, bf16[3,64,768]{2,1,0:T(8,128)(2,1)S(1)} %copy-done), custom_call_target="tpu_custom_call" | custom-call | flops 301989888 | bytes 1179648 | tf_op jit(solution)/shard_map/embed_products/pallas_call | solution.py:420
  14.1 1.5 %collective-permute-done.1.got_ref = f32[40,128]{1,0:T(8,128)S(1)} collective-permute-done((f32[40,128]{1,0:T(8,128)S(1)}, f32[40,128]{1,0:T(8,128)S(1)}, u32[]{:S(2)}, u32[]{:S(2)}) %collective-permute-start.1) | collective-permute-done | bytes 20512 | tf_op jit(solution)/shard_map/ppermute | solution.py:34
  15.7 0.0 collective-permute-done.2.first_ref
  15.7 0.5 %modulated_maps.1 = (f32[216,128]{1,0:T(8,128)S(1)}, bf16[32,128]{1,0:T(8,128)(2,1)S(1)}) custom-call(f32[40,128]{1,0:T(8,128)S(1)} %get-tuple-element.34.kept_ref, f32[40,128]{1,0:T(8,128)S(1)} %collective-permute-done.1.got_ref, f32[3,64,1536]{2,1,0:T(8,128)S(1)} %get-tuple-element.25.rows_ref, bf16[3,64,1536]{2,1,0:T(8,128)(2,1)S(1)} %get-tuple-element.26.through_ref, ...), custom_call_target="tpu_custom_call" | custom-call | tf_op jit(solution)/shard_map/modulated_maps/pallas_call | solution.py:523
  16.2 0.1 collective-permute-start.4
  16.3 1.3 %collective-permute-done.4 = f32[216,128]{1,0:T(8,128)S(1)} collective-permute-done((f32[216,128]{1,0:T(8,128)S(1)}, f32[216,128]{1,0:T(8,128)S(1)}, u32[]{:S(2)}, u32[]{:S(2)}) %collective-permute-start.4) | collective-permute-done | bytes 110624 | tf_op jit(solution)/shard_map/ppermute | solution.py:34
  17.6 1.6 %collective-permute-start.5 = (bf16[216,128]{1,0:T(8,128)(2,1)S(1)}, bf16[216,128]{1,0:T(8,128)(2,1)S(1)}, u32[]{:S(2)}, u32[]{:S(2)}) collective-permute-start(bf16[216,128]{1,0:T(8,128)(2,1)S(1)} %add_convert_fusion.maps_a), channel_id=1, source_target_pairs={{0,16},{4,20},{8,12},{12,8},{16,0},{20,4},{24,28},{28,24},{1,17},{... | collective-permute-start | bytes 165896 | tf_op jit(solution)/shard_map/ppermute | solution.py:51
  19.1 0.0 collective-permute-start.3
  19.1 1.3 %collective-permute-start.7 = (bf16[216,128]{1,0:T(8,128)(2,1)S(1)}, bf16[216,128]{1,0:T(8,128)(2,1)S(1)}, u32[]{:S(2)}, u32[]{:S(2)}) collective-permute-start(bf16[216,128]{1,0:T(8,128)(2,1)S(1)} %add_convert_fusion.maps_a), channel_id=1, source_target_pairs={{0,20},{4,16},{8,28},{12,24},{16,4},{20,0},{24,12},{28,8},{1,21},{... | collective-permute-start | bytes 165896 | tf_op jit(solution)/shard_map/ppermute | solution.py:34
  20.5 1.3 %collective-permute-done.5.maps_b = bf16[216,128]{1,0:T(8,128)(2,1)S(1)} collective-permute-done((bf16[216,128]{1,0:T(8,128)(2,1)S(1)}, bf16[216,128]{1,0:T(8,128)(2,1)S(1)}, u32[]{:S(2)}, u32[]{:S(2)}) %collective-permute-start.5) | collective-permute-done | bytes 55328 | tf_op jit(solution)/shard_map/ppermute | solution.py:51
  21.8 0.0 collective-permute-start.6
  21.8 0.0 collective-permute-done.3.second_ref
  21.8 0.5 %noise_statistics.1 = (f32[512,128]{1,0:T(8,128)S(1)}, bf16[512,128]{1,0:T(8,128)(2,1)S(1)}) custom-call(f32[256,128]{1,0:T(8,128)S(1)} %bitcast.4, bf16[256,128]{1,0:T(8,128)(2,1)S(1)} %collective-permute-done.2.first_ref, bf16[256,128]{1,0:T(8,128)(2,1)S(1)} %collective-permute-done.3.second_ref, bf16[3,128,384]{2,1,0:T(8,128)(2,1)S(1)} %get-tuple-element.21.gram_ref), custom_call_target="tpu_custom_call" | custom-call | tf_op jit(solution)/shard_map/noise_statistics/pallas_call | solution.py:475
  22.4 2.0 %collective-permute-done.7.maps_d = bf16[216,128]{1,0:T(8,128)(2,1)S(1)} collective-permute-done((bf16[216,128]{1,0:T(8,128)(2,1)S(1)}, bf16[216,128]{1,0:T(8,128)(2,1)S(1)}, u32[]{:S(2)}, u32[]{:S(2)}) %collective-permute-start.7) | collective-permute-done | bytes 55328 | tf_op jit(solution)/shard_map/ppermute | solution.py:34
  24.3 1.4 %tokens.1 = (f32[256,128]{1,0:T(8,128)S(1)}, bf16[112,128]{1,0:T(8,128)(2,1)S(1)}) custom-call(f32[1]{0:T(128)S(6)} %div.3.level_ref, f32[256,128]{1,0:T(8,128)S(1)} %bitcast.5, bf16[256,128]{1,0:T(8,128)(2,1)S(1)} %collective-permute-done.2.first_ref, bf16[256,128]{1,0:T(8,128)(2,1)S(1)} %collective-permute-done.3.second_ref, f32[256,128]{1,0:T(8,128)S(1)} %bitcast.7, ...), custom_call_target="tpu_custom_call" | custom-call | tf_op jit(solution)/shard_map/tokens/pallas_call | solution.py:611
  25.8 1.6 %collective-permute-start.8 = (bf16[112,128]{1,0:T(8,128)(2,1)S(1)}, bf16[112,128]{1,0:T(8,128)(2,1)S(1)}, u32[]{:S(2)}, u32[]{:S(2)}) collective-permute-start(bf16[112,128]{1,0:T(8,128)(2,1)S(1)} %get-tuple-element.30.block_a), channel_id=1, source_target_pairs={{0,1},{1,0},{2,3},{3,2},{8,10},{9,11},{10,8},{11,9},{16,17},{17,16... | collective-permute-start | bytes 86024 | tf_op jit(solution)/shard_map/ppermute | solution.py:65
  27.4 2.5 %collective-permute-start.10 = (bf16[112,128]{1,0:T(8,128)(2,1)S(1)}, bf16[112,128]{1,0:T(8,128)(2,1)S(1)}, u32[]{:S(2)}, u32[]{:S(2)}) collective-permute-start(bf16[112,128]{1,0:T(8,128)(2,1)S(1)} %get-tuple-element.30.block_a), channel_id=1, source_target_pairs={{0,3},{1,2},{2,1},{3,0},{4,7},{5,6},{6,5},{7,4},{8,11},{9,10},{10,... | collective-permute-start | bytes 86024 | tf_op jit(solution)/shard_map/ppermute | solution.py:34
  29.9 3.2 %collective-permute-done.10.block_d = bf16[112,128]{1,0:T(8,128)(2,1)S(1)} collective-permute-done((bf16[112,128]{1,0:T(8,128)(2,1)S(1)}, bf16[112,128]{1,0:T(8,128)(2,1)S(1)}, u32[]{:S(2)}, u32[]{:S(2)}) %collective-permute-start.10) | collective-permute-done | bytes 28704 | tf_op jit(solution)/shard_map/ppermute | solution.py:34
  33.1 2.8 %gradient.1 = (f32[1536,768]{1,0:T(8,128)}, f32[256,128]{1,0:T(8,128)}) custom-call(bf16[112,128]{1,0:T(8,128)(2,1)S(1)} %get-tuple-element.30.block_a, bf16[112,128]{1,0:T(8,128)(2,1)S(1)} %collective-permute-done.8.block_b, bf16[112,128]{1,0:T(8,128)(2,1)S(1)} %collective-permute-done.9.block_c, bf16[112,128]{1,0:T(8,128)(2,1)S(1)} %collective-permute-done.10.block_d, ...), custom_call_target="tpu_custom_call" | custom-call | tf_op jit(solution)/shard_map/gradient/pallas_call | solution.py:682
  (14 shorter events, 0.1 us)
Async XLA Ops:
  1.9 11.0 %copy-start = (bf16[3,64,768]{2,1,0:T(8,128)(2,1)S(1)}, bf16[3,64,768]{2,1,0:T(8,128)(2,1)}, u32[]{:S(2)}) copy-start(bf16[3,64,768]{2,1,0:T(8,128)(2,1)} %unembed_ref.3) | copy-start | bytes 884740
  1.9 11.0 %copy-start.2 = (bf16[3,64,3072]{2,1,0:T(8,128)(2,1)S(1)}, bf16[3,64,3072]{2,1,0:T(8,128)(2,1)}, u32[]{:S(2)}) copy-start(bf16[3,64,3072]{2,1,0:T(8,128)(2,1)} %embed_ref.1) | copy-start | bytes 3538948
  1.9 19.9 %copy-start.1 = (f32[1,256,128]{2,1,0:T(8,128)S(1)}, f32[1,256,128]{2,1,0:T(8,128)}, u32[]{:S(2)}) copy-start(f32[1,256,128]{2,1,0:T(8,128)} %param.9) | copy-start | bytes 393220
  2.0 22.4 %copy-start.3 = (f32[1,256,128]{2,1,0:T(8,128)S(1)}, f32[1,256,128]{2,1,0:T(8,128)}, u32[]{:S(2)}) copy-start(f32[1,256,128]{2,1,0:T(8,128)} %param.10) | copy-start | bytes 393220
  8.7 3.1 %collective-permute-start = (f32[40,128]{1,0:T(8,128)S(1)}, f32[40,128]{1,0:T(8,128)S(1)}, u32[]{:S(2)}, u32[]{:S(2)}) collective-permute-start(f32[40,128]{1,0:T(8,128)S(1)} %get-tuple-element.18), channel_id=1, source_target_pairs={{0,8},{8,0},{16,24},{24,16},{1,9},{9,1},{17,25},{25,17},{2,10},{10... | collective-permute-start | bytes 61448 | tf_op jit(solution)/shard_map/ppermute | solution.py:34
  9.2 6.5 %collective-permute-start.2 = (bf16[256,128]{1,0:T(8,128)(2,1)S(1)}, bf16[256,128]{1,0:T(8,128)(2,1)S(1)}, u32[]{:S(2)}, u32[]{:S(2)}) collective-permute-start(bf16[256,128]{1,0:T(8,128)(2,1)S(1)} %get-tuple-element.19), channel_id=1, source_target_pairs={{0,4},{4,0},{1,5},{5,1},{2,6},{6,2},{3,7},{7,3},{8,12},{12,8},{9,1... | collective-permute-start | bytes 196616 | tf_op jit(solution)/shard_map/ppermute | solution.py:34
  11.8 3.8 %collective-permute-start.1 = (f32[40,128]{1,0:T(8,128)S(1)}, f32[40,128]{1,0:T(8,128)S(1)}, u32[]{:S(2)}, u32[]{:S(2)}) collective-permute-start(f32[40,128]{1,0:T(8,128)S(1)} %get-tuple-element.35), channel_id=1, source_target_pairs={{0,4},{4,0},{1,5},{5,1},{2,6},{6,2},{3,7},{7,3},{8,12},{12,8},{9,1... | collective-permute-start | bytes 61448 | tf_op jit(solution)/shard_map/ppermute | solution.py:34
  16.2 1.4 %collective-permute-start.4 = (f32[216,128]{1,0:T(8,128)S(1)}, f32[216,128]{1,0:T(8,128)S(1)}, u32[]{:S(2)}, u32[]{:S(2)}) collective-permute-start(f32[216,128]{1,0:T(8,128)S(1)} %get-tuple-element.28), channel_id=1, source_target_pairs={{0,8},{8,0},{16,24},{24,16},{1,9},{9,1},{17,25},{25,17},{2,10},{10... | collective-permute-start | bytes 331784 | tf_op jit(solution)/shard_map/ppermute | solution.py:34
  17.6 4.2 %collective-permute-start.5 = (bf16[216,128]{1,0:T(8,128)(2,1)S(1)}, bf16[216,128]{1,0:T(8,128)(2,1)S(1)}, u32[]{:S(2)}, u32[]{:S(2)}) collective-permute-start(bf16[216,128]{1,0:T(8,128)(2,1)S(1)} %add_convert_fusion.maps_a), channel_id=1, source_target_pairs={{0,16},{4,20},{8,12},{12,8},{16,0},{20,4},{24,28},{28,24},{1,17},{... | collective-permute-start | bytes 165896 | tf_op jit(solution)/shard_map/ppermute | solution.py:51
  19.1 2.7 %collective-permute-start.3 = (bf16[256,128]{1,0:T(8,128)(2,1)S(1)}, bf16[256,128]{1,0:T(8,128)(2,1)S(1)}, u32[]{:S(2)}, u32[]{:S(2)}) collective-permute-start(bf16[256,128]{1,0:T(8,128)(2,1)S(1)} %collective-permute-done.2.first_ref), channel_id=1, source_target_pairs={{0,8},{8,0},{16,24},{24,16},{1,9},{9,1},{17,25},{25,17},{2,10},{10... | collective-permute-start | bytes 196616 | tf_op jit(solution)/shard_map/ppermute | solution.py:34
  19.1 5.2 %collective-permute-start.7 = (bf16[216,128]{1,0:T(8,128)(2,1)S(1)}, bf16[216,128]{1,0:T(8,128)(2,1)S(1)}, u32[]{:S(2)}, u32[]{:S(2)}) collective-permute-start(bf16[216,128]{1,0:T(8,128)(2,1)S(1)} %add_convert_fusion.maps_a), channel_id=1, source_target_pairs={{0,20},{4,16},{8,28},{12,24},{16,4},{20,0},{24,12},{28,8},{1,21},{... | collective-permute-start | bytes 165896 | tf_op jit(solution)/shard_map/ppermute | solution.py:34
  21.8 2.5 %collective-permute-start.6 = (bf16[216,128]{1,0:T(8,128)(2,1)S(1)}, bf16[216,128]{1,0:T(8,128)(2,1)S(1)}, u32[]{:S(2)}, u32[]{:S(2)}) collective-permute-start(bf16[216,128]{1,0:T(8,128)(2,1)S(1)} %collective-permute-done.5.maps_b), channel_id=1, source_target_pairs={{0,8},{8,0},{16,24},{24,16},{1,9},{9,1},{17,25},{25,17},{2,10},{10... | collective-permute-start | bytes 165896 | tf_op jit(solution)/shard_map/ppermute | solution.py:34
  25.8 4.1 %collective-permute-start.8 = (bf16[112,128]{1,0:T(8,128)(2,1)S(1)}, bf16[112,128]{1,0:T(8,128)(2,1)S(1)}, u32[]{:S(2)}, u32[]{:S(2)}) collective-permute-start(bf16[112,128]{1,0:T(8,128)(2,1)S(1)} %get-tuple-element.30.block_a), channel_id=1, source_target_pairs={{0,1},{1,0},{2,3},{3,2},{8,10},{9,11},{10,8},{11,9},{16,17},{17,16... | collective-permute-start | bytes 86024 | tf_op jit(solution)/shard_map/ppermute | solution.py:65
  27.4 5.7 %collective-permute-start.10 = (bf16[112,128]{1,0:T(8,128)(2,1)S(1)}, bf16[112,128]{1,0:T(8,128)(2,1)S(1)}, u32[]{:S(2)}, u32[]{:S(2)}) collective-permute-start(bf16[112,128]{1,0:T(8,128)(2,1)S(1)} %get-tuple-element.30.block_a), channel_id=1, source_target_pairs={{0,3},{1,2},{2,1},{3,0},{4,7},{5,6},{6,5},{7,4},{8,11},{9,10},{10,... | collective-permute-start | bytes 86024 | tf_op jit(solution)/shard_map/ppermute | solution.py:34
  29.9 3.2 %collective-permute-start.9 = (bf16[112,128]{1,0:T(8,128)(2,1)S(1)}, bf16[112,128]{1,0:T(8,128)(2,1)S(1)}, u32[]{:S(2)}, u32[]{:S(2)}) collective-permute-start(bf16[112,128]{1,0:T(8,128)(2,1)S(1)} %collective-permute-done.8.block_b), channel_id=1, source_target_pairs={{0,8},{8,0},{16,24},{24,16},{1,9},{9,1},{17,25},{25,17},{2,10},{10... | collective-permute-start | bytes 86024 | tf_op jit(solution)/shard_map/ppermute | solution.py:34

commit v6 on v5

--- a/solution.py
+++ b/solution.py
@@ -492,6 +492,7 @@
     kept, got = kept_ref[...], got_ref[...]
     shift = jnp.where(f == 0, kept, got)
     scale = jnp.where(f == 0, got, kept)
+    offsets = []
     for m in range(3):
         pieces = []
         for j in range(packs):
@@ -511,9 +512,9 @@
         product = lax.dot_general(
             left, through, CONTRACT_LAST, preferred_element_type=jnp.float32
         )
-        base = m * (CH + 8)
-        maps_ref[base : base + CH] = product[:CH] + direct_ref[m]
-        maps_ref[base + CH : base + CH + 8] = product[CH:]
+        maps_ref[m * CH : (m + 1) * CH] = product[:CH] + direct_ref[m]
+        offsets.append(product[CH : CH + 1])
+    maps_ref[3 * CH :] = jnp.concatenate(offsets + [jnp.zeros((5, PACK), jnp.float32)], 0)
     rest = jnp.zeros((mod_ref.shape[0] - 2 * packs, PACK), jnp.float32)
     mod_ref[...] = jnp.concatenate([shift[:packs], scale[:packs], rest], 0).astype(jnp.bfloat16)
 
@@ -523,7 +524,7 @@
     return pl.pallas_call(
         maps_kernel,
         out_shape=[
-            jax.ShapeDtypeStruct((3 * (CH + 8), 2 * CH), jnp.float32),
+            jax.ShapeDtypeStruct((3 * CH + 8, 2 * CH), jnp.float32),
             jax.ShapeDtypeStruct((-(-2 * packs // 16) * 16, PACK), jnp.bfloat16),
         ],
         in_specs=whole_specs(5),
@@ -561,17 +562,17 @@
     ones = pair_ones()
 
     def model_matrix(m):
-        base = m * (CH + 8)
+        base = m * CH
         pair = maps[base : base + CH]
         turned = pltpu.roll(pair, CH, 1)
-        direct = split_two(block_diagonal(pair, turned))
-        modulated = split_two(block_diagonal(turned, pair))
-        offset = maps[base + CH : base + CH + 1]
-        return jnp.concatenate(direct + modulated, 1), offset + pltpu.roll(offset, CH, 1)
+        direct = block_diagonal(pair, turned)
+        modulated = block_diagonal(turned, pair)
+        matrix = jnp.concatenate([direct, modulated], 1).astype(jnp.bfloat16)
+        offset = maps[3 * CH + m : 3 * CH + m + 1]
+        return matrix, offset + pltpu.roll(offset, CH, 1)
 
     def combine(product, inverse, offset):
-        direct = columns(product, 0) + columns(product, 1)
-        return direct + inverse * (columns(product, 2) + columns(product, 3)) + offset
+        return columns(product, 0) + inverse * columns(product, 1) + offset
 
     noise, other_renoise = sample_latents(noise_ref, first_ref, second_ref)
     renoise = jnp.concatenate([renoise_ref[...], other_renoise.astype(jnp.float32)], 0)
@@ -585,7 +586,7 @@
         matrix, offset = model_matrix(m)
         matrix = jnp.concatenate([matrix, gram_ref[m]], 1)
         product = jnp.dot(noisy, matrix, preferred_element_type=jnp.float32)
-        by_gram = columns(product, 4) + columns(product, 5) + columns(product, 6)
+        by_gram = columns(product, 2) + columns(product, 3) + columns(product, 4)
         return combine(product, inverse_deviation(noisy_wide, by_gram, ones), offset)
 
     real_v = velocity(1)

time: 36 us -> 35.8 us (level)
  no operation moved by 1% of the time
where the time goes in v6:
time: 35.8 us; the launch traced here: 35.6 us
  Pallas kernels  13.1 us (37%)
  starting transfers between devices  11.3 us (32%)
  waiting for transfers between devices  9.21 us (26%)
  between operations  2.02 us (6%)
    ppermute x9, starting transfers between devices, swap(): return lax.ppermute(x, axes, [(i, i ^ mask) for i in range(count)])  8.1 us
    ppermute x9, waiting for transfers between devices, swap(): return lax.ppermute(x, axes, [(i, i ^ mask) for i in range(count)])  7.92 us
    pallas_call x1, Pallas kernels, streamed_weights(): pl.pallas_call(stream_kernel, out_shape=[jax.ShapeDtypeStruct((pack_rows,...  6.71 us
    pallas_call x1, Pallas kernels, gradient(): pl.pallas_call(grad_kernel, out_shape=[jax.ShapeDtypeStruct((rows, cols),...  2.79 us
    ppermute x1, starting transfers between devices, gather_samples(): near = lax.ppermute(x, ('mp', 'dp'), pairs)  1.64 us
    ppermute x1, starting transfers between devices, chip_blocks(): side = lax.ppermute(x, ('mp', 'fsdp'), pairs)  1.55 us
    ppermute x1, waiting for transfers between devices, chip_blocks(): side = lax.ppermute(x, ('mp', 'fsdp'), pairs)  1.29 us
    pallas_call x1, Pallas kernels, token_phase(): pl.pallas_call(token_kernel, out_shape=[jax.ShapeDtypeStruct(renoise.shap...  1.27 us
  transfers between devices with their start and end apart: 11, of which 5 were waited for; matrix products, arithmetic and copies ran while one was open for 0% of the time, Pallas kernels for 5%

profile of v6, /device:TPU:0, one launch (start us, length us, event | category | flops | bytes accessed | tf_op | source)
XLA Modules:
  0.0 35.6 jit_solution(1734842923577086420)
XLA Ops:
  2.0 6.7 %stream_weights.1 = (f32[40,128]{1,0:T(8,128)S(1)}, bf16[256,128]{1,0:T(8,128)(2,1)S(1)}, bf16[3,64,1536]{2,1,0:T(8,128)(2,1)S(1)}) custom-call(s32[1]{0:T(128)S(6)} %copy.11.gen_step_ref, s32[1]{0:T(128)S(6)} %copy.12.renoise_step_ref, bf16[1,768]{1,0:T(2,128)(2,1)} %text_hbm.1, f32[256,128]{1,0:T(8,128)} %bitcast.3, f32[256,128]{1,0:T(8,128)} %bitcast.6, ...), custom_call_target="tpu_custom_call" | custom-call | tf_op jit(solution)/shard_map/stream_weights/pallas_call | solution.py:362
  8.7 0.5 %collective-permute-start = (f32[40,128]{1,0:T(8,128)S(1)}, f32[40,128]{1,0:T(8,128)S(1)}, u32[]{:S(2)}, u32[]{:S(2)}) collective-permute-start(f32[40,128]{1,0:T(8,128)S(1)} %get-tuple-element.18), channel_id=1, source_target_pairs={{0,8},{8,0},{16,24},{24,16},{1,9},{9,1},{17,25},{25,17},{2,10},{10... | collective-permute-start | bytes 61448 | tf_op jit(solution)/shard_map/ppermute | solution.py:34
  9.2 2.6 %collective-permute-start.2 = (bf16[256,128]{1,0:T(8,128)(2,1)S(1)}, bf16[256,128]{1,0:T(8,128)(2,1)S(1)}, u32[]{:S(2)}, u32[]{:S(2)}) collective-permute-start(bf16[256,128]{1,0:T(8,128)(2,1)S(1)} %get-tuple-element.19), channel_id=1, source_target_pairs={{0,4},{4,0},{1,5},{5,1},{2,6},{6,2},{3,7},{7,3},{8,12},{12,8},{9,1... | collective-permute-start | bytes 196616 | tf_op jit(solution)/shard_map/ppermute | solution.py:34
  11.8 1.1 %collective-permute-start.1 = (f32[40,128]{1,0:T(8,128)S(1)}, f32[40,128]{1,0:T(8,128)S(1)}, u32[]{:S(2)}, u32[]{:S(2)}) collective-permute-start(f32[40,128]{1,0:T(8,128)S(1)} %get-tuple-element.35), channel_id=1, source_target_pairs={{0,4},{4,0},{1,5},{5,1},{2,6},{6,2},{3,7},{7,3},{8,12},{12,8},{9,1... | collective-permute-start | bytes 61448 | tf_op jit(solution)/shard_map/ppermute | solution.py:34
  12.9 1.2 %embed_products.1 = (bf16[3,128,384]{2,1,0:T(8,128)(2,1)S(1)}, f32[3,64,1536]{2,1,0:T(8,128)S(1)}, f32[3,64,128]{2,1,0:T(8,128)S(1)}) custom-call(bf16[3,64,3072]{2,1,0:T(8,128)(2,1)S(1)} %copy-done.2, bf16[3,64,768]{2,1,0:T(8,128)(2,1)S(1)} %copy-done), custom_call_target="tpu_custom_call" | custom-call | flops 301989888 | bytes 1179648 | tf_op jit(solution)/shard_map/embed_products/pallas_call | solution.py:420
  14.1 1.5 %collective-permute-done.1.got_ref = f32[40,128]{1,0:T(8,128)S(1)} collective-permute-done((f32[40,128]{1,0:T(8,128)S(1)}, f32[40,128]{1,0:T(8,128)S(1)}, u32[]{:S(2)}, u32[]{:S(2)}) %collective-permute-start.1) | collective-permute-done | bytes 20512 | tf_op jit(solution)/shard_map/ppermute | solution.py:34
  15.7 0.0 collective-permute-done.2.first_ref
  15.7 0.5 %modulated_maps.1 = (f32[200,128]{1,0:T(8,128)S(1)}, bf16[32,128]{1,0:T(8,128)(2,1)S(1)}) custom-call(f32[40,128]{1,0:T(8,128)S(1)} %get-tuple-element.34.kept_ref, f32[40,128]{1,0:T(8,128)S(1)} %collective-permute-done.1.got_ref, f32[3,64,1536]{2,1,0:T(8,128)S(1)} %get-tuple-element.25.rows_ref, bf16[3,64,1536]{2,1,0:T(8,128)(2,1)S(1)} %get-tuple-element.26.through_ref, ...), custom_call_target="tpu_custom_call" | custom-call | tf_op jit(solution)/shard_map/modulated_maps/pallas_call | solution.py:524
  16.2 0.1 collective-permute-start.4
  16.3 1.3 %collective-permute-done.4 = f32[200,128]{1,0:T(8,128)S(1)} collective-permute-done((f32[200,128]{1,0:T(8,128)S(1)}, f32[200,128]{1,0:T(8,128)S(1)}, u32[]{:S(2)}, u32[]{:S(2)}) %collective-permute-start.4) | collective-permute-done | bytes 102432 | tf_op jit(solution)/shard_map/ppermute | solution.py:34
  17.6 1.6 %collective-permute-start.5 = (bf16[200,128]{1,0:T(8,128)(2,1)S(1)}, bf16[200,128]{1,0:T(8,128)(2,1)S(1)}, u32[]{:S(2)}, u32[]{:S(2)}) collective-permute-start(bf16[200,128]{1,0:T(8,128)(2,1)S(1)} %add_convert_fusion.maps_a), channel_id=1, source_target_pairs={{0,16},{4,20},{8,12},{12,8},{16,0},{20,4},{24,28},{28,24},{1,17},{... | collective-permute-start | bytes 153608 | tf_op jit(solution)/shard_map/ppermute | solution.py:51
  19.1 0.0 collective-permute-start.3
  19.1 1.3 %collective-permute-start.7 = (bf16[200,128]{1,0:T(8,128)(2,1)S(1)}, bf16[200,128]{1,0:T(8,128)(2,1)S(1)}, u32[]{:S(2)}, u32[]{:S(2)}) collective-permute-start(bf16[200,128]{1,0:T(8,128)(2,1)S(1)} %add_convert_fusion.maps_a), channel_id=1, source_target_pairs={{0,20},{4,16},{8,28},{12,24},{16,4},{20,0},{24,12},{28,8},{1,21},{... | collective-permute-start | bytes 153608 | tf_op jit(solution)/shard_map/ppermute | solution.py:34
  20.5 1.3 %collective-permute-done.5.maps_b = bf16[200,128]{1,0:T(8,128)(2,1)S(1)} collective-permute-done((bf16[200,128]{1,0:T(8,128)(2,1)S(1)}, bf16[200,128]{1,0:T(8,128)(2,1)S(1)}, u32[]{:S(2)}, u32[]{:S(2)}) %collective-permute-start.5) | collective-permute-done | bytes 51232 | tf_op jit(solution)/shard_map/ppermute | solution.py:51
  21.8 0.5 %noise_statistics.1 = (f32[512,128]{1,0:T(8,128)S(1)}, bf16[512,128]{1,0:T(8,128)(2,1)S(1)}) custom-call(f32[256,128]{1,0:T(8,128)S(1)} %bitcast.4, bf16[256,128]{1,0:T(8,128)(2,1)S(1)} %collective-permute-done.2.first_ref, bf16[256,128]{1,0:T(8,128)(2,1)S(1)} %collective-permute-done.3.second_ref, bf16[3,128,384]{2,1,0:T(8,128)(2,1)S(1)} %get-tuple-element.21.gram_ref), custom_call_target="tpu_custom_call" | custom-call | tf_op jit(solution)/shard_map/noise_statistics/pallas_call | solution.py:475
  22.3 1.9 %collective-permute-done.7.maps_d = bf16[200,128]{1,0:T(8,128)(2,1)S(1)} collective-permute-done((bf16[200,128]{1,0:T(8,128)(2,1)S(1)}, bf16[200,128]{1,0:T(8,128)(2,1)S(1)}, u32[]{:S(2)}, u32[]{:S(2)}) %collective-permute-start.7) | collective-permute-done | bytes 51232 | tf_op jit(solution)/shard_map/ppermute | solution.py:34
  24.2 0.0 collective-permute-done.6.maps_c
  24.2 1.3 %tokens.1 = (f32[256,128]{1,0:T(8,128)S(1)}, bf16[112,128]{1,0:T(8,128)(2,1)S(1)}) custom-call(f32[1]{0:T(128)S(6)} %div.3.level_ref, f32[256,128]{1,0:T(8,128)S(1)} %bitcast.5, bf16[256,128]{1,0:T(8,128)(2,1)S(1)} %collective-permute-done.2.first_ref, bf16[256,128]{1,0:T(8,128)(2,1)S(1)} %collective-permute-done.3.second_ref, f32[256,128]{1,0:T(8,128)S(1)} %bitcast.7, ...), custom_call_target="tpu_custom_call" | custom-call | tf_op jit(solution)/shard_map/tokens/pallas_call | solution.py:612
  25.5 1.6 %collective-permute-start.8 = (bf16[112,128]{1,0:T(8,128)(2,1)S(1)}, bf16[112,128]{1,0:T(8,128)(2,1)S(1)}, u32[]{:S(2)}, u32[]{:S(2)}) collective-permute-start(bf16[112,128]{1,0:T(8,128)(2,1)S(1)} %get-tuple-element.30.block_a), channel_id=1, source_target_pairs={{0,1},{1,0},{2,3},{3,2},{8,10},{9,11},{10,8},{11,9},{16,17},{17,16... | collective-permute-start | bytes 86024 | tf_op jit(solution)/shard_map/ppermute | solution.py:65
  27.2 2.5 %collective-permute-start.10 = (bf16[112,128]{1,0:T(8,128)(2,1)S(1)}, bf16[112,128]{1,0:T(8,128)(2,1)S(1)}, u32[]{:S(2)}, u32[]{:S(2)}) collective-permute-start(bf16[112,128]{1,0:T(8,128)(2,1)S(1)} %get-tuple-element.30.block_a), channel_id=1, source_target_pairs={{0,3},{1,2},{2,1},{3,0},{4,7},{5,6},{6,5},{7,4},{8,11},{9,10},{10,... | collective-permute-start | bytes 86024 | tf_op jit(solution)/shard_map/ppermute | solution.py:34
  29.6 0.0 collective-permute-done.8.block_b
  29.6 0.0 collective-permute-start.9
  29.6 3.2 %collective-permute-done.10.block_d = bf16[112,128]{1,0:T(8,128)(2,1)S(1)} collective-permute-done((bf16[112,128]{1,0:T(8,128)(2,1)S(1)}, bf16[112,128]{1,0:T(8,128)(2,1)S(1)}, u32[]{:S(2)}, u32[]{:S(2)}) %collective-permute-start.10) | collective-permute-done | bytes 28704 | tf_op jit(solution)/shard_map/ppermute | solution.py:34
  32.8 2.8 %gradient.1 = (f32[1536,768]{1,0:T(8,128)}, f32[256,128]{1,0:T(8,128)}) custom-call(bf16[112,128]{1,0:T(8,128)(2,1)S(1)} %get-tuple-element.30.block_a, bf16[112,128]{1,0:T(8,128)(2,1)S(1)} %collective-permute-done.8.block_b, bf16[112,128]{1,0:T(8,128)(2,1)S(1)} %collective-permute-done.9.block_c, bf16[112,128]{1,0:T(8,128)(2,1)S(1)} %collective-permute-done.10.block_d, ...), custom_call_target="tpu_custom_call" | custom-call | tf_op jit(solution)/shard_map/gradient/pallas_call | solution.py:683
  (14 shorter events, 0.0 us)
Async XLA Ops:
  1.9 11.0 %copy-start = (bf16[3,64,768]{2,1,0:T(8,128)(2,1)S(1)}, bf16[3,64,768]{2,1,0:T(8,128)(2,1)}, u32[]{:S(2)}) copy-start(bf16[3,64,768]{2,1,0:T(8,128)(2,1)} %unembed_ref.3) | copy-start | bytes 884740
  1.9 11.0 %copy-start.2 = (bf16[3,64,3072]{2,1,0:T(8,128)(2,1)S(1)}, bf16[3,64,3072]{2,1,0:T(8,128)(2,1)}, u32[]{:S(2)}) copy-start(bf16[3,64,3072]{2,1,0:T(8,128)(2,1)} %embed_ref.1) | copy-start | bytes 3538948
  1.9 19.8 %copy-start.1 = (f32[1,256,128]{2,1,0:T(8,128)S(1)}, f32[1,256,128]{2,1,0:T(8,128)}, u32[]{:S(2)}) copy-start(f32[1,256,128]{2,1,0:T(8,128)} %param.9) | copy-start | bytes 393220
  2.0 22.3 %copy-start.3 = (f32[1,256,128]{2,1,0:T(8,128)S(1)}, f32[1,256,128]{2,1,0:T(8,128)}, u32[]{:S(2)}) copy-start(f32[1,256,128]{2,1,0:T(8,128)} %param.10) | copy-start | bytes 393220
  8.7 3.1 %collective-permute-start = (f32[40,128]{1,0:T(8,128)S(1)}, f32[40,128]{1,0:T(8,128)S(1)}, u32[]{:S(2)}, u32[]{:S(2)}) collective-permute-start(f32[40,128]{1,0:T(8,128)S(1)} %get-tuple-element.18), channel_id=1, source_target_pairs={{0,8},{8,0},{16,24},{24,16},{1,9},{9,1},{17,25},{25,17},{2,10},{10... | collective-permute-start | bytes 61448 | tf_op jit(solution)/shard_map/ppermute | solution.py:34
  9.2 6.5 %collective-permute-start.2 = (bf16[256,128]{1,0:T(8,128)(2,1)S(1)}, bf16[256,128]{1,0:T(8,128)(2,1)S(1)}, u32[]{:S(2)}, u32[]{:S(2)}) collective-permute-start(bf16[256,128]{1,0:T(8,128)(2,1)S(1)} %get-tuple-element.19), channel_id=1, source_target_pairs={{0,4},{4,0},{1,5},{5,1},{2,6},{6,2},{3,7},{7,3},{8,12},{12,8},{9,1... | collective-permute-start | bytes 196616 | tf_op jit(solution)/shard_map/ppermute | solution.py:34
  11.8 3.8 %collective-permute-start.1 = (f32[40,128]{1,0:T(8,128)S(1)}, f32[40,128]{1,0:T(8,128)S(1)}, u32[]{:S(2)}, u32[]{:S(2)}) collective-permute-start(f32[40,128]{1,0:T(8,128)S(1)} %get-tuple-element.35), channel_id=1, source_target_pairs={{0,4},{4,0},{1,5},{5,1},{2,6},{6,2},{3,7},{7,3},{8,12},{12,8},{9,1... | collective-permute-start | bytes 61448 | tf_op jit(solution)/shard_map/ppermute | solution.py:34
  16.2 1.4 %collective-permute-start.4 = (f32[200,128]{1,0:T(8,128)S(1)}, f32[200,128]{1,0:T(8,128)S(1)}, u32[]{:S(2)}, u32[]{:S(2)}) collective-permute-start(f32[200,128]{1,0:T(8,128)S(1)} %get-tuple-element.28), channel_id=1, source_target_pairs={{0,8},{8,0},{16,24},{24,16},{1,9},{9,1},{17,25},{25,17},{2,10},{10... | collective-permute-start | bytes 307208 | tf_op jit(solution)/shard_map/ppermute | solution.py:34
  17.6 4.2 %collective-permute-start.5 = (bf16[200,128]{1,0:T(8,128)(2,1)S(1)}, bf16[200,128]{1,0:T(8,128)(2,1)S(1)}, u32[]{:S(2)}, u32[]{:S(2)}) collective-permute-start(bf16[200,128]{1,0:T(8,128)(2,1)S(1)} %add_convert_fusion.maps_a), channel_id=1, source_target_pairs={{0,16},{4,20},{8,12},{12,8},{16,0},{20,4},{24,28},{28,24},{1,17},{... | collective-permute-start | bytes 153608 | tf_op jit(solution)/shard_map/ppermute | solution.py:51
  19.1 2.6 %collective-permute-start.3 = (bf16[256,128]{1,0:T(8,128)(2,1)S(1)}, bf16[256,128]{1,0:T(8,128)(2,1)S(1)}, u32[]{:S(2)}, u32[]{:S(2)}) collective-permute-start(bf16[256,128]{1,0:T(8,128)(2,1)S(1)} %collective-permute-done.2.first_ref), channel_id=1, source_target_pairs={{0,8},{8,0},{16,24},{24,16},{1,9},{9,1},{17,25},{25,17},{2,10},{10... | collective-permute-start | bytes 196616 | tf_op jit(solution)/shard_map/ppermute | solution.py:34
  19.1 5.1 %collective-permute-start.7 = (bf16[200,128]{1,0:T(8,128)(2,1)S(1)}, bf16[200,128]{1,0:T(8,128)(2,1)S(1)}, u32[]{:S(2)}, u32[]{:S(2)}) collective-permute-start(bf16[200,128]{1,0:T(8,128)(2,1)S(1)} %add_convert_fusion.maps_a), channel_id=1, source_target_pairs={{0,20},{4,16},{8,28},{12,24},{16,4},{20,0},{24,12},{28,8},{1,21},{... | collective-permute-start | bytes 153608 | tf_op jit(solution)/shard_map/ppermute | solution.py:34
  21.8 2.5 %collective-permute-start.6 = (bf16[200,128]{1,0:T(8,128)(2,1)S(1)}, bf16[200,128]{1,0:T(8,128)(2,1)S(1)}, u32[]{:S(2)}, u32[]{:S(2)}) collective-permute-start(bf16[200,128]{1,0:T(8,128)(2,1)S(1)} %collective-permute-done.5.maps_b), channel_id=1, source_target_pairs={{0,8},{8,0},{16,24},{24,16},{1,9},{9,1},{17,25},{25,17},{2,10},{10... | collective-permute-start | bytes 153608 | tf_op jit(solution)/shard_map/ppermute | solution.py:34
  25.5 4.1 %collective-permute-start.8 = (bf16[112,128]{1,0:T(8,128)(2,1)S(1)}, bf16[112,128]{1,0:T(8,128)(2,1)S(1)}, u32[]{:S(2)}, u32[]{:S(2)}) collective-permute-start(bf16[112,128]{1,0:T(8,128)(2,1)S(1)} %get-tuple-element.30.block_a), channel_id=1, source_target_pairs={{0,1},{1,0},{2,3},{3,2},{8,10},{9,11},{10,8},{11,9},{16,17},{17,16... | collective-permute-start | bytes 86024 | tf_op jit(solution)/shard_map/ppermute | solution.py:65
  27.2 5.7 %collective-permute-start.10 = (bf16[112,128]{1,0:T(8,128)(2,1)S(1)}, bf16[112,128]{1,0:T(8,128)(2,1)S(1)}, u32[]{:S(2)}, u32[]{:S(2)}) collective-permute-start(bf16[112,128]{1,0:T(8,128)(2,1)S(1)} %get-tuple-element.30.block_a), channel_id=1, source_target_pairs={{0,3},{1,2},{2,1},{3,0},{4,7},{5,6},{6,5},{7,4},{8,11},{9,10},{10,... | collective-permute-start | bytes 86024 | tf_op jit(solution)/shard_map/ppermute | solution.py:34
  29.6 3.2 %collective-permute-start.9 = (bf16[112,128]{1,0:T(8,128)(2,1)S(1)}, bf16[112,128]{1,0:T(8,128)(2,1)S(1)}, u32[]{:S(2)}, u32[]{:S(2)}) collective-permute-start(bf16[112,128]{1,0:T(8,128)(2,1)S(1)} %collective-permute-done.8.block_b), channel_id=1, source_target_pairs={{0,8},{8,0},{16,24},{24,16},{1,9},{9,1},{17,25},{25,17},{2,10},{10... | collective-permute-start | bytes 86024 | tf_op jit(solution)/shard_map/ppermute | solution.py:34

commit v7 on v6

--- a/solution.py
+++ b/solution.py
@@ -249,13 +249,15 @@
     mod_hbm,
     proj_hbm,
     unembed_hbm,
+    embed_hbm,
     mod_ref,
     latents_ref,
     through_ref,
-    text_ref,
     noise_ref,
     renoise_ref,
     unembed_ref,
+    embed_ref,
+    text_ref,
     mod_buffer,
     proj_buffer,
     mod_sems,
@@ -288,6 +290,7 @@
                 (unembed_hbm, unembed_ref),
                 (noise_hbm, noise_ref),
                 (renoise_hbm, renoise_ref),
+                (embed_hbm, embed_ref),
             )
         )
     ]
@@ -295,7 +298,7 @@
     for m in range(3):
         order += [proj_piece(m, k) for k in range(PROJ_PIECES)]
         order += [mod_piece(m, k) for k in range(MOD_PIECES)]
-    order = small[:2] + order[:LATENTS_AFTER] + small[2:] + order[LATENTS_AFTER:]
+    order = small[:2] + order[:LATENTS_AFTER] + small[2:4] + order[LATENTS_AFTER:] + small[4:]
     for copy in order[:IN_FLIGHT]:
         copy.start()
 
@@ -351,10 +354,11 @@
             line = total[1:2]
         for j in range(packs):
             mod_ref[m * packs + j : m * packs + j + 1] = line[:, j * PACK : (j + 1) * PACK]
+    take(len(order) - 1)
 
 
 def streamed_weights(
-    gen_step, renoise_step, text, noise, renoise, mod_weight, proj_weight, unembed
+    gen_step, renoise_step, text, noise, renoise, mod_weight, proj_weight, unembed, embed
 ):
     depth, width = mod_weight.shape[1], mod_weight.shape[2] // 2
     rows, cols = proj_weight.shape[1:]
@@ -365,20 +369,21 @@
             jax.ShapeDtypeStruct((pack_rows, PACK), jnp.float32),
             jax.ShapeDtypeStruct(noise.shape, jnp.bfloat16),
             jax.ShapeDtypeStruct((3, CH, rows), jnp.bfloat16),
+            jax.ShapeDtypeStruct(noise.shape, noise.dtype),
+            jax.ShapeDtypeStruct(renoise.shape, renoise.dtype),
+            jax.ShapeDtypeStruct(unembed.shape, unembed.dtype),
+            jax.ShapeDtypeStruct(embed.shape, embed.dtype),
         ],
         in_specs=[pl.BlockSpec(memory_space=pltpu.SMEM)] * 2
-        + [pl.BlockSpec(memory_space=pltpu.HBM)] * 6,
-        out_specs=whole_specs(3),
+        + [pl.BlockSpec(memory_space=pltpu.HBM)] * 7,
+        out_specs=whole_specs(7),
         scratch_shapes=[
             pltpu.VMEM(text.shape, text.dtype),
-            pltpu.VMEM(noise.shape, noise.dtype),
-            pltpu.VMEM(renoise.shape, renoise.dtype),
-            pltpu.VMEM(unembed.shape, unembed.dtype),
             pltpu.VMEM((3, depth, width), jnp.bfloat16),
             pltpu.VMEM((3, rows, cols), jnp.bfloat16),
             pltpu.SemaphoreType.DMA((3, MOD_PIECES)),
             pltpu.SemaphoreType.DMA((3, PROJ_PIECES)),
-            pltpu.SemaphoreType.DMA((4,)),
+            pltpu.SemaphoreType.DMA((5,)),
         ],
         compiler_params=vmem_params(),
         name="stream_weights",
@@ -387,7 +392,7 @@
         renoise_step,
         *(
             pltpu.with_memory_space_constraint(x, pltpu.HBM)
-            for x in (text, noise, renoise, mod_weight, proj_weight, unembed)
+            for x in (text, noise, renoise, mod_weight, proj_weight, unembed, embed)
         ),
     )
 
@@ -700,7 +705,7 @@
 def body(
     gen_noise, renoise, gen_step, renoise_step, text_pooled, embed, mod_weight, proj_weight, unembed
 ):
-    mine, latents, through = streamed_weights(
+    mine, latents, through, noise, renoise, unembed, embed = streamed_weights(
         gen_step,
         renoise_step,
         text_pooled,
@@ -709,6 +714,7 @@
         mod_weight,
         proj_weight,
         unembed,
+        embed,
     )
     f = lax.axis_index("fsdp")
     theirs = swap(mine, "mp", 1)
@@ -721,11 +727,11 @@
     gram, rows_part, direct = embed_products(embed, unembed, proj_weight.shape[1])
     maps, mod = modulated_maps(kept, got, rows_part, through, direct)
     maps = (maps + swap(maps, "mp", 1)).astype(jnp.bfloat16)
-    inverse, normal = noise_statistics(gen_noise[0], first, second, gram)
+    inverse, normal = noise_statistics(noise, first, second, gram)
     maps = chip_blocks(maps)
     level = renoise_step.astype(jnp.float32) / 1000.0
     score, payload = token_phase(
-        level, gen_noise[0], first, second, renoise[0], inverse, normal, gram, maps, mod
+        level, noise, first, second, renoise, inverse, normal, gram, maps, mod
     )
     blocks = gather_samples(payload)
     gen_grad, score_gap = gradient(blocks, rows_part, unembed, score)

time: 35.8 us -> 35.8 us (level)
  no operation moved by 1% of the time
where the time goes in v7:
time: 35.8 us; the launch traced here: 35.6 us
  Pallas kernels  13 us (36%)
  starting transfers between devices  11.3 us (32%)
  waiting for transfers between devices  9.23 us (26%)
  between operations  1.98 us (6%)
    ppermute x9, starting transfers between devices, swap(): return lax.ppermute(x, axes, [(i, i ^ mask) for i in range(count)])  8.1 us
    ppermute x9, waiting for transfers between devices, swap(): return lax.ppermute(x, axes, [(i, i ^ mask) for i in range(count)])  7.94 us
    pallas_call x1, Pallas kernels, streamed_weights(): pl.pallas_call(stream_kernel, out_shape=[jax.ShapeDtypeStruct((pack_rows,...  6.71 us
    pallas_call x1, Pallas kernels, gradient(): pl.pallas_call(grad_kernel, out_shape=[jax.ShapeDtypeStruct((rows, cols),...  2.79 us
    ppermute x1, starting transfers between devices, gather_samples(): near = lax.ppermute(x, ('mp', 'dp'), pairs)  1.64 us
    ppermute x1, starting transfers between devices, chip_blocks(): side = lax.ppermute(x, ('mp', 'fsdp'), pairs)  1.56 us
    ppermute x1, waiting for transfers between devices, chip_blocks(): side = lax.ppermute(x, ('mp', 'fsdp'), pairs)  1.28 us
    pallas_call x1, Pallas kernels, token_phase(): pl.pallas_call(token_kernel, out_shape=[jax.ShapeDtypeStruct(renoise.shap...  1.26 us
  transfers between devices with their start and end apart: 11, of which 5 were waited for; matrix products, arithmetic and copies ran while one was open for 0% of the time, Pallas kernels for 5%

profile of v7, /device:TPU:0, one launch (start us, length us, event | category | flops | bytes accessed | tf_op | source)
XLA Modules:
  0.0 35.6 jit_solution(10868953802903262186)
XLA Ops:
  1.9 6.7 %stream_weights.1 = (f32[40,128]{1,0:T(8,128)S(1)}, bf16[256,128]{1,0:T(8,128)(2,1)S(1)}, bf16[3,64,1536]{2,1,0:T(8,128)(2,1)S(1)}, f32[256,128]{1,0:T(8,128)S(1...) custom-call(s32[1]{0:T(128)S(6)} %copy.11.gen_step_ref, ...), custom_call_target="tpu_custom_call" | custom-call | tf_op jit(solution)/shard_map/stream_weights/pallas_call | solution.py:366
  8.6 0.5 %collective-permute-start = (f32[40,128]{1,0:T(8,128)S(1)}, f32[40,128]{1,0:T(8,128)S(1)}, u32[]{:S(2)}, u32[]{:S(2)}) collective-permute-start(f32[40,128]{1,0:T(8,128)S(1)} %get-tuple-element.23), channel_id=1, source_target_pairs={{0,8},{8,0},{16,24},{24,16},{1,9},{9,1},{17,25},{25,17},{2,10},{10... | collective-permute-start | bytes 61448 | tf_op jit(solution)/shard_map/ppermute | solution.py:34
  9.2 2.6 %collective-permute-start.2 = (bf16[256,128]{1,0:T(8,128)(2,1)S(1)}, bf16[256,128]{1,0:T(8,128)(2,1)S(1)}, u32[]{:S(2)}, u32[]{:S(2)}) collective-permute-start(bf16[256,128]{1,0:T(8,128)(2,1)S(1)} %get-tuple-element.24), channel_id=1, source_target_pairs={{0,4},{4,0},{1,5},{5,1},{2,6},{6,2},{3,7},{7,3},{8,12},{12,8},{9,1... | collective-permute-start | bytes 196616 | tf_op jit(solution)/shard_map/ppermute | solution.py:34
  11.7 0.0 collective-permute-done
  11.8 1.1 %collective-permute-start.1 = (f32[40,128]{1,0:T(8,128)S(1)}, f32[40,128]{1,0:T(8,128)S(1)}, u32[]{:S(2)}, u32[]{:S(2)}) collective-permute-start(f32[40,128]{1,0:T(8,128)S(1)} %get-tuple-element.43), channel_id=1, source_target_pairs={{0,4},{4,0},{1,5},{5,1},{2,6},{6,2},{3,7},{7,3},{8,12},{12,8},{9,1... | collective-permute-start | bytes 61448 | tf_op jit(solution)/shard_map/ppermute | solution.py:34
  12.9 1.2 %embed_products.1 = (bf16[3,128,384]{2,1,0:T(8,128)(2,1)S(1)}, f32[3,64,1536]{2,1,0:T(8,128)S(1)}, f32[3,64,128]{2,1,0:T(8,128)S(1)}) custom-call(bf16[3,64,3072]{2,1,0:T(8,128)(2,1)S(1)} %get-tuple-element.27.embed_ref, bf16[3,64,768]{2,1,0:T(8,128)(2,1)S(1)} %get-tuple-element.28.unembed_ref), custom_call_target="tpu_custom_call" | custom-call | flops 301989888 | bytes 1179648 | tf_op jit(solution)/shard_map/embed_products/pallas_call | solution.py:425
  14.1 1.5 %collective-permute-done.1.got_ref = f32[40,128]{1,0:T(8,128)S(1)} collective-permute-done((f32[40,128]{1,0:T(8,128)S(1)}, f32[40,128]{1,0:T(8,128)S(1)}, u32[]{:S(2)}, u32[]{:S(2)}) %collective-permute-start.1) | collective-permute-done | bytes 20512 | tf_op jit(solution)/shard_map/ppermute | solution.py:34
  15.6 0.0 collective-permute-done.2.first_ref
  15.6 0.5 %modulated_maps.1 = (f32[200,128]{1,0:T(8,128)S(1)}, bf16[32,128]{1,0:T(8,128)(2,1)S(1)}) custom-call(f32[40,128]{1,0:T(8,128)S(1)} %get-tuple-element.42.kept_ref, f32[40,128]{1,0:T(8,128)S(1)} %collective-permute-done.1.got_ref, f32[3,64,1536]{2,1,0:T(8,128)S(1)} %get-tuple-element.33.rows_ref, bf16[3,64,1536]{2,1,0:T(8,128)(2,1)S(1)} %get-tuple-element.34.through_ref, ...), custom_call_target="tpu_custom_call" | custom-call | tf_op jit(solution)/shard_map/modulated_maps/pallas_call | solution.py:529
  16.1 0.1 collective-permute-start.4
  16.2 1.3 %collective-permute-done.4 = f32[200,128]{1,0:T(8,128)S(1)} collective-permute-done((f32[200,128]{1,0:T(8,128)S(1)}, f32[200,128]{1,0:T(8,128)S(1)}, u32[]{:S(2)}, u32[]{:S(2)}) %collective-permute-start.4) | collective-permute-done | bytes 102432 | tf_op jit(solution)/shard_map/ppermute | solution.py:34
  17.5 1.6 %collective-permute-start.5 = (bf16[200,128]{1,0:T(8,128)(2,1)S(1)}, bf16[200,128]{1,0:T(8,128)(2,1)S(1)}, u32[]{:S(2)}, u32[]{:S(2)}) collective-permute-start(bf16[200,128]{1,0:T(8,128)(2,1)S(1)} %add_convert_fusion.maps_a), channel_id=1, source_target_pairs={{0,16},{4,20},{8,12},{12,8},{16,0},{20,4},{24,28},{28,24},{1,17},{... | collective-permute-start | bytes 153608 | tf_op jit(solution)/shard_map/ppermute | solution.py:51
  19.1 1.3 %collective-permute-start.7 = (bf16[200,128]{1,0:T(8,128)(2,1)S(1)}, bf16[200,128]{1,0:T(8,128)(2,1)S(1)}, u32[]{:S(2)}, u32[]{:S(2)}) collective-permute-start(bf16[200,128]{1,0:T(8,128)(2,1)S(1)} %add_convert_fusion.maps_a), channel_id=1, source_target_pairs={{0,20},{4,16},{8,28},{12,24},{16,4},{20,0},{24,12},{28,8},{1,21},{... | collective-permute-start | bytes 153608 | tf_op jit(solution)/shard_map/ppermute | solution.py:34
  20.4 1.3 %collective-permute-done.5.maps_b = bf16[200,128]{1,0:T(8,128)(2,1)S(1)} collective-permute-done((bf16[200,128]{1,0:T(8,128)(2,1)S(1)}, bf16[200,128]{1,0:T(8,128)(2,1)S(1)}, u32[]{:S(2)}, u32[]{:S(2)}) %collective-permute-start.5) | collective-permute-done | bytes 51232 | tf_op jit(solution)/shard_map/ppermute | solution.py:51
  21.7 0.0 collective-permute-start.6
  21.7 0.0 collective-permute-done.3.second_ref
  21.7 0.5 %noise_statistics.1 = (f32[512,128]{1,0:T(8,128)S(1)}, bf16[512,128]{1,0:T(8,128)(2,1)S(1)}) custom-call(f32[256,128]{1,0:T(8,128)S(1)} %get-tuple-element.22.noise_ref, bf16[256,128]{1,0:T(8,128)(2,1)S(1)} %collective-permute-done.2.first_ref, bf16[256,128]{1,0:T(8,128)(2,1)S(1)} %collective-permute-done.3.second_ref, ...), custom_call_target="tpu_custom_call" | custom-call | tf_op jit(solution)/shard_map/noise_statistics/pallas_call | solution.py:480
  22.3 1.9 %collective-permute-done.7.maps_d = bf16[200,128]{1,0:T(8,128)(2,1)S(1)} collective-permute-done((bf16[200,128]{1,0:T(8,128)(2,1)S(1)}, bf16[200,128]{1,0:T(8,128)(2,1)S(1)}, u32[]{:S(2)}, u32[]{:S(2)}) %collective-permute-start.7) | collective-permute-done | bytes 51232 | tf_op jit(solution)/shard_map/ppermute | solution.py:34
  24.2 1.3 %tokens.1 = (f32[256,128]{1,0:T(8,128)S(1)}, bf16[112,128]{1,0:T(8,128)(2,1)S(1)}) custom-call(f32[1]{0:T(128)S(6)} %div.3.level_ref, f32[256,128]{1,0:T(8,128)S(1)} %get-tuple-element.22.noise_ref, bf16[256,128]{1,0:T(8,128)(2,1)S(1)} %collective-permute-done.2.first_ref, bf16[256,128]{1,0:T(8,128)(2,1)S(1)} %collective-permute-done.3.second_ref, ...), custom_call_target="tpu_custom_call" | custom-call | tf_op jit(solution)/shard_map/tokens/pallas_call | solution.py:617
  25.5 1.6 %collective-permute-start.8 = (bf16[112,128]{1,0:T(8,128)(2,1)S(1)}, bf16[112,128]{1,0:T(8,128)(2,1)S(1)}, u32[]{:S(2)}, u32[]{:S(2)}) collective-permute-start(bf16[112,128]{1,0:T(8,128)(2,1)S(1)} %get-tuple-element.38.block_a), channel_id=1, source_target_pairs={{0,1},{1,0},{2,3},{3,2},{8,10},{9,11},{10,8},{11,9},{16,17},{17,16... | collective-permute-start | bytes 86024 | tf_op jit(solution)/shard_map/ppermute | solution.py:65
  27.1 2.5 %collective-permute-start.10 = (bf16[112,128]{1,0:T(8,128)(2,1)S(1)}, bf16[112,128]{1,0:T(8,128)(2,1)S(1)}, u32[]{:S(2)}, u32[]{:S(2)}) collective-permute-start(bf16[112,128]{1,0:T(8,128)(2,1)S(1)} %get-tuple-element.38.block_a), channel_id=1, source_target_pairs={{0,3},{1,2},{2,1},{3,0},{4,7},{5,6},{6,5},{7,4},{8,11},{9,10},{10,... | collective-permute-start | bytes 86024 | tf_op jit(solution)/shard_map/ppermute | solution.py:34
  29.6 3.2 %collective-permute-done.10.block_d = bf16[112,128]{1,0:T(8,128)(2,1)S(1)} collective-permute-done((bf16[112,128]{1,0:T(8,128)(2,1)S(1)}, bf16[112,128]{1,0:T(8,128)(2,1)S(1)}, u32[]{:S(2)}, u32[]{:S(2)}) %collective-permute-start.10) | collective-permute-done | bytes 28704 | tf_op jit(solution)/shard_map/ppermute | solution.py:34
  32.8 0.0 collective-permute-done.9.block_c
  32.8 2.8 %gradient.1 = (f32[1536,768]{1,0:T(8,128)}, f32[256,128]{1,0:T(8,128)}) custom-call(bf16[112,128]{1,0:T(8,128)(2,1)S(1)} %get-tuple-element.38.block_a, bf16[112,128]{1,0:T(8,128)(2,1)S(1)} %collective-permute-done.8.block_b, bf16[112,128]{1,0:T(8,128)(2,1)S(1)} %collective-permute-done.9.block_c, bf16[112,128]{1,0:T(8,128)(2,1)S(1)} %collective-permute-done.10.block_d, ...), custom_call_target="tpu_custom_call" | custom-call | tf_op jit(solution)/shard_map/gradient/pallas_call | solution.py:688
  (6 shorter events, 0.0 us)
Async XLA Ops:
  8.6 3.1 %collective-permute-start = (f32[40,128]{1,0:T(8,128)S(1)}, f32[40,128]{1,0:T(8,128)S(1)}, u32[]{:S(2)}, u32[]{:S(2)}) collective-permute-start(f32[40,128]{1,0:T(8,128)S(1)} %get-tuple-element.23), channel_id=1, source_target_pairs={{0,8},{8,0},{16,24},{24,16},{1,9},{9,1},{17,25},{25,17},{2,10},{10... | collective-permute-start | bytes 61448 | tf_op jit(solution)/shard_map/ppermute | solution.py:34
  9.2 6.5 %collective-permute-start.2 = (bf16[256,128]{1,0:T(8,128)(2,1)S(1)}, bf16[256,128]{1,0:T(8,128)(2,1)S(1)}, u32[]{:S(2)}, u32[]{:S(2)}) collective-permute-start(bf16[256,128]{1,0:T(8,128)(2,1)S(1)} %get-tuple-element.24), channel_id=1, source_target_pairs={{0,4},{4,0},{1,5},{5,1},{2,6},{6,2},{3,7},{7,3},{8,12},{12,8},{9,1... | collective-permute-start | bytes 196616 | tf_op jit(solution)/shard_map/ppermute | solution.py:34
  11.8 3.8 %collective-permute-start.1 = (f32[40,128]{1,0:T(8,128)S(1)}, f32[40,128]{1,0:T(8,128)S(1)}, u32[]{:S(2)}, u32[]{:S(2)}) collective-permute-start(f32[40,128]{1,0:T(8,128)S(1)} %get-tuple-element.43), channel_id=1, source_target_pairs={{0,4},{4,0},{1,5},{5,1},{2,6},{6,2},{3,7},{7,3},{8,12},{12,8},{9,1... | collective-permute-start | bytes 61448 | tf_op jit(solution)/shard_map/ppermute | solution.py:34
  16.1 1.4 %collective-permute-start.4 = (f32[200,128]{1,0:T(8,128)S(1)}, f32[200,128]{1,0:T(8,128)S(1)}, u32[]{:S(2)}, u32[]{:S(2)}) collective-permute-start(f32[200,128]{1,0:T(8,128)S(1)} %get-tuple-element.36), channel_id=1, source_target_pairs={{0,8},{8,0},{16,24},{24,16},{1,9},{9,1},{17,25},{25,17},{2,10},{10... | collective-permute-start | bytes 307208 | tf_op jit(solution)/shard_map/ppermute | solution.py:34
  17.5 4.2 %collective-permute-start.5 = (bf16[200,128]{1,0:T(8,128)(2,1)S(1)}, bf16[200,128]{1,0:T(8,128)(2,1)S(1)}, u32[]{:S(2)}, u32[]{:S(2)}) collective-permute-start(bf16[200,128]{1,0:T(8,128)(2,1)S(1)} %add_convert_fusion.maps_a), channel_id=1, source_target_pairs={{0,16},{4,20},{8,12},{12,8},{16,0},{20,4},{24,28},{28,24},{1,17},{... | collective-permute-start | bytes 153608 | tf_op jit(solution)/shard_map/ppermute | solution.py:51
  19.1 2.6 %collective-permute-start.3 = (bf16[256,128]{1,0:T(8,128)(2,1)S(1)}, bf16[256,128]{1,0:T(8,128)(2,1)S(1)}, u32[]{:S(2)}, u32[]{:S(2)}) collective-permute-start(bf16[256,128]{1,0:T(8,128)(2,1)S(1)} %collective-permute-done.2.first_ref), channel_id=1, source_target_pairs={{0,8},{8,0},{16,24},{24,16},{1,9},{9,1},{17,25},{25,17},{2,10},{10... | collective-permute-start | bytes 196616 | tf_op jit(solution)/shard_map/ppermute | solution.py:34
  19.1 5.1 %collective-permute-start.7 = (bf16[200,128]{1,0:T(8,128)(2,1)S(1)}, bf16[200,128]{1,0:T(8,128)(2,1)S(1)}, u32[]{:S(2)}, u32[]{:S(2)}) collective-permute-start(bf16[200,128]{1,0:T(8,128)(2,1)S(1)} %add_convert_fusion.maps_a), channel_id=1, source_target_pairs={{0,20},{4,16},{8,28},{12,24},{16,4},{20,0},{24,12},{28,8},{1,21},{... | collective-permute-start | bytes 153608 | tf_op jit(solution)/shard_map/ppermute | solution.py:34
  21.7 2.5 %collective-permute-start.6 = (bf16[200,128]{1,0:T(8,128)(2,1)S(1)}, bf16[200,128]{1,0:T(8,128)(2,1)S(1)}, u32[]{:S(2)}, u32[]{:S(2)}) collective-permute-start(bf16[200,128]{1,0:T(8,128)(2,1)S(1)} %collective-permute-done.5.maps_b), channel_id=1, source_target_pairs={{0,8},{8,0},{16,24},{24,16},{1,9},{9,1},{17,25},{25,17},{2,10},{10... | collective-permute-start | bytes 153608 | tf_op jit(solution)/shard_map/ppermute | solution.py:34
  25.5 4.1 %collective-permute-start.8 = (bf16[112,128]{1,0:T(8,128)(2,1)S(1)}, bf16[112,128]{1,0:T(8,128)(2,1)S(1)}, u32[]{:S(2)}, u32[]{:S(2)}) collective-permute-start(bf16[112,128]{1,0:T(8,128)(2,1)S(1)} %get-tuple-element.38.block_a), channel_id=1, source_target_pairs={{0,1},{1,0},{2,3},{3,2},{8,10},{9,11},{10,8},{11,9},{16,17},{17,16... | collective-permute-start | bytes 86024 | tf_op jit(solution)/shard_map/ppermute | solution.py:65
  27.1 5.7 %collective-permute-start.10 = (bf16[112,128]{1,0:T(8,128)(2,1)S(1)}, bf16[112,128]{1,0:T(8,128)(2,1)S(1)}, u32[]{:S(2)}, u32[]{:S(2)}) collective-permute-start(bf16[112,128]{1,0:T(8,128)(2,1)S(1)} %get-tuple-element.38.block_a), channel_id=1, source_target_pairs={{0,3},{1,2},{2,1},{3,0},{4,7},{5,6},{6,5},{7,4},{8,11},{9,10},{10,... | collective-permute-start | bytes 86024 | tf_op jit(solution)/shard_map/ppermute | solution.py:34
  29.6 3.2 %collective-permute-start.9 = (bf16[112,128]{1,0:T(8,128)(2,1)S(1)}, bf16[112,128]{1,0:T(8,128)(2,1)S(1)}, u32[]{:S(2)}, u32[]{:S(2)}) collective-permute-start(bf16[112,128]{1,0:T(8,128)(2,1)S(1)} %collective-permute-done.8.block_b), channel_id=1, source_target_pairs={{0,8},{8,0},{16,24},{24,16},{1,9},{9,1},{17,25},{25,17},{2,10},{10... | collective-permute-start | bytes 86024 | tf_op jit(solution)/shard_map/ppermute | solution.py:34

commit v8 on v7

--- a/solution.py
+++ b/solution.py
@@ -328,8 +328,9 @@
             if place == LATENTS_AFTER + 2:
                 take(place)
                 take(place + 1)
-                latents = jnp.where(lax.axis_index("mp") % 2 == 0, noise_ref[...], renoise_ref[...])
-                latents_ref[...] = latents.astype(jnp.bfloat16)
+                half = noise_ref.shape[0]
+                latents_ref[:half] = noise_ref[...].astype(jnp.bfloat16)
+                latents_ref[half:] = renoise_ref[...].astype(jnp.bfloat16)
                 place += 2
             take(place)
             place += 1
@@ -367,7 +368,7 @@
         stream_kernel,
         out_shape=[
             jax.ShapeDtypeStruct((pack_rows, PACK), jnp.float32),
-            jax.ShapeDtypeStruct(noise.shape, jnp.bfloat16),
+            jax.ShapeDtypeStruct((2 * noise.shape[0], noise.shape[1]), jnp.bfloat16),
             jax.ShapeDtypeStruct((3, CH, rows), jnp.bfloat16),
             jax.ShapeDtypeStruct(noise.shape, noise.dtype),
             jax.ShapeDtypeStruct(renoise.shape, renoise.dtype),
@@ -457,16 +458,14 @@
     return product[:, i * 2 * CH : (i + 1) * 2 * CH]
 
 
-def sample_latents(noise_ref, first_ref, second_ref):
-    first, second = first_ref[...], second_ref[...]
-    core = lax.axis_index("mp") % 2
-    other = jnp.where(core == 0, first, second)
-    other_renoise = jnp.where(core == 0, second, first)
-    return jnp.concatenate([noise_ref[...].astype(jnp.bfloat16), other], 0), other_renoise
-
-
-def noise_kernel(noise_ref, first_ref, second_ref, gram_ref, inverse_ref, normal_ref):
-    noise, _ = sample_latents(noise_ref, first_ref, second_ref)
+def sample_latents(noise_ref, other_ref):
+    half = noise_ref.shape[0]
+    noise = jnp.concatenate([noise_ref[...].astype(jnp.bfloat16), other_ref[:half]], 0)
+    return noise, other_ref[half:]
+
+
+def noise_kernel(noise_ref, other_ref, gram_ref, inverse_ref, normal_ref):
+    noise, _ = sample_latents(noise_ref, other_ref)
     product = jnp.dot(noise, gram_ref[0], preferred_element_type=jnp.float32)
     noise = noise.astype(jnp.float32)
     by_gram = columns(product, 0) + columns(product, 1) + columns(product, 2)
@@ -475,7 +474,7 @@
     normal_ref[...] = (noise * inverse).astype(jnp.bfloat16)
 
 
-def noise_statistics(noise, first, second, gram):
+def noise_statistics(noise, other, gram):
     shape = (2 * noise.shape[0], noise.shape[1])
     return pl.pallas_call(
         noise_kernel,
@@ -483,11 +482,11 @@
             jax.ShapeDtypeStruct(shape, jnp.float32),
             jax.ShapeDtypeStruct(shape, jnp.bfloat16),
         ],
-        in_specs=whole_specs(4),
+        in_specs=whole_specs(3),
         out_specs=whole_specs(2),
         compiler_params=vmem_params(),
         name="noise_statistics",
-    )(noise, first, second, gram)
+    )(noise, other, gram)
 
 
 def maps_kernel(kept_ref, got_ref, rows_ref, through_ref, direct_ref, maps_ref, mod_ref):
@@ -517,9 +516,11 @@
         product = lax.dot_general(
             left, through, CONTRACT_LAST, preferred_element_type=jnp.float32
         )
-        maps_ref[m * CH : (m + 1) * CH] = product[:CH] + direct_ref[m]
+        maps_ref[m * CH : (m + 1) * CH] = (product[:CH] + direct_ref[m]).astype(jnp.bfloat16)
         offsets.append(product[CH : CH + 1])
-    maps_ref[3 * CH :] = jnp.concatenate(offsets + [jnp.zeros((5, PACK), jnp.float32)], 0)
+    maps_ref[3 * CH :] = jnp.concatenate(
+        offsets + [jnp.zeros((5, PACK), jnp.float32)], 0
+    ).astype(jnp.bfloat16)
     rest = jnp.zeros((mod_ref.shape[0] - 2 * packs, PACK), jnp.float32)
     mod_ref[...] = jnp.concatenate([shift[:packs], scale[:packs], rest], 0).astype(jnp.bfloat16)
 
@@ -529,7 +530,7 @@
     return pl.pallas_call(
         maps_kernel,
         out_shape=[
-            jax.ShapeDtypeStruct((3 * CH + 8, 2 * CH), jnp.float32),
+            jax.ShapeDtypeStruct((3 * CH + 8, 2 * CH), jnp.bfloat16),
             jax.ShapeDtypeStruct((-(-2 * packs // 16) * 16, PACK), jnp.bfloat16),
         ],
         in_specs=whole_specs(5),
@@ -545,8 +546,7 @@
 def token_kernel(
     level_ref,
     noise_ref,
-    first_ref,
-    second_ref,
+    other_ref,
     renoise_ref,
     inverse_ref,
     normal_ref,
@@ -579,7 +579,7 @@
     def combine(product, inverse, offset):
         return columns(product, 0) + inverse * columns(product, 1) + offset
 
-    noise, other_renoise = sample_latents(noise_ref, first_ref, second_ref)
+    noise, other_renoise = sample_latents(noise_ref, other_ref)
     renoise = jnp.concatenate([renoise_ref[...], other_renoise.astype(jnp.float32)], 0)
     matrix, offset = model_matrix(0)
     product = jnp.dot(noise, matrix, preferred_element_type=jnp.float32)
@@ -613,18 +613,18 @@
     payload_ref[MAP_ROWS:] = mod_ref[...]
 
 
-def token_phase(level, noise, first, second, renoise, inverse, normal, gram, maps, mod):
+def token_phase(level, noise, other, renoise, inverse, normal, gram, maps, mod):
     return pl.pallas_call(
         token_kernel,
         out_shape=[
             jax.ShapeDtypeStruct(renoise.shape, jnp.float32),
             jax.ShapeDtypeStruct((MAP_ROWS + mod.shape[0], 2 * CH), jnp.bfloat16),
         ],
-        in_specs=[pl.BlockSpec(memory_space=pltpu.SMEM)] + whole_specs(12),
+        in_specs=[pl.BlockSpec(memory_space=pltpu.SMEM)] + whole_specs(11),
         out_specs=whole_specs(2),
         compiler_params=vmem_params(),
         name="tokens",
-    )(level, noise, first, second, renoise, inverse, normal, gram, *maps, mod)
+    )(level, noise, other, renoise, inverse, normal, gram, *maps, mod)
 
 
 GRAD_PIECES = 6
@@ -720,18 +720,19 @@
     theirs = swap(mine, "mp", 1)
     own_half = lax.axis_index("mp") % 2 == f
     kept = jnp.where(own_half, mine, theirs)
-    got = swap(jnp.where(own_half, theirs, mine), "fsdp", 1)
-    first = swap(latents, "fsdp", 1)
-    got, first = lax.optimization_barrier((got, first))
-    second = swap(first, "mp", 1)
+    sent = jnp.where(own_half, theirs, mine)
+    sent, latents = lax.optimization_barrier((sent, latents))
+    got = swap(sent, "fsdp", 1)
+    other = swap(latents, "fsdp", 1)
     gram, rows_part, direct = embed_products(embed, unembed, proj_weight.shape[1])
     maps, mod = modulated_maps(kept, got, rows_part, through, direct)
-    maps = (maps + swap(maps, "mp", 1)).astype(jnp.bfloat16)
-    inverse, normal = noise_statistics(noise, first, second, gram)
+    maps = maps.astype(jnp.float32) + swap(maps, "mp", 1).astype(jnp.float32)
+    maps = maps.astype(jnp.bfloat16)
     maps = chip_blocks(maps)
+    inverse, normal = noise_statistics(noise, other, gram)
     level = renoise_step.astype(jnp.float32) / 1000.0
     score, payload = token_phase(
-        level, noise, first, second, renoise, inverse, normal, gram, maps, mod
+        level, noise, other, renoise, inverse, normal, gram, maps, mod
     )
     blocks = gather_samples(payload)
     gen_grad, score_gap = gradient(blocks, rows_part, unembed, score)

time: 35.8 us -> 35.5 us (level)
  waiting for transfers between devices: 9.23 us -> 7.71 us
  starting transfers between devices: 11.3 us -> 12.6 us
    ppermute x9 -> x8, waiting for transfers between devices: 7.94 us -> 5.96 us  [swap(): return lax.ppermute(x, axes, [(i, i ^ mask) for i in range(count)])]
    ppermute x9 -> x8, starting transfers between devices: 8.1 us -> 9.35 us  [swap(): return lax.ppermute(x, axes, [(i, i ^ mask) for i in range(count)])]
    ppermute x1, waiting for transfers between devices: 1.28 us -> 1.75 us  [chip_blocks(): side = lax.ppermute(x, ('mp', 'fsdp'), pairs)]
  transfers between devices with their start and end apart: 11 -> 10, of which waited for: 5 -> 5; matrix products, arithmetic and copies ran while one was open for 0% -> 0% of each run, Pallas kernels for 5% -> 5%
where the time goes in v8:
time: 35.5 us; the launch traced here: 35.3 us
  Pallas kernels  13 us (37%)
  starting transfers between devices  12.6 us (35%)
  waiting for transfers between devices  7.71 us (22%)
  between operations  1.98 us (6%)
    ppermute x8, starting transfers between devices, swap(): return lax.ppermute(x, axes, [(i, i ^ mask) for i in range(count)])  9.35 us
    pallas_call x1, Pallas kernels, streamed_weights(): pl.pallas_call(stream_kernel, out_shape=[jax.ShapeDtypeStruct((pack_rows,...  6.71 us
    ppermute x8, waiting for transfers between devices, swap(): return lax.ppermute(x, axes, [(i, i ^ mask) for i in range(count)])  5.96 us
    pallas_call x1, Pallas kernels, gradient(): pl.pallas_call(grad_kernel, out_shape=[jax.ShapeDtypeStruct((rows, cols),...  2.79 us
    ppermute x1, waiting for transfers between devices, chip_blocks(): side = lax.ppermute(x, ('mp', 'fsdp'), pairs)  1.75 us
    ppermute x1, starting transfers between devices, gather_samples(): near = lax.ppermute(x, ('mp', 'dp'), pairs)  1.65 us
    ppermute x1, starting transfers between devices, chip_blocks(): side = lax.ppermute(x, ('mp', 'fsdp'), pairs)  1.55 us
    pallas_call x1, Pallas kernels, token_phase(): pl.pallas_call(token_kernel, out_shape=[jax.ShapeDtypeStruct(renoise.shap...  1.26 us
  transfers between devices with their start and end apart: 10, of which 5 were waited for; matrix products, arithmetic and copies ran while one was open for 0% of the time, Pallas kernels for 5%

profile of v8, /device:TPU:0, one launch (start us, length us, event | category | flops | bytes accessed | tf_op | source)
XLA Modules:
  0.0 35.3 jit_solution(17969659565657813202)
XLA Ops:
  1.9 6.7 %stream_weights.1 = (f32[40,128]{1,0:T(8,128)S(1)}, bf16[512,128]{1,0:T(8,128)(2,1)S(1)}, bf16[3,64,1536]{2,1,0:T(8,128)(2,1)S(1)}, f32[256,128]{1,0:T(8,128)S(1...) custom-call(s32[1]{0:T(128)S(6)} %copy.11.gen_step_ref, ...), custom_call_target="tpu_custom_call" | custom-call | tf_op jit(solution)/shard_map/stream_weights/pallas_call | solution.py:367
  8.6 0.5 %collective-permute-start = (f32[40,128]{1,0:T(8,128)S(1)}, f32[40,128]{1,0:T(8,128)S(1)}, u32[]{:S(2)}, u32[]{:S(2)}) collective-permute-start(f32[40,128]{1,0:T(8,128)S(1)} %get-tuple-element.23), channel_id=1, source_target_pairs={{0,8},{8,0},{16,24},{24,16},{1,9},{9,1},{17,25},{25,17},{2,10},{10... | collective-permute-start | bytes 61448 | tf_op jit(solution)/shard_map/ppermute | solution.py:34
  9.2 0.8 %collective-permute-done = f32[40,128]{1,0:T(8,128)S(1)} collective-permute-done((f32[40,128]{1,0:T(8,128)S(1)}, f32[40,128]{1,0:T(8,128)S(1)}, u32[]{:S(2)}, u32[]{:S(2)}) %collective-permute-start) | collective-permute-done | bytes 20512 | tf_op jit(solution)/shard_map/ppermute | solution.py:34
  10.0 2.9 %collective-permute-start.2 = (f32[40,128]{1,0:T(8,128)S(1)}, f32[40,128]{1,0:T(8,128)S(1)}, u32[]{:S(2)}, u32[]{:S(2)}) collective-permute-start(f32[40,128]{1,0:T(8,128)S(1)} %get-tuple-element.32), channel_id=1, source_target_pairs={{0,4},{4,0},{1,5},{5,1},{2,6},{6,2},{3,7},{7,3},{8,12},{12,8},{9,1... | collective-permute-start | bytes 61448 | tf_op jit(solution)/shard_map/ppermute | solution.py:34
  12.9 1.2 %embed_products.1 = (bf16[3,128,384]{2,1,0:T(8,128)(2,1)S(1)}, f32[3,64,1536]{2,1,0:T(8,128)S(1)}, f32[3,64,128]{2,1,0:T(8,128)S(1)}) custom-call(bf16[3,64,3072]{2,1,0:T(8,128)(2,1)S(1)} %get-tuple-element.27.embed_ref, bf16[3,64,768]{2,1,0:T(8,128)(2,1)S(1)} %get-tuple-element.28.unembed_ref), custom_call_target="tpu_custom_call" | custom-call | flops 301989888 | bytes 1179648 | tf_op jit(solution)/shard_map/embed_products/pallas_call | solution.py:426
  14.1 0.5 %collective-permute-done.2.got_ref = f32[40,128]{1,0:T(8,128)S(1)} collective-permute-done((f32[40,128]{1,0:T(8,128)S(1)}, f32[40,128]{1,0:T(8,128)S(1)}, u32[]{:S(2)}, u32[]{:S(2)}) %collective-permute-start.2) | collective-permute-done | bytes 20512 | tf_op jit(solution)/shard_map/ppermute | solution.py:34
  14.6 0.5 %modulated_maps.1 = (bf16[200,128]{1,0:T(8,128)(2,1)S(1)}, bf16[32,128]{1,0:T(8,128)(2,1)S(1)}) custom-call(f32[40,128]{1,0:T(8,128)S(1)} %get-tuple-element.42.kept_ref, f32[40,128]{1,0:T(8,128)S(1)} %collective-permute-done.2.got_ref, f32[3,64,1536]{2,1,0:T(8,128)S(1)} %get-tuple-element.33.rows_ref, ...), custom_call_target="tpu_custom_call" | custom-call | tf_op jit(solution)/shard_map/modulated_maps/pallas_call | solution.py:530
  15.2 0.1 collective-permute-start.3
  15.2 2.1 %collective-permute-start.1 = (bf16[512,128]{1,0:T(8,128)(2,1)S(1)}, bf16[512,128]{1,0:T(8,128)(2,1)S(1)}, u32[]{:S(2)}, u32[]{:S(2)}) collective-permute-start(bf16[512,128]{1,0:T(8,128)(2,1)S(1)} %get-tuple-element.25), channel_id=1, source_target_pairs={{0,4},{4,0},{1,5},{5,1},{2,6},{6,2},{3,7},{7,3},{8,12},{12,8},{9,1... | collective-permute-start | bytes 393224 | tf_op jit(solution)/shard_map/ppermute | solution.py:34
  17.3 0.0 collective-permute-done.3
  17.3 1.6 %collective-permute-start.4 = (bf16[200,128]{1,0:T(8,128)(2,1)S(1)}, bf16[200,128]{1,0:T(8,128)(2,1)S(1)}, u32[]{:S(2)}, u32[]{:S(2)}) collective-permute-start(bf16[200,128]{1,0:T(8,128)(2,1)S(1)} %add_convert_fusion.maps_a), channel_id=1, source_target_pairs={{0,16},{4,20},{8,12},{12,8},{16,0},{20,4},{24,28},{28,24},{1,17},{... | collective-permute-start | bytes 153608 | tf_op jit(solution)/shard_map/ppermute | solution.py:51
  18.9 1.1 %collective-permute-start.6 = (bf16[200,128]{1,0:T(8,128)(2,1)S(1)}, bf16[200,128]{1,0:T(8,128)(2,1)S(1)}, u32[]{:S(2)}, u32[]{:S(2)}) collective-permute-start(bf16[200,128]{1,0:T(8,128)(2,1)S(1)} %add_convert_fusion.maps_a), channel_id=1, source_target_pairs={{0,20},{4,16},{8,28},{12,24},{16,4},{20,0},{24,12},{28,8},{1,21},{... | collective-permute-start | bytes 153608 | tf_op jit(solution)/shard_map/ppermute | solution.py:34
  20.0 1.7 %collective-permute-done.4.maps_b = bf16[200,128]{1,0:T(8,128)(2,1)S(1)} collective-permute-done((bf16[200,128]{1,0:T(8,128)(2,1)S(1)}, bf16[200,128]{1,0:T(8,128)(2,1)S(1)}, u32[]{:S(2)}, u32[]{:S(2)}) %collective-permute-start.4) | collective-permute-done | bytes 51232 | tf_op jit(solution)/shard_map/ppermute | solution.py:51
  21.8 0.2 collective-permute-start.5
  22.0 0.0 collective-permute-done.1.other_ref
  22.0 0.5 %noise_statistics.1 = (f32[512,128]{1,0:T(8,128)S(1)}, bf16[512,128]{1,0:T(8,128)(2,1)S(1)}) custom-call(f32[256,128]{1,0:T(8,128)S(1)} %get-tuple-element.22.noise_ref, bf16[512,128]{1,0:T(8,128)(2,1)S(1)} %collective-permute-done.1.other_ref, bf16[3,128,384]{2,1,0:T(8,128)(2,1)S(1)} %get-tuple-element.29.gram_ref), custom_call_target="tpu_custom_call" | custom-call | tf_op jit(solution)/shard_map/noise_statistics/pallas_call | solution.py:479
  22.6 1.4 %collective-permute-done.6.maps_d = bf16[200,128]{1,0:T(8,128)(2,1)S(1)} collective-permute-done((bf16[200,128]{1,0:T(8,128)(2,1)S(1)}, bf16[200,128]{1,0:T(8,128)(2,1)S(1)}, u32[]{:S(2)}, u32[]{:S(2)}) %collective-permute-start.6) | collective-permute-done | bytes 51232 | tf_op jit(solution)/shard_map/ppermute | solution.py:34
  23.9 0.0 collective-permute-done.5.maps_c
  23.9 1.3 %tokens.1 = (f32[256,128]{1,0:T(8,128)S(1)}, bf16[112,128]{1,0:T(8,128)(2,1)S(1)}) custom-call(f32[1]{0:T(128)S(6)} %div.3.level_ref, f32[256,128]{1,0:T(8,128)S(1)} %get-tuple-element.22.noise_ref, bf16[512,128]{1,0:T(8,128)(2,1)S(1)} %collective-permute-done.1.other_ref, f32[256,128]{1,0:T(8,128)S(1)} %get-tuple-element.26.renoise_ref, ...), custom_call_target="tpu_custom_call" | custom-call | tf_op jit(solution)/shard_map/tokens/pallas_call | solution.py:617
  25.2 1.6 %collective-permute-start.7 = (bf16[112,128]{1,0:T(8,128)(2,1)S(1)}, bf16[112,128]{1,0:T(8,128)(2,1)S(1)}, u32[]{:S(2)}, u32[]{:S(2)}) collective-permute-start(bf16[112,128]{1,0:T(8,128)(2,1)S(1)} %get-tuple-element.38.block_a), channel_id=1, source_target_pairs={{0,1},{1,0},{2,3},{3,2},{8,10},{9,11},{10,8},{11,9},{16,17},{17,16... | collective-permute-start | bytes 86024 | tf_op jit(solution)/shard_map/ppermute | solution.py:65
  26.8 2.5 %collective-permute-start.9 = (bf16[112,128]{1,0:T(8,128)(2,1)S(1)}, bf16[112,128]{1,0:T(8,128)(2,1)S(1)}, u32[]{:S(2)}, u32[]{:S(2)}) collective-permute-start(bf16[112,128]{1,0:T(8,128)(2,1)S(1)} %get-tuple-element.38.block_a), channel_id=1, source_target_pairs={{0,3},{1,2},{2,1},{3,0},{4,7},{5,6},{6,5},{7,4},{8,11},{9,10},{10,... | collective-permute-start | bytes 86024 | tf_op jit(solution)/shard_map/ppermute | solution.py:34
  29.3 0.0 collective-permute-done.7.block_b
  29.3 3.2 %collective-permute-done.9.block_d = bf16[112,128]{1,0:T(8,128)(2,1)S(1)} collective-permute-done((bf16[112,128]{1,0:T(8,128)(2,1)S(1)}, bf16[112,128]{1,0:T(8,128)(2,1)S(1)}, u32[]{:S(2)}, u32[]{:S(2)}) %collective-permute-start.9) | collective-permute-done | bytes 28704 | tf_op jit(solution)/shard_map/ppermute | solution.py:34
  32.5 2.8 %gradient.1 = (f32[1536,768]{1,0:T(8,128)}, f32[256,128]{1,0:T(8,128)}) custom-call(bf16[112,128]{1,0:T(8,128)(2,1)S(1)} %get-tuple-element.38.block_a, bf16[112,128]{1,0:T(8,128)(2,1)S(1)} %collective-permute-done.7.block_b, bf16[112,128]{1,0:T(8,128)(2,1)S(1)} %collective-permute-done.8.block_c, bf16[112,128]{1,0:T(8,128)(2,1)S(1)} %collective-permute-done.9.block_d, ...), custom_call_target="tpu_custom_call" | custom-call | tf_op jit(solution)/shard_map/gradient/pallas_call | solution.py:688
  (4 shorter events, 0.0 us)
Async XLA Ops:
  8.6 1.4 %collective-permute-start = (f32[40,128]{1,0:T(8,128)S(1)}, f32[40,128]{1,0:T(8,128)S(1)}, u32[]{:S(2)}, u32[]{:S(2)}) collective-permute-start(f32[40,128]{1,0:T(8,128)S(1)} %get-tuple-element.23), channel_id=1, source_target_pairs={{0,8},{8,0},{16,24},{24,16},{1,9},{9,1},{17,25},{25,17},{2,10},{10... | collective-permute-start | bytes 61448 | tf_op jit(solution)/shard_map/ppermute | solution.py:34
  10.0 4.6 %collective-permute-start.2 = (f32[40,128]{1,0:T(8,128)S(1)}, f32[40,128]{1,0:T(8,128)S(1)}, u32[]{:S(2)}, u32[]{:S(2)}) collective-permute-start(f32[40,128]{1,0:T(8,128)S(1)} %get-tuple-element.32), channel_id=1, source_target_pairs={{0,4},{4,0},{1,5},{5,1},{2,6},{6,2},{3,7},{7,3},{8,12},{12,8},{9,1... | collective-permute-start | bytes 61448 | tf_op jit(solution)/shard_map/ppermute | solution.py:34
  15.2 2.2 %collective-permute-start.3 = (bf16[200,128]{1,0:T(8,128)(2,1)S(1)}, bf16[200,128]{1,0:T(8,128)(2,1)S(1)}, u32[]{:S(2)}, u32[]{:S(2)}) collective-permute-start(bf16[200,128]{1,0:T(8,128)(2,1)S(1)} %get-tuple-element.36), channel_id=1, source_target_pairs={{0,8},{8,0},{16,24},{24,16},{1,9},{9,1},{17,25},{25,17},{2,10},{10... | collective-permute-start | bytes 153608 | tf_op jit(solution)/shard_map/ppermute | solution.py:34
  15.2 6.8 %collective-permute-start.1 = (bf16[512,128]{1,0:T(8,128)(2,1)S(1)}, bf16[512,128]{1,0:T(8,128)(2,1)S(1)}, u32[]{:S(2)}, u32[]{:S(2)}) collective-permute-start(bf16[512,128]{1,0:T(8,128)(2,1)S(1)} %get-tuple-element.25), channel_id=1, source_target_pairs={{0,4},{4,0},{1,5},{5,1},{2,6},{6,2},{3,7},{7,3},{8,12},{12,8},{9,1... | collective-permute-start | bytes 393224 | tf_op jit(solution)/shard_map/ppermute | solution.py:34
  17.3 4.4 %collective-permute-start.4 = (bf16[200,128]{1,0:T(8,128)(2,1)S(1)}, bf16[200,128]{1,0:T(8,128)(2,1)S(1)}, u32[]{:S(2)}, u32[]{:S(2)}) collective-permute-start(bf16[200,128]{1,0:T(8,128)(2,1)S(1)} %add_convert_fusion.maps_a), channel_id=1, source_target_pairs={{0,16},{4,20},{8,12},{12,8},{16,0},{20,4},{24,28},{28,24},{1,17},{... | collective-permute-start | bytes 153608 | tf_op jit(solution)/shard_map/ppermute | solution.py:51
  18.9 5.0 %collective-permute-start.6 = (bf16[200,128]{1,0:T(8,128)(2,1)S(1)}, bf16[200,128]{1,0:T(8,128)(2,1)S(1)}, u32[]{:S(2)}, u32[]{:S(2)}) collective-permute-start(bf16[200,128]{1,0:T(8,128)(2,1)S(1)} %add_convert_fusion.maps_a), channel_id=1, source_target_pairs={{0,20},{4,16},{8,28},{12,24},{16,4},{20,0},{24,12},{28,8},{1,21},{... | collective-permute-start | bytes 153608 | tf_op jit(solution)/shard_map/ppermute | solution.py:34
  21.8 2.1 %collective-permute-start.5 = (bf16[200,128]{1,0:T(8,128)(2,1)S(1)}, bf16[200,128]{1,0:T(8,128)(2,1)S(1)}, u32[]{:S(2)}, u32[]{:S(2)}) collective-permute-start(bf16[200,128]{1,0:T(8,128)(2,1)S(1)} %collective-permute-done.4.maps_b), channel_id=1, source_target_pairs={{0,8},{8,0},{16,24},{24,16},{1,9},{9,1},{17,25},{25,17},{2,10},{10... | collective-permute-start | bytes 153608 | tf_op jit(solution)/shard_map/ppermute | solution.py:34
  25.2 4.1 %collective-permute-start.7 = (bf16[112,128]{1,0:T(8,128)(2,1)S(1)}, bf16[112,128]{1,0:T(8,128)(2,1)S(1)}, u32[]{:S(2)}, u32[]{:S(2)}) collective-permute-start(bf16[112,128]{1,0:T(8,128)(2,1)S(1)} %get-tuple-element.38.block_a), channel_id=1, source_target_pairs={{0,1},{1,0},{2,3},{3,2},{8,10},{9,11},{10,8},{11,9},{16,17},{17,16... | collective-permute-start | bytes 86024 | tf_op jit(solution)/shard_map/ppermute | solution.py:65
  26.8 5.7 %collective-permute-start.9 = (bf16[112,128]{1,0:T(8,128)(2,1)S(1)}, bf16[112,128]{1,0:T(8,128)(2,1)S(1)}, u32[]{:S(2)}, u32[]{:S(2)}) collective-permute-start(bf16[112,128]{1,0:T(8,128)(2,1)S(1)} %get-tuple-element.38.block_a), channel_id=1, source_target_pairs={{0,3},{1,2},{2,1},{3,0},{4,7},{5,6},{6,5},{7,4},{8,11},{9,10},{10,... | collective-permute-start | bytes 86024 | tf_op jit(solution)/shard_map/ppermute | solution.py:34
  29.3 3.2 %collective-permute-start.8 = (bf16[112,128]{1,0:T(8,128)(2,1)S(1)}, bf16[112,128]{1,0:T(8,128)(2,1)S(1)}, u32[]{:S(2)}, u32[]{:S(2)}) collective-permute-start(bf16[112,128]{1,0:T(8,128)(2,1)S(1)} %collective-permute-done.7.block_b), channel_id=1, source_target_pairs={{0,8},{8,0},{16,24},{24,16},{1,9},{9,1},{17,25},{25,17},{2,10},{10... | collective-permute-start | bytes 86024 | tf_op jit(solution)/shard_map/ppermute | solution.py:34

commit v9 on v8

--- a/solution.py
+++ b/solution.py
@@ -720,9 +720,10 @@
     theirs = swap(mine, "mp", 1)
     own_half = lax.axis_index("mp") % 2 == f
     kept = jnp.where(own_half, mine, theirs)
-    sent = jnp.where(own_half, theirs, mine)
-    sent, latents = lax.optimization_barrier((sent, latents))
-    got = swap(sent, "fsdp", 1)
+    straight = swap(mine, "fsdp", 1)
+    cross = swap(mine, ("mp", "fsdp"), 3)
+    got = jnp.where(own_half, straight, cross)
+    got, latents = lax.optimization_barrier((got, latents))
     other = swap(latents, "fsdp", 1)
     gram, rows_part, direct = embed_products(embed, unembed, proj_weight.shape[1])
     maps, mod = modulated_maps(kept, got, rows_part, through, direct)

time: 35.5 us -> 35.9 us (1.011)
  waiting for transfers between devices: 7.71 us -> 9.2 us
  starting transfers between devices: 12.6 us -> 11.4 us
    ppermute x8 -> x9, waiting for transfers between devices: 5.96 us -> 7.16 us  [swap(): return lax.ppermute(x, axes, [(i, i ^ mask) for i in range(count)])]
    ppermute x8 -> x9, starting transfers between devices: 9.35 us -> 8.24 us  [swap(): return lax.ppermute(x, axes, [(i, i ^ mask) for i in range(count)])]
  transfers between devices with their start and end apart: 10 -> 11, of which waited for: 5 -> 7; matrix products, arithmetic and copies ran while one was open for 0% -> 0% of each run, Pallas kernels for 5% -> 5%
where the time goes in v9:
time: 35.9 us; the launch traced here: 35.7 us
  Pallas kernels  13 us (36%)
  starting transfers between devices  11.4 us (32%)
  waiting for transfers between devices  9.2 us (26%)
  between operations  1.99 us (6%)
    ppermute x9, starting transfers between devices, swap(): return lax.ppermute(x, axes, [(i, i ^ mask) for i in range(count)])  8.24 us
    ppermute x9, waiting for transfers between devices, swap(): return lax.ppermute(x, axes, [(i, i ^ mask) for i in range(count)])  7.16 us
    pallas_call x1, Pallas kernels, streamed_weights(): pl.pallas_call(stream_kernel, out_shape=[jax.ShapeDtypeStruct((pack_rows,...  6.71 us
    pallas_call x1, Pallas kernels, gradient(): pl.pallas_call(grad_kernel, out_shape=[jax.ShapeDtypeStruct((rows, cols),...  2.79 us
    ppermute x1, waiting for transfers between devices, chip_blocks(): side = lax.ppermute(x, ('mp', 'fsdp'), pairs)  2.04 us
    ppermute x1, starting transfers between devices, gather_samples(): near = lax.ppermute(x, ('mp', 'dp'), pairs)  1.65 us
    ppermute x1, starting transfers between devices, chip_blocks(): side = lax.ppermute(x, ('mp', 'fsdp'), pairs)  1.55 us
    pallas_call x1, Pallas kernels, token_phase(): pl.pallas_call(token_kernel, out_shape=[jax.ShapeDtypeStruct(renoise.shap...  1.25 us
  transfers between devices with their start and end apart: 11, of which 7 were waited for; matrix products, arithmetic and copies ran while one was open for 0% of the time, Pallas kernels for 5%

profile of v9, /device:TPU:0, one launch (start us, length us, event | category | flops | bytes accessed | tf_op | source)
XLA Modules:
  0.0 35.7 jit_solution(10144269871727637770)
XLA Ops:
  1.9 6.7 %stream_weights.1 = (f32[40,128]{1,0:T(8,128)S(1)}, bf16[512,128]{1,0:T(8,128)(2,1)S(1)}, bf16[3,64,1536]{2,1,0:T(8,128)(2,1)S(1)}, f32[256,128]{1,0:T(8,128)S(1...) custom-call(s32[1]{0:T(128)S(6)} %copy.11.gen_step_ref, ...), custom_call_target="tpu_custom_call" | custom-call | tf_op jit(solution)/shard_map/stream_weights/pallas_call | solution.py:367
  8.6 0.5 %collective-permute-start.3 = (f32[40,128]{1,0:T(8,128)S(1)}, f32[40,128]{1,0:T(8,128)S(1)}, u32[]{:S(2)}, u32[]{:S(2)}) collective-permute-start(f32[40,128]{1,0:T(8,128)S(1)} %get-tuple-element.23), channel_id=1, source_target_pairs={{0,8},{8,0},{16,24},{24,16},{1,9},{9,1},{17,25},{25,17},{2,10},{10... | collective-permute-start | bytes 61448 | tf_op jit(solution)/shard_map/ppermute | solution.py:34
  9.2 2.6 %collective-permute-start.1 = (f32[40,128]{1,0:T(8,128)S(1)}, f32[40,128]{1,0:T(8,128)S(1)}, u32[]{:S(2)}, u32[]{:S(2)}) collective-permute-start(f32[40,128]{1,0:T(8,128)S(1)} %get-tuple-element.23), channel_id=1, source_target_pairs={{0,12},{4,8},{8,4},{12,0},{16,28},{20,24},{24,20},{28,16},{1,13},{... | collective-permute-start | bytes 61448 | tf_op jit(solution)/shard_map/ppermute | solution.py:34
  11.8 0.0 collective-permute-start
  11.8 1.2 %embed_products.1 = (bf16[3,128,384]{2,1,0:T(8,128)(2,1)S(1)}, f32[3,64,1536]{2,1,0:T(8,128)S(1)}, f32[3,64,128]{2,1,0:T(8,128)S(1)}) custom-call(bf16[3,64,3072]{2,1,0:T(8,128)(2,1)S(1)} %get-tuple-element.27.embed_ref, bf16[3,64,768]{2,1,0:T(8,128)(2,1)S(1)} %get-tuple-element.28.unembed_ref), custom_call_target="tpu_custom_call" | custom-call | flops 301989888 | bytes 1179648 | tf_op jit(solution)/shard_map/embed_products/pallas_call | solution.py:426
  13.1 0.2 collective-permute-done.1
  13.3 2.3 %collective-permute-done = f32[40,128]{1,0:T(8,128)S(1)} collective-permute-done((f32[40,128]{1,0:T(8,128)S(1)}, f32[40,128]{1,0:T(8,128)S(1)}, u32[]{:S(2)}, u32[]{:S(2)}) %collective-permute-start) | collective-permute-done | bytes 20512 | tf_op jit(solution)/shard_map/ppermute | solution.py:34
  15.6 0.0 collective-permute-done.3
  15.6 0.5 %modulated_maps.1 = (bf16[200,128]{1,0:T(8,128)(2,1)S(1)}, bf16[32,128]{1,0:T(8,128)(2,1)S(1)}) custom-call(f32[40,128]{1,0:T(8,128)S(1)} %broadcast_select_fusion.kept_ref, f32[40,128]{1,0:T(8,128)S(1)} %broadcast_select_fusion.1.got_ref, f32[3,64,1536]{2,1,0:T(8,128)S(1)} %get-tuple-element.33.rows_ref, ...), custom_call_target="tpu_custom_call" | custom-call | tf_op jit(solution)/shard_map/modulated_maps/pallas_call | solution.py:530
  16.1 0.1 collective-permute-start.4
  16.2 0.3 collective-permute-start.2
  16.5 0.9 %collective-permute-done.4 = bf16[200,128]{1,0:T(8,128)(2,1)S(1)} collective-permute-done((bf16[200,128]{1,0:T(8,128)(2,1)S(1)}, bf16[200,128]{1,0:T(8,128)(2,1)S(1)}, u32[]{:S(2)}, u32[]{:S(2)}) %collective-permute-start.4) | collective-permute-done | bytes 51232 | tf_op jit(solution)/shard_map/ppermute | solution.py:34
  17.5 1.6 %collective-permute-start.5 = (bf16[200,128]{1,0:T(8,128)(2,1)S(1)}, bf16[200,128]{1,0:T(8,128)(2,1)S(1)}, u32[]{:S(2)}, u32[]{:S(2)}) collective-permute-start(bf16[200,128]{1,0:T(8,128)(2,1)S(1)} %add_convert_fusion.maps_a), channel_id=1, source_target_pairs={{0,16},{4,20},{8,12},{12,8},{16,0},{20,4},{24,28},{28,24},{1,17},{... | collective-permute-start | bytes 153608 | tf_op jit(solution)/shard_map/ppermute | solution.py:51
  19.0 0.8 %collective-permute-start.7 = (bf16[200,128]{1,0:T(8,128)(2,1)S(1)}, bf16[200,128]{1,0:T(8,128)(2,1)S(1)}, u32[]{:S(2)}, u32[]{:S(2)}) collective-permute-start(bf16[200,128]{1,0:T(8,128)(2,1)S(1)} %add_convert_fusion.maps_a), channel_id=1, source_target_pairs={{0,20},{4,16},{8,28},{12,24},{16,4},{20,0},{24,12},{28,8},{1,21},{... | collective-permute-start | bytes 153608 | tf_op jit(solution)/shard_map/ppermute | solution.py:34
  19.9 2.0 %collective-permute-done.5.maps_b = bf16[200,128]{1,0:T(8,128)(2,1)S(1)} collective-permute-done((bf16[200,128]{1,0:T(8,128)(2,1)S(1)}, bf16[200,128]{1,0:T(8,128)(2,1)S(1)}, u32[]{:S(2)}, u32[]{:S(2)}) %collective-permute-start.5) | collective-permute-done | bytes 51232 | tf_op jit(solution)/shard_map/ppermute | solution.py:51
  21.9 1.3 %collective-permute-start.6 = (bf16[200,128]{1,0:T(8,128)(2,1)S(1)}, bf16[200,128]{1,0:T(8,128)(2,1)S(1)}, u32[]{:S(2)}, u32[]{:S(2)}) collective-permute-start(bf16[200,128]{1,0:T(8,128)(2,1)S(1)} %collective-permute-done.5.maps_b), channel_id=1, source_target_pairs={{0,8},{8,0},{16,24},{24,16},{1,9},{9,1},{17,25},{25,17},{2,10},{10... | collective-permute-start | bytes 153608 | tf_op jit(solution)/shard_map/ppermute | solution.py:34
  23.2 0.5 %noise_statistics.1 = (f32[512,128]{1,0:T(8,128)S(1)}, bf16[512,128]{1,0:T(8,128)(2,1)S(1)}) custom-call(f32[256,128]{1,0:T(8,128)S(1)} %get-tuple-element.22.noise_ref, bf16[512,128]{1,0:T(8,128)(2,1)S(1)} %collective-permute-done.2.other_ref, bf16[3,128,384]{2,1,0:T(8,128)(2,1)S(1)} %get-tuple-element.29.gram_ref), custom_call_target="tpu_custom_call" | custom-call | tf_op jit(solution)/shard_map/noise_statistics/pallas_call | solution.py:479
  23.8 0.2 collective-permute-done.7.maps_d
  24.0 0.1 collective-permute-done.6.maps_c
  24.1 1.2 %tokens.1 = (f32[256,128]{1,0:T(8,128)S(1)}, bf16[112,128]{1,0:T(8,128)(2,1)S(1)}) custom-call(f32[1]{0:T(128)S(6)} %div.3.level_ref, f32[256,128]{1,0:T(8,128)S(1)} %get-tuple-element.22.noise_ref, bf16[512,128]{1,0:T(8,128)(2,1)S(1)} %collective-permute-done.2.other_ref, f32[256,128]{1,0:T(8,128)S(1)} %get-tuple-element.26.renoise_ref, ...), custom_call_target="tpu_custom_call" | custom-call | tf_op jit(solution)/shard_map/tokens/pallas_call | solution.py:617
  25.4 1.6 %collective-permute-start.8 = (bf16[112,128]{1,0:T(8,128)(2,1)S(1)}, bf16[112,128]{1,0:T(8,128)(2,1)S(1)}, u32[]{:S(2)}, u32[]{:S(2)}) collective-permute-start(bf16[112,128]{1,0:T(8,128)(2,1)S(1)} %get-tuple-element.38.block_a), channel_id=1, source_target_pairs={{0,1},{1,0},{2,3},{3,2},{8,10},{9,11},{10,8},{11,9},{16,17},{17,16... | collective-permute-start | bytes 86024 | tf_op jit(solution)/shard_map/ppermute | solution.py:65
  27.0 2.5 %collective-permute-start.10 = (bf16[112,128]{1,0:T(8,128)(2,1)S(1)}, bf16[112,128]{1,0:T(8,128)(2,1)S(1)}, u32[]{:S(2)}, u32[]{:S(2)}) collective-permute-start(bf16[112,128]{1,0:T(8,128)(2,1)S(1)} %get-tuple-element.38.block_a), channel_id=1, source_target_pairs={{0,3},{1,2},{2,1},{3,0},{4,7},{5,6},{6,5},{7,4},{8,11},{9,10},{10,... | collective-permute-start | bytes 86024 | tf_op jit(solution)/shard_map/ppermute | solution.py:34
  29.5 3.4 %collective-permute-done.10.block_d = bf16[112,128]{1,0:T(8,128)(2,1)S(1)} collective-permute-done((bf16[112,128]{1,0:T(8,128)(2,1)S(1)}, bf16[112,128]{1,0:T(8,128)(2,1)S(1)}, u32[]{:S(2)}, u32[]{:S(2)}) %collective-permute-start.10) | collective-permute-done | bytes 28704 | tf_op jit(solution)/shard_map/ppermute | solution.py:34
  32.9 2.8 %gradient.1 = (f32[1536,768]{1,0:T(8,128)}, f32[256,128]{1,0:T(8,128)}) custom-call(bf16[112,128]{1,0:T(8,128)(2,1)S(1)} %get-tuple-element.38.block_a, bf16[112,128]{1,0:T(8,128)(2,1)S(1)} %collective-permute-done.8.block_b, bf16[112,128]{1,0:T(8,128)(2,1)S(1)} %collective-permute-done.9.block_c, bf16[112,128]{1,0:T(8,128)(2,1)S(1)} %collective-permute-done.10.block_d, ...), custom_call_target="tpu_custom_call" | custom-call | tf_op jit(solution)/shard_map/gradient/pallas_call | solution.py:688
  (7 shorter events, 0.0 us)
Async XLA Ops:
  8.6 7.0 %collective-permute-start.3 = (f32[40,128]{1,0:T(8,128)S(1)}, f32[40,128]{1,0:T(8,128)S(1)}, u32[]{:S(2)}, u32[]{:S(2)}) collective-permute-start(f32[40,128]{1,0:T(8,128)S(1)} %get-tuple-element.23), channel_id=1, source_target_pairs={{0,8},{8,0},{16,24},{24,16},{1,9},{9,1},{17,25},{25,17},{2,10},{10... | collective-permute-start | bytes 61448 | tf_op jit(solution)/shard_map/ppermute | solution.py:34
  9.2 4.1 %collective-permute-start.1 = (f32[40,128]{1,0:T(8,128)S(1)}, f32[40,128]{1,0:T(8,128)S(1)}, u32[]{:S(2)}, u32[]{:S(2)}) collective-permute-start(f32[40,128]{1,0:T(8,128)S(1)} %get-tuple-element.23), channel_id=1, source_target_pairs={{0,12},{4,8},{8,4},{12,0},{16,28},{20,24},{24,20},{28,16},{1,13},{... | collective-permute-start | bytes 61448 | tf_op jit(solution)/shard_map/ppermute | solution.py:34
  11.8 3.8 %collective-permute-start = (f32[40,128]{1,0:T(8,128)S(1)}, f32[40,128]{1,0:T(8,128)S(1)}, u32[]{:S(2)}, u32[]{:S(2)}) collective-permute-start(f32[40,128]{1,0:T(8,128)S(1)} %get-tuple-element.23), channel_id=1, source_target_pairs={{0,4},{4,0},{1,5},{5,1},{2,6},{6,2},{3,7},{7,3},{8,12},{12,8},{9,1... | collective-permute-start | bytes 61448 | tf_op jit(solution)/shard_map/ppermute | solution.py:34
  16.1 1.3 %collective-permute-start.4 = (bf16[200,128]{1,0:T(8,128)(2,1)S(1)}, bf16[200,128]{1,0:T(8,128)(2,1)S(1)}, u32[]{:S(2)}, u32[]{:S(2)}) collective-permute-start(bf16[200,128]{1,0:T(8,128)(2,1)S(1)} %get-tuple-element.36), channel_id=1, source_target_pairs={{0,8},{8,0},{16,24},{24,16},{1,9},{9,1},{17,25},{25,17},{2,10},{10... | collective-permute-start | bytes 153608 | tf_op jit(solution)/shard_map/ppermute | solution.py:34
  16.2 7.0 %collective-permute-start.2 = (bf16[512,128]{1,0:T(8,128)(2,1)S(1)}, bf16[512,128]{1,0:T(8,128)(2,1)S(1)}, u32[]{:S(2)}, u32[]{:S(2)}) collective-permute-start(bf16[512,128]{1,0:T(8,128)(2,1)S(1)} %get-tuple-element.25), channel_id=1, source_target_pairs={{0,4},{4,0},{1,5},{5,1},{2,6},{6,2},{3,7},{7,3},{8,12},{12,8},{9,1... | collective-permute-start | bytes 393224 | tf_op jit(solution)/shard_map/ppermute | solution.py:34
  17.5 4.4 %collective-permute-start.5 = (bf16[200,128]{1,0:T(8,128)(2,1)S(1)}, bf16[200,128]{1,0:T(8,128)(2,1)S(1)}, u32[]{:S(2)}, u32[]{:S(2)}) collective-permute-start(bf16[200,128]{1,0:T(8,128)(2,1)S(1)} %add_convert_fusion.maps_a), channel_id=1, source_target_pairs={{0,16},{4,20},{8,12},{12,8},{16,0},{20,4},{24,28},{28,24},{1,17},{... | collective-permute-start | bytes 153608 | tf_op jit(solution)/shard_map/ppermute | solution.py:51
  19.0 5.0 %collective-permute-start.7 = (bf16[200,128]{1,0:T(8,128)(2,1)S(1)}, bf16[200,128]{1,0:T(8,128)(2,1)S(1)}, u32[]{:S(2)}, u32[]{:S(2)}) collective-permute-start(bf16[200,128]{1,0:T(8,128)(2,1)S(1)} %add_convert_fusion.maps_a), channel_id=1, source_target_pairs={{0,20},{4,16},{8,28},{12,24},{16,4},{20,0},{24,12},{28,8},{1,21},{... | collective-permute-start | bytes 153608 | tf_op jit(solution)/shard_map/ppermute | solution.py:34
  21.9 2.2 %collective-permute-start.6 = (bf16[200,128]{1,0:T(8,128)(2,1)S(1)}, bf16[200,128]{1,0:T(8,128)(2,1)S(1)}, u32[]{:S(2)}, u32[]{:S(2)}) collective-permute-start(bf16[200,128]{1,0:T(8,128)(2,1)S(1)} %collective-permute-done.5.maps_b), channel_id=1, source_target_pairs={{0,8},{8,0},{16,24},{24,16},{1,9},{9,1},{17,25},{25,17},{2,10},{10... | collective-permute-start | bytes 153608 | tf_op jit(solution)/shard_map/ppermute | solution.py:34
  25.4 4.1 %collective-permute-start.8 = (bf16[112,128]{1,0:T(8,128)(2,1)S(1)}, bf16[112,128]{1,0:T(8,128)(2,1)S(1)}, u32[]{:S(2)}, u32[]{:S(2)}) collective-permute-start(bf16[112,128]{1,0:T(8,128)(2,1)S(1)} %get-tuple-element.38.block_a), channel_id=1, source_target_pairs={{0,1},{1,0},{2,3},{3,2},{8,10},{9,11},{10,8},{11,9},{16,17},{17,16... | collective-permute-start | bytes 86024 | tf_op jit(solution)/shard_map/ppermute | solution.py:65
  27.0 5.9 %collective-permute-start.10 = (bf16[112,128]{1,0:T(8,128)(2,1)S(1)}, bf16[112,128]{1,0:T(8,128)(2,1)S(1)}, u32[]{:S(2)}, u32[]{:S(2)}) collective-permute-start(bf16[112,128]{1,0:T(8,128)(2,1)S(1)} %get-tuple-element.38.block_a), channel_id=1, source_target_pairs={{0,3},{1,2},{2,1},{3,0},{4,7},{5,6},{6,5},{7,4},{8,11},{9,10},{10,... | collective-permute-start | bytes 86024 | tf_op jit(solution)/shard_map/ppermute | solution.py:34
  29.5 3.4 %collective-permute-start.9 = (bf16[112,128]{1,0:T(8,128)(2,1)S(1)}, bf16[112,128]{1,0:T(8,128)(2,1)S(1)}, u32[]{:S(2)}, u32[]{:S(2)}) collective-permute-start(bf16[112,128]{1,0:T(8,128)(2,1)S(1)} %collective-permute-done.8.block_b), channel_id=1, source_target_pairs={{0,8},{8,0},{16,24},{24,16},{1,9},{9,1},{17,25},{25,17},{2,10},{10... | collective-permute-start | bytes 86024 | tf_op jit(solution)/shard_map/ppermute | solution.py:34

commit v10 on v8

--- a/solution.py
+++ b/solution.py
@@ -234,7 +234,7 @@
 MOD_PIECES = 4
 PROJ_PIECES = 3
 IN_FLIGHT = 12
-LATENTS_AFTER = 8
+LATENTS_AFTER = 4
 PACK = 128
 CONTRACT_LAST = (((1,), (1,)), ((), ()))
 CONTRACT_FIRST = (((0,), (0,)), ((), ()))

time: 35.5 us -> 35.5 us (level)
  no operation moved by 1% of the time
where the time goes in v10:
time: 35.5 us; the launch traced here: 35.3 us
  Pallas kernels  13 us (37%)
  starting transfers between devices  12.6 us (35%)
  waiting for transfers between devices  7.71 us (22%)
  between operations  1.98 us (6%)
    ppermute x8, starting transfers between devices, swap(): return lax.ppermute(x, axes, [(i, i ^ mask) for i in range(count)])  9.35 us
    pallas_call x1, Pallas kernels, streamed_weights(): pl.pallas_call(stream_kernel, out_shape=[jax.ShapeDtypeStruct((pack_rows,...  6.71 us
    ppermute x8, waiting for transfers between devices, swap(): return lax.ppermute(x, axes, [(i, i ^ mask) for i in range(count)])  5.96 us
    pallas_call x1, Pallas kernels, gradient(): pl.pallas_call(grad_kernel, out_shape=[jax.ShapeDtypeStruct((rows, cols),...  2.79 us
    ppermute x1, waiting for transfers between devices, chip_blocks(): side = lax.ppermute(x, ('mp', 'fsdp'), pairs)  1.75 us
    ppermute x1, starting transfers between devices, gather_samples(): near = lax.ppermute(x, ('mp', 'dp'), pairs)  1.65 us
    ppermute x1, starting transfers between devices, chip_blocks(): side = lax.ppermute(x, ('mp', 'fsdp'), pairs)  1.55 us
    pallas_call x1, Pallas kernels, token_phase(): pl.pallas_call(token_kernel, out_shape=[jax.ShapeDtypeStruct(renoise.shap...  1.26 us
  transfers between devices with their start and end apart: 10, of which 5 were waited for; matrix products, arithmetic and copies ran while one was open for 0% of the time, Pallas kernels for 5%

profile of v10, /device:TPU:0, one launch (start us, length us, event | category | flops | bytes accessed | tf_op | source)
XLA Modules:
  0.0 35.3 jit_solution(3935650569788328784)
XLA Ops:
  1.9 6.7 %stream_weights.1 = (f32[40,128]{1,0:T(8,128)S(1)}, bf16[512,128]{1,0:T(8,128)(2,1)S(1)}, bf16[3,64,1536]{2,1,0:T(8,128)(2,1)S(1)}, f32[256,128]{1,0:T(8,128)S(1...) custom-call(s32[1]{0:T(128)S(6)} %copy.11.gen_step_ref, ...), custom_call_target="tpu_custom_call" | custom-call | tf_op jit(solution)/shard_map/stream_weights/pallas_call | solution.py:367
  8.6 0.5 %collective-permute-start = (f32[40,128]{1,0:T(8,128)S(1)}, f32[40,128]{1,0:T(8,128)S(1)}, u32[]{:S(2)}, u32[]{:S(2)}) collective-permute-start(f32[40,128]{1,0:T(8,128)S(1)} %get-tuple-element.23), channel_id=1, source_target_pairs={{0,8},{8,0},{16,24},{24,16},{1,9},{9,1},{17,25},{25,17},{2,10},{10... | collective-permute-start | bytes 61448 | tf_op jit(solution)/shard_map/ppermute | solution.py:34
  9.2 0.8 %collective-permute-done = f32[40,128]{1,0:T(8,128)S(1)} collective-permute-done((f32[40,128]{1,0:T(8,128)S(1)}, f32[40,128]{1,0:T(8,128)S(1)}, u32[]{:S(2)}, u32[]{:S(2)}) %collective-permute-start) | collective-permute-done | bytes 20512 | tf_op jit(solution)/shard_map/ppermute | solution.py:34
  10.0 2.9 %collective-permute-start.2 = (f32[40,128]{1,0:T(8,128)S(1)}, f32[40,128]{1,0:T(8,128)S(1)}, u32[]{:S(2)}, u32[]{:S(2)}) collective-permute-start(f32[40,128]{1,0:T(8,128)S(1)} %get-tuple-element.32), channel_id=1, source_target_pairs={{0,4},{4,0},{1,5},{5,1},{2,6},{6,2},{3,7},{7,3},{8,12},{12,8},{9,1... | collective-permute-start | bytes 61448 | tf_op jit(solution)/shard_map/ppermute | solution.py:34
  12.9 1.2 %embed_products.1 = (bf16[3,128,384]{2,1,0:T(8,128)(2,1)S(1)}, f32[3,64,1536]{2,1,0:T(8,128)S(1)}, f32[3,64,128]{2,1,0:T(8,128)S(1)}) custom-call(bf16[3,64,3072]{2,1,0:T(8,128)(2,1)S(1)} %get-tuple-element.27.embed_ref, bf16[3,64,768]{2,1,0:T(8,128)(2,1)S(1)} %get-tuple-element.28.unembed_ref), custom_call_target="tpu_custom_call" | custom-call | flops 301989888 | bytes 1179648 | tf_op jit(solution)/shard_map/embed_products/pallas_call | solution.py:426
  14.1 0.5 %collective-permute-done.2.got_ref = f32[40,128]{1,0:T(8,128)S(1)} collective-permute-done((f32[40,128]{1,0:T(8,128)S(1)}, f32[40,128]{1,0:T(8,128)S(1)}, u32[]{:S(2)}, u32[]{:S(2)}) %collective-permute-start.2) | collective-permute-done | bytes 20512 | tf_op jit(solution)/shard_map/ppermute | solution.py:34
  14.6 0.5 %modulated_maps.1 = (bf16[200,128]{1,0:T(8,128)(2,1)S(1)}, bf16[32,128]{1,0:T(8,128)(2,1)S(1)}) custom-call(f32[40,128]{1,0:T(8,128)S(1)} %get-tuple-element.42.kept_ref, f32[40,128]{1,0:T(8,128)S(1)} %collective-permute-done.2.got_ref, f32[3,64,1536]{2,1,0:T(8,128)S(1)} %get-tuple-element.33.rows_ref, ...), custom_call_target="tpu_custom_call" | custom-call | tf_op jit(solution)/shard_map/modulated_maps/pallas_call | solution.py:530
  15.2 0.1 collective-permute-start.3
  15.2 2.1 %collective-permute-start.1 = (bf16[512,128]{1,0:T(8,128)(2,1)S(1)}, bf16[512,128]{1,0:T(8,128)(2,1)S(1)}, u32[]{:S(2)}, u32[]{:S(2)}) collective-permute-start(bf16[512,128]{1,0:T(8,128)(2,1)S(1)} %get-tuple-element.25), channel_id=1, source_target_pairs={{0,4},{4,0},{1,5},{5,1},{2,6},{6,2},{3,7},{7,3},{8,12},{12,8},{9,1... | collective-permute-start | bytes 393224 | tf_op jit(solution)/shard_map/ppermute | solution.py:34
  17.3 0.0 collective-permute-done.3
  17.3 1.6 %collective-permute-start.4 = (bf16[200,128]{1,0:T(8,128)(2,1)S(1)}, bf16[200,128]{1,0:T(8,128)(2,1)S(1)}, u32[]{:S(2)}, u32[]{:S(2)}) collective-permute-start(bf16[200,128]{1,0:T(8,128)(2,1)S(1)} %add_convert_fusion.maps_a), channel_id=1, source_target_pairs={{0,16},{4,20},{8,12},{12,8},{16,0},{20,4},{24,28},{28,24},{1,17},{... | collective-permute-start | bytes 153608 | tf_op jit(solution)/shard_map/ppermute | solution.py:51
  18.9 1.1 %collective-permute-start.6 = (bf16[200,128]{1,0:T(8,128)(2,1)S(1)}, bf16[200,128]{1,0:T(8,128)(2,1)S(1)}, u32[]{:S(2)}, u32[]{:S(2)}) collective-permute-start(bf16[200,128]{1,0:T(8,128)(2,1)S(1)} %add_convert_fusion.maps_a), channel_id=1, source_target_pairs={{0,20},{4,16},{8,28},{12,24},{16,4},{20,0},{24,12},{28,8},{1,21},{... | collective-permute-start | bytes 153608 | tf_op jit(solution)/shard_map/ppermute | solution.py:34
  20.0 1.7 %collective-permute-done.4.maps_b = bf16[200,128]{1,0:T(8,128)(2,1)S(1)} collective-permute-done((bf16[200,128]{1,0:T(8,128)(2,1)S(1)}, bf16[200,128]{1,0:T(8,128)(2,1)S(1)}, u32[]{:S(2)}, u32[]{:S(2)}) %collective-permute-start.4) | collective-permute-done | bytes 51232 | tf_op jit(solution)/shard_map/ppermute | solution.py:51
  21.8 0.2 collective-permute-start.5
  22.0 0.0 collective-permute-done.1.other_ref
  22.0 0.5 %noise_statistics.1 = (f32[512,128]{1,0:T(8,128)S(1)}, bf16[512,128]{1,0:T(8,128)(2,1)S(1)}) custom-call(f32[256,128]{1,0:T(8,128)S(1)} %get-tuple-element.22.noise_ref, bf16[512,128]{1,0:T(8,128)(2,1)S(1)} %collective-permute-done.1.other_ref, bf16[3,128,384]{2,1,0:T(8,128)(2,1)S(1)} %get-tuple-element.29.gram_ref), custom_call_target="tpu_custom_call" | custom-call | tf_op jit(solution)/shard_map/noise_statistics/pallas_call | solution.py:479
  22.6 1.4 %collective-permute-done.6.maps_d = bf16[200,128]{1,0:T(8,128)(2,1)S(1)} collective-permute-done((bf16[200,128]{1,0:T(8,128)(2,1)S(1)}, bf16[200,128]{1,0:T(8,128)(2,1)S(1)}, u32[]{:S(2)}, u32[]{:S(2)}) %collective-permute-start.6) | collective-permute-done | bytes 51232 | tf_op jit(solution)/shard_map/ppermute | solution.py:34
  23.9 0.0 collective-permute-done.5.maps_c
  23.9 1.3 %tokens.1 = (f32[256,128]{1,0:T(8,128)S(1)}, bf16[112,128]{1,0:T(8,128)(2,1)S(1)}) custom-call(f32[1]{0:T(128)S(6)} %div.3.level_ref, f32[256,128]{1,0:T(8,128)S(1)} %get-tuple-element.22.noise_ref, bf16[512,128]{1,0:T(8,128)(2,1)S(1)} %collective-permute-done.1.other_ref, f32[256,128]{1,0:T(8,128)S(1)} %get-tuple-element.26.renoise_ref, ...), custom_call_target="tpu_custom_call" | custom-call | tf_op jit(solution)/shard_map/tokens/pallas_call | solution.py:617
  25.2 1.6 %collective-permute-start.7 = (bf16[112,128]{1,0:T(8,128)(2,1)S(1)}, bf16[112,128]{1,0:T(8,128)(2,1)S(1)}, u32[]{:S(2)}, u32[]{:S(2)}) collective-permute-start(bf16[112,128]{1,0:T(8,128)(2,1)S(1)} %get-tuple-element.38.block_a), channel_id=1, source_target_pairs={{0,1},{1,0},{2,3},{3,2},{8,10},{9,11},{10,8},{11,9},{16,17},{17,16... | collective-permute-start | bytes 86024 | tf_op jit(solution)/shard_map/ppermute | solution.py:65
  26.8 2.5 %collective-permute-start.9 = (bf16[112,128]{1,0:T(8,128)(2,1)S(1)}, bf16[112,128]{1,0:T(8,128)(2,1)S(1)}, u32[]{:S(2)}, u32[]{:S(2)}) collective-permute-start(bf16[112,128]{1,0:T(8,128)(2,1)S(1)} %get-tuple-element.38.block_a), channel_id=1, source_target_pairs={{0,3},{1,2},{2,1},{3,0},{4,7},{5,6},{6,5},{7,4},{8,11},{9,10},{10,... | collective-permute-start | bytes 86024 | tf_op jit(solution)/shard_map/ppermute | solution.py:34
  29.3 0.0 collective-permute-done.7.block_b
  29.3 3.2 %collective-permute-done.9.block_d = bf16[112,128]{1,0:T(8,128)(2,1)S(1)} collective-permute-done((bf16[112,128]{1,0:T(8,128)(2,1)S(1)}, bf16[112,128]{1,0:T(8,128)(2,1)S(1)}, u32[]{:S(2)}, u32[]{:S(2)}) %collective-permute-start.9) | collective-permute-done | bytes 28704 | tf_op jit(solution)/shard_map/ppermute | solution.py:34
  32.5 2.8 %gradient.1 = (f32[1536,768]{1,0:T(8,128)}, f32[256,128]{1,0:T(8,128)}) custom-call(bf16[112,128]{1,0:T(8,128)(2,1)S(1)} %get-tuple-element.38.block_a, bf16[112,128]{1,0:T(8,128)(2,1)S(1)} %collective-permute-done.7.block_b, bf16[112,128]{1,0:T(8,128)(2,1)S(1)} %collective-permute-done.8.block_c, bf16[112,128]{1,0:T(8,128)(2,1)S(1)} %collective-permute-done.9.block_d, ...), custom_call_target="tpu_custom_call" | custom-call | tf_op jit(solution)/shard_map/gradient/pallas_call | solution.py:688
  (4 shorter events, 0.0 us)
Async XLA Ops:
  8.6 1.4 %collective-permute-start = (f32[40,128]{1,0:T(8,128)S(1)}, f32[40,128]{1,0:T(8,128)S(1)}, u32[]{:S(2)}, u32[]{:S(2)}) collective-permute-start(f32[40,128]{1,0:T(8,128)S(1)} %get-tuple-element.23), channel_id=1, source_target_pairs={{0,8},{8,0},{16,24},{24,16},{1,9},{9,1},{17,25},{25,17},{2,10},{10... | collective-permute-start | bytes 61448 | tf_op jit(solution)/shard_map/ppermute | solution.py:34
  10.0 4.6 %collective-permute-start.2 = (f32[40,128]{1,0:T(8,128)S(1)}, f32[40,128]{1,0:T(8,128)S(1)}, u32[]{:S(2)}, u32[]{:S(2)}) collective-permute-start(f32[40,128]{1,0:T(8,128)S(1)} %get-tuple-element.32), channel_id=1, source_target_pairs={{0,4},{4,0},{1,5},{5,1},{2,6},{6,2},{3,7},{7,3},{8,12},{12,8},{9,1... | collective-permute-start | bytes 61448 | tf_op jit(solution)/shard_map/ppermute | solution.py:34
  15.2 2.2 %collective-permute-start.3 = (bf16[200,128]{1,0:T(8,128)(2,1)S(1)}, bf16[200,128]{1,0:T(8,128)(2,1)S(1)}, u32[]{:S(2)}, u32[]{:S(2)}) collective-permute-start(bf16[200,128]{1,0:T(8,128)(2,1)S(1)} %get-tuple-element.36), channel_id=1, source_target_pairs={{0,8},{8,0},{16,24},{24,16},{1,9},{9,1},{17,25},{25,17},{2,10},{10... | collective-permute-start | bytes 153608 | tf_op jit(solution)/shard_map/ppermute | solution.py:34
  15.2 6.8 %collective-permute-start.1 = (bf16[512,128]{1,0:T(8,128)(2,1)S(1)}, bf16[512,128]{1,0:T(8,128)(2,1)S(1)}, u32[]{:S(2)}, u32[]{:S(2)}) collective-permute-start(bf16[512,128]{1,0:T(8,128)(2,1)S(1)} %get-tuple-element.25), channel_id=1, source_target_pairs={{0,4},{4,0},{1,5},{5,1},{2,6},{6,2},{3,7},{7,3},{8,12},{12,8},{9,1... | collective-permute-start | bytes 393224 | tf_op jit(solution)/shard_map/ppermute | solution.py:34
  17.3 4.4 %collective-permute-start.4 = (bf16[200,128]{1,0:T(8,128)(2,1)S(1)}, bf16[200,128]{1,0:T(8,128)(2,1)S(1)}, u32[]{:S(2)}, u32[]{:S(2)}) collective-permute-start(bf16[200,128]{1,0:T(8,128)(2,1)S(1)} %add_convert_fusion.maps_a), channel_id=1, source_target_pairs={{0,16},{4,20},{8,12},{12,8},{16,0},{20,4},{24,28},{28,24},{1,17},{... | collective-permute-start | bytes 153608 | tf_op jit(solution)/shard_map/ppermute | solution.py:51
  18.9 5.0 %collective-permute-start.6 = (bf16[200,128]{1,0:T(8,128)(2,1)S(1)}, bf16[200,128]{1,0:T(8,128)(2,1)S(1)}, u32[]{:S(2)}, u32[]{:S(2)}) collective-permute-start(bf16[200,128]{1,0:T(8,128)(2,1)S(1)} %add_convert_fusion.maps_a), channel_id=1, source_target_pairs={{0,20},{4,16},{8,28},{12,24},{16,4},{20,0},{24,12},{28,8},{1,21},{... | collective-permute-start | bytes 153608 | tf_op jit(solution)/shard_map/ppermute | solution.py:34
  21.8 2.1 %collective-permute-start.5 = (bf16[200,128]{1,0:T(8,128)(2,1)S(1)}, bf16[200,128]{1,0:T(8,128)(2,1)S(1)}, u32[]{:S(2)}, u32[]{:S(2)}) collective-permute-start(bf16[200,128]{1,0:T(8,128)(2,1)S(1)} %collective-permute-done.4.maps_b), channel_id=1, source_target_pairs={{0,8},{8,0},{16,24},{24,16},{1,9},{9,1},{17,25},{25,17},{2,10},{10... | collective-permute-start | bytes 153608 | tf_op jit(solution)/shard_map/ppermute | solution.py:34
  25.2 4.1 %collective-permute-start.7 = (bf16[112,128]{1,0:T(8,128)(2,1)S(1)}, bf16[112,128]{1,0:T(8,128)(2,1)S(1)}, u32[]{:S(2)}, u32[]{:S(2)}) collective-permute-start(bf16[112,128]{1,0:T(8,128)(2,1)S(1)} %get-tuple-element.38.block_a), channel_id=1, source_target_pairs={{0,1},{1,0},{2,3},{3,2},{8,10},{9,11},{10,8},{11,9},{16,17},{17,16... | collective-permute-start | bytes 86024 | tf_op jit(solution)/shard_map/ppermute | solution.py:65
  26.8 5.7 %collective-permute-start.9 = (bf16[112,128]{1,0:T(8,128)(2,1)S(1)}, bf16[112,128]{1,0:T(8,128)(2,1)S(1)}, u32[]{:S(2)}, u32[]{:S(2)}) collective-permute-start(bf16[112,128]{1,0:T(8,128)(2,1)S(1)} %get-tuple-element.38.block_a), channel_id=1, source_target_pairs={{0,3},{1,2},{2,1},{3,0},{4,7},{5,6},{6,5},{7,4},{8,11},{9,10},{10,... | collective-permute-start | bytes 86024 | tf_op jit(solution)/shard_map/ppermute | solution.py:34
  29.3 3.2 %collective-permute-start.8 = (bf16[112,128]{1,0:T(8,128)(2,1)S(1)}, bf16[112,128]{1,0:T(8,128)(2,1)S(1)}, u32[]{:S(2)}, u32[]{:S(2)}) collective-permute-start(bf16[112,128]{1,0:T(8,128)(2,1)S(1)} %collective-permute-done.7.block_b), channel_id=1, source_target_pairs={{0,8},{8,0},{16,24},{24,16},{1,9},{9,1},{17,25},{25,17},{2,10},{10... | collective-permute-start | bytes 86024 | tf_op jit(solution)/shard_map/ppermute | solution.py:34
